TPU v7x, 32 devices: a whole 2x2x4 slice. The times are simulated.
32 devices in a mesh: ka: 2 (over x), br: 4 (over y, core), bc: 4 (over z).
Axes of the slice: x: 2, y: 2, z: 4, core: 2. Of those that a mesh axis runs over, the one named last changes fastest.
Arguments:
- green_lesser: float32 [2, 15, 2, 512, 512], P('ka', None, None, 'br', 'bc'), may hold values from -6 to 6
- screened: float32 [5, 8, 2, 512, 512], P(None, None, None, 'br', 'bc'), may hold values from -0.6 to 0.6
- slot_table: int32 [5, 2, 1], P(None, 'ka'), may hold values from 0 to 4
Outputs:
- sigma_lesser: float32 [2, 8, 2, 512, 512], P('ka', None, None, 'br', 'bc')
All inputs are finite; a program needn't handle non-finite values.
Results may differ from a plain program's by a relative error of at most 0.0003.
Values sent between devices are 32-bit elements; how exact they have to be, the bound alone decides.
No kernel may reach another device: no remote copies, remote signals or barrier semaphores. Data moves between devices by JAX's collectives and lax.ppermute only.
A program may use at most 64 MiB of HBM per device.

v0:
```python
import jax
import jax.numpy as jnp
from jax import lax
from jax.sharding import PartitionSpec as P

NE = 8


def shifted(x, axis, by):
    size = lax.axis_size(axis)
    return lax.ppermute(x, axis, [(i, (i + by) % size) for i in range(size)])


def stop_terms(remote, slot_row, screened, energies):
    freq_count = screened.shape[1]
    real_sum = jnp.zeros((energies,) + remote.shape[3:], jnp.float32)
    imag_sum = jnp.zeros((energies,) + remote.shape[3:], jnp.float32)
    chosen = lax.dynamic_index_in_dim(screened, slot_row[0, 0], 0, keepdims=False)
    for freq_index in range(freq_count):
        lag_start = freq_count - 1 - freq_index
        window = remote[0, lag_start : lag_start + energies]
        green_real = window[:, 0]
        green_imag = window[:, 1]
        inter_real = chosen[freq_index, 0]
        inter_imag = chosen[freq_index, 1]
        real_sum = real_sum - (green_real * inter_imag + green_imag * inter_real)
        imag_sum = imag_sum + (green_real * inter_real - green_imag * inter_imag)
    blocks_out = [jnp.stack((real_sum, imag_sum), 1)]
    return jnp.stack(blocks_out, 0)


def on_device(green_lesser, screened, slot_table):
    own_count = green_lesser.shape[0]
    accumulated = jnp.zeros((own_count, NE) + green_lesser.shape[2:], jnp.float32)

    def add_stop(partial_sum, remote, stop_index):
        return partial_sum + stop_terms(remote, slot_table[stop_index], screened, NE)

    accumulated = add_stop(accumulated, green_lesser, 0)
    lower_side = green_lesser
    upper_side = green_lesser
    for down_stop, up_stop in ((1, 2), (3, 4)):
        lower_side = shifted(lower_side, "ka", 1)
        upper_side = shifted(upper_side, "ka", -1)
        accumulated = add_stop(accumulated, lower_side, down_stop)
        accumulated = add_stop(accumulated, upper_side, up_stop)
    tile_rows = accumulated.shape[3]
    tile_cols = accumulated.shape[4]
    flattened = accumulated.reshape(own_count * NE * 2, 1, tile_rows, tile_cols)
    spread = lax.all_to_all(flattened, ("br", "bc"), split_axis=0, concat_axis=1, tiled=True)
    grid_rows = lax.axis_size("br")
    grid_cols = lax.axis_size("bc")
    per_device = spread.shape[0]
    tile_grid = spread.reshape(per_device, grid_rows, grid_cols, tile_rows, tile_cols)
    mirrored = jnp.swapaxes(tile_grid, 1, 2).reshape(spread.shape)
    device_number = lax.axis_index("br") * grid_cols + lax.axis_index("bc")
    item_number = device_number * per_device + jnp.arange(per_device, dtype=jnp.int32)
    parity = (item_number % 2).reshape(per_device, 1, 1, 1)
    signs = jnp.where(parity == 0, -1.0, 1.0).astype(jnp.float32)
    symmetric = (spread + signs * jnp.swapaxes(mirrored, -1, -2)) * 0.5
    returned = lax.all_to_all(symmetric, ("br", "bc"), split_axis=1, concat_axis=0, tiled=True)
    return returned.reshape(own_count, NE, 2, tile_rows, tile_cols)


def solution(mesh):
    in_specs = (
        P("ka", None, None, "br", "bc"),
        P(None, None, None, "br", "bc"),
        P(None, "ka", None),
    )
    out_specs = P("ka", None, None, "br", "bc")
    return jax.shard_map(
        on_device, mesh=mesh, in_specs=in_specs, out_specs=out_specs, check_vma=False
    )
```

profile of v0, /device:TPU:1, one launch (start us, length us, event | category | flops | bytes accessed | tf_op | source)
XLA Modules:
  0.0 163.4 jit_solution(9994002564526879311)
XLA Ops:
  0.0 3.1 %copy.31 = f32[1,15,2,128,128]{4,3,1,2,0:T(8,128)} copy(f32[1,15,2,128,128]{4,3,2,1,0:T(8,128)} %param.3) | data formatting | bytes 3932160 | tf_op args[0]
  3.1 2.0 %collective-permute-start = (f32[1,15,2,128,128]{4,3,1,2,0:T(8,128)}, f32[1,15,2,128,128]{4,3,1,2,0:T(8,128)S(1)}, u32[]{:S(2)}, u32[]{:S(2)}) collective-permute-start(f32[1,15,2,128,128]{4,3,1,2,0:T(8,128)} %copy.31), channel_id=1, source_target_pairs={{0,16},{16,0},{1,17},{17,1},{2,18},{18,2},{3,19},{19,3},{4,20},{20... | collective-permute-start | bytes 5898248 | tf_op jit(solution)/shard_map/ppermute | solution.py:11
  5.1 0.7 fusion.4
  15.5 2.8 %dynamic-slice_bitcast_fusion.1 = (f32[8,2,128,128]{3,2,1,0:T(8,128)S(1)}, f32[8,2,128,128]{3,2,1,0:T(8,128)S(1)}, f32[8,2,128,128]{3,2,1,0:T(8,128)S(1)}, f32[8...) fusion(f32[5,8,2,128,128]{4,3,2,1,0:T(8,128)} %param.4, s32[]{:T(128)S(6)} %select_n.31, s32[]{:T(128)S(6)} %select_n.30, ...), kind=kLoop, calls=%fused_computation.32 | loop fusion | bytes 10485780 | tf_op jit(solution)/shard_map/jit(dynamic_index_in_dim)/squeeze | solution.py:18
  18.4 0.1 slice_bitcast_fusion.55
  18.5 0.1 slice_bitcast_fusion.71
  18.7 0.1 slice_bitcast_fusion.103
  18.8 0.1 slice_bitcast_fusion.39
  18.9 1.3 copy-done
  20.2 1.0 slice_bitcast_fusion.23
  21.3 1.0 add_bitcast_fusion.4
  22.3 1.0 subtract_bitcast_fusion.4
  23.3 24.5 %collective-permute-done = f32[1,15,2,128,128]{4,3,1,2,0:T(8,128)S(1)} collective-permute-done((f32[1,15,2,128,128]{4,3,1,2,0:T(8,128)}, f32[1,15,2,128,128]{4,3,1,2,0:T(8,128)S(1)}, u32[]{:S(2)}, u32[]{:S(2)}) %collective-permute-start) | collective-permute-done | bytes 1966112 | tf_op jit(solution)/shard_map/ppermute | solution.py:11
  47.9 1.1 collective-permute-start.1
  49.0 1.0 slice_bitcast_fusion.15
  50.1 1.0 add_bitcast_fusion.2
  51.1 1.0 add_bitcast_fusion.3
  52.1 1.0 subtract_bitcast_fusion.2
  53.1 1.0 subtract_bitcast_fusion.3
  54.2 36.8 %collective-permute-done.1 = f32[1,15,2,128,128]{4,3,1,2,0:T(8,128)S(1)} collective-permute-done((f32[1,15,2,128,128]{4,3,1,2,0:T(8,128)S(1)}, f32[1,15,2,128,128]{4,3,1,2,0:T(8,128)S(1)}, u32[]{:S(2)}, u32[]{:S(2)}) %collective-permute-start.1) | collective-permute-done | bytes 1966112 | tf_op jit(solution)/shard_map/ppermute | solution.py:11
  91.0 1.0 slice_bitcast_fusion.7
  92.0 1.0 subtract_bitcast_fusion
  93.0 1.0 add_bitcast_fusion
  94.1 1.2 subtract_bitcast_fusion.1
  95.3 1.0 add_bitcast_fusion.1
  96.3 1.4 maximum_add_fusion.1
  97.6 7.9 %all-to-all-start = ((f32[16,1,128,128]{3,2,1,0:T(8,128)}), f32[16,1,128,128]{3,2,1,0:T(8,128)S(1)}, u32[]{:S(2)}, u32[]{:S(2)}) async-start(f32[16,1,128,128]{3,2,1,0:T(8,128)} %bitcast.126), calls=%async_computation | async-start | bytes 2097152 | tf_op jit(solution)/shard_map/all_to_all | solution.py:50
  105.6 26.2 %all-to-all-done = f32[16,1,128,128]{3,2,1,0:T(8,128)S(1)} async-done(((f32[16,1,128,128]{3,2,1,0:T(8,128)}), f32[16,1,128,128]{3,2,1,0:T(8,128)S(1)}, u32[]{:S(2)}, u32[]{:S(2)}) %all-to-all-start) | async-done | bytes 1048608 | tf_op jit(solution)/shard_map/all_to_all | solution.py:50
  131.9 0.3 copy.43
  132.2 0.1 fusion.3
  132.4 30.1 %all_to_all.21 = f32[1,16,128,128]{3,2,0,1:T(8,128)S(1)} all-to-all(f32[1,16,128,128]{3,2,0,1:T(8,128)S(1)} %fusion.3), channel_id=1, replica_groups=mesh['ka'=2,'br'=4,'bc'=4] {'br','bc'}, dimensions={1} | all-to-all | bytes 2097152 | tf_op jit(solution)/shard_map/all_to_all | solution.py:61
  162.5 1.0 copy.49
  (5 shorter events, 0.2 us)
Async XLA Ops:
  0.0 5.1 %copy-start.1 = (s32[5,1,1]{0,2,1:T(1,128)S(1)}, s32[5,1,1]{0,2,1:T(1,128)}, u32[]{:S(2)}) copy-start(s32[5,1,1]{0,2,1:T(1,128)} %param.5) | copy-start | bytes 64
  3.1 44.8 %collective-permute-start = (f32[1,15,2,128,128]{4,3,1,2,0:T(8,128)}, f32[1,15,2,128,128]{4,3,1,2,0:T(8,128)S(1)}, u32[]{:S(2)}, u32[]{:S(2)}) collective-permute-start(f32[1,15,2,128,128]{4,3,1,2,0:T(8,128)} %copy.31), channel_id=1, source_target_pairs={{0,16},{16,0},{1,17},{17,1},{2,18},{18,2},{3,19},{19,3},{4,20},{20... | collective-permute-start | bytes 5898248 | tf_op jit(solution)/shard_map/ppermute | solution.py:11
  18.7 1.5 copy-start
  47.9 43.1 %collective-permute-start.1 = (f32[1,15,2,128,128]{4,3,1,2,0:T(8,128)S(1)}, f32[1,15,2,128,128]{4,3,1,2,0:T(8,128)S(1)}, u32[]{:S(2)}, u32[]{:S(2)}) collective-permute-start(f32[1,15,2,128,128]{4,3,1,2,0:T(8,128)S(1)} %collective-permute-done), channel_id=1, source_target_pairs={{0,16},{16,0},{1,17},{17,1},{2,18},{18,2},{3,19},{19,3},{4,20},{20... | collective-permute-start | bytes 5898248 | tf_op jit(solution)/shard_map/ppermute | solution.py:11
  97.6 34.2 %all-to-all-start = ((f32[16,1,128,128]{3,2,1,0:T(8,128)}), f32[16,1,128,128]{3,2,1,0:T(8,128)S(1)}, u32[]{:S(2)}, u32[]{:S(2)}) async-start(f32[16,1,128,128]{3,2,1,0:T(8,128)} %bitcast.126), calls=%async_computation | async-start | bytes 2097152 | tf_op jit(solution)/shard_map/all_to_all | solution.py:50
where the time goes:
time: 165 us; the launch traced here: 163 us
  waiting for transfers between devices  87.6 us (53%)
  blocking collectives  30.1 us (18%)
  local copies, waits for them, and re-layouts  12.8 us (8%)
  other arithmetic  11.9 us (7%)
  starting transfers between devices  11.1 us (7%)
  between operations  9.92 us (6%)
    ppermute x2, waiting for transfers between devices, shifted(): return lax.ppermute(x, axis, [(i, (i + by) % size) for i in range(size)])  61.3 us
    all_to_all x1, blocking collectives, on_device(): lax.all_to_all(symmetric, ('br', 'bc'), split_axis=1, concat_axis=0, tile...  30.1 us
    all_to_all x1, waiting for transfers between devices, on_device(): lax.all_to_all(flattened, ('br', 'bc'), split_axis=0, concat_axis=1, tile...  26.2 us
    another operation x10, other arithmetic, stop_terms(): blocks_out = [jnp.stack((real_sum, imag_sum), 1)]  10.4 us
    all_to_all x1, starting transfers between devices, on_device(): lax.all_to_all(flattened, ('br', 'bc'), split_axis=0, concat_axis=1, tile...  7.93 us
    unnamed x6, local copies, waits for them, and re-layouts  5.38 us
  transfers between devices with their start and end apart: 3, of which 3 were waited for; matrix products, arithmetic and copies ran while one was open for 7% of the time, Pallas kernels for 0%

commit v1 on v0

v1 whole, which is shorter than its diff:
```python
import functools

import jax
import jax.numpy as jnp
from jax import lax
from jax.experimental import pallas as pl
from jax.experimental.pallas import tpu as pltpu
from jax.sharding import PartitionSpec as P

NE = 8
HOPS = (0, 1, -1, 2, -2)
SUBLANES = 8
AXES = ("ka", "br", "bc")
VMEM_LIMIT = 32 * 1024 * 1024


def spans_of(energies, parts):
    parts = min(parts, energies)
    cuts = [energies * part // parts for part in range(parts + 1)]
    return [(low, high - low) for low, high in zip(cuts, cuts[1:])]


def correlate_kernel(first, counts, freqs, group, slots_ref, green_ref, *refs):
    del slots_ref
    screened_refs, out_refs = refs[:group], refs[group:]
    rows = green_ref.shape[3]

    def rows_step(step, carry):
        at = pl.ds(pl.multiple_of(step * SUBLANES, SUBLANES), SUBLANES)

        def inter(freq, part):
            value = screened_refs[0][0, freq, part, at, :]
            for ref in screened_refs[1:]:
                value = value + ref[0, freq, part, at, :]
            return value

        energies = sum(counts)
        real = [None] * energies
        imag = [None] * energies
        weights = [(inter(freq, 0), inter(freq, 1)) for freq in range(freqs)]
        for lag in range(energies + freqs - 1):
            green_real = green_ref[0, first + lag, 0, at, :]
            green_imag = green_ref[0, first + lag, 1, at, :]
            for energy in range(energies):
                freq = energy + freqs - 1 - lag
                if 0 <= freq < freqs:
                    inter_real, inter_imag = weights[freq]
                    real_term = green_real * inter_imag + green_imag * inter_real
                    imag_term = green_real * inter_real - green_imag * inter_imag
                    if real[energy] is None:
                        real[energy], imag[energy] = -real_term, imag_term
                    else:
                        real[energy] = real[energy] - real_term
                        imag[energy] = imag[energy] + imag_term
        energy = 0
        for out_ref, count in zip(out_refs, counts):
            for place in range(count):
                out_ref[place, 0, at, :] = real[energy]
                out_ref[place, 1, at, :] = imag[energy]
                energy += 1
        return carry

    lax.fori_loop(0, rows // SUBLANES, rows_step, 0)


def correlate(green, screened, slots, spans, row_blocks):
    freqs = screened.shape[1]
    rows, cols = green.shape[3:]
    block_rows = rows // row_blocks
    group = slots.shape[0]
    first = spans[0][0]
    counts = tuple(count for _, count in spans)

    def green_map(block, slots_ref):
        return (0, 0, 0, block, 0)

    def screened_map(place, block, slots_ref):
        return (slots_ref[place], 0, 0, block, 0)

    return pl.pallas_call(
        functools.partial(correlate_kernel, first, counts, freqs, group),
        grid_spec=pltpu.PrefetchScalarGridSpec(
            num_scalar_prefetch=1,
            grid=(row_blocks,),
            in_specs=[pl.BlockSpec((1,) + green.shape[1:3] + (block_rows, cols), green_map)]
            + [
                pl.BlockSpec((1,) + screened.shape[1:3] + (block_rows, cols), functools.partial(screened_map, place))
                for place in range(group)
            ],
            out_specs=[
                pl.BlockSpec((count, 2, block_rows, cols), lambda block, slots_ref: (0, 0, block, 0))
                for count in counts
            ],
        ),
        out_shape=[jax.ShapeDtypeStruct((count, 2, rows, cols), jnp.float32) for count in counts],
        compiler_params=pltpu.CompilerParams(vmem_limit_bytes=VMEM_LIMIT),
        name="correlate",
    )(slots, green, *([screened] * group))


def mix_kernel(received, flags_ref, own_ref, *refs):
    recv_refs = refs[:received]
    held_real_ref, held_imag_ref = refs[received : received + 2]
    raw_ref, real_ref, imag_ref = refs[received + 2 :]
    far = flags_ref[0] == 1
    count = own_ref.shape[0]
    held = held_real_ref.shape[0]
    for place in range(count):
        for part, held_ref, send_ref in ((0, held_real_ref, real_ref), (1, held_imag_ref, imag_ref)):
            value = own_ref[place, part]
            for ref in recv_refs:
                value = value + ref[place, part]
            raw_ref[place, part] = value
            if place < held:
                send_ref[place] = jnp.where(far, value, held_ref[place])
            else:
                send_ref[place] = value
    for place in range(count, held):
        for held_ref, send_ref in ((held_real_ref, real_ref), (held_imag_ref, imag_ref)):
            send_ref[place] = held_ref[place]


def mix(flags, own, received, held_real, held_imag):
    count = own.shape[0]
    tile = own.shape[2:]
    longest = max(count, held_real.shape[0])
    vmem = pl.BlockSpec(memory_space=pltpu.VMEM)
    return pl.pallas_call(
        functools.partial(mix_kernel, len(received)),
        grid_spec=pltpu.PrefetchScalarGridSpec(
            num_scalar_prefetch=1,
            grid=(),
            in_specs=[vmem] * (3 + len(received)),
            out_specs=[vmem] * 3,
        ),
        out_shape=[
            jax.ShapeDtypeStruct(own.shape, jnp.float32),
            jax.ShapeDtypeStruct((longest,) + tile, jnp.float32),
            jax.ShapeDtypeStruct((longest,) + tile, jnp.float32),
        ],
        compiler_params=pltpu.CompilerParams(vmem_limit_bytes=VMEM_LIMIT),
        name="mix",
    )(flags, own, *received, held_real, held_imag)


def skew_kernel(flags_ref, raw_ref, near_ref, far_real_ref, far_imag_ref, *refs):
    out_ref = refs[-1]

    def write(real, imag):
        out_ref[0, 0, 0] = (raw_ref[0, 0] - real.T) * 0.5
        out_ref[0, 0, 1] = (raw_ref[0, 1] + imag.T) * 0.5

    @pl.when(flags_ref[0] == 1)
    def _():
        write(far_real_ref[0], far_imag_ref[0])

    @pl.when(flags_ref[0] == 0)
    def _():
        write(near_ref[0, 0], near_ref[0, 1])

    @pl.when(flags_ref[0] == 2)
    def _():
        write(raw_ref[0, 0], raw_ref[0, 1])


def skew(flags, raw, near, far_real, far_imag, first, energies, out):
    count = raw.shape[0]
    tile = raw.shape[2:]
    pair = pl.BlockSpec((1, 2) + tile, lambda place, flags_ref: (place, 0, 0, 0))
    single = pl.BlockSpec((1,) + tile, lambda place, flags_ref: (place, 0, 0))
    operands = [raw, near, far_real, far_imag]
    in_specs = [pair, pair, single, single]
    aliases = {}
    if out is not None:
        aliases = {1 + len(operands): 0}
        operands.append(out)
        in_specs.append(pl.BlockSpec(memory_space=pl.ANY))
    return pl.pallas_call(
        skew_kernel,
        grid_spec=pltpu.PrefetchScalarGridSpec(
            num_scalar_prefetch=1,
            grid=(count,),
            in_specs=in_specs,
            out_specs=pl.BlockSpec((1, 1, 2) + tile, lambda place, flags_ref: (0, first + place, 0, 0, 0)),
        ),
        out_shape=jax.ShapeDtypeStruct((1, energies, 2) + tile, jnp.float32),
        input_output_aliases=aliases,
        compiler_params=pltpu.CompilerParams(vmem_limit_bytes=VMEM_LIMIT),
        name="skew",
    )(flags, *operands)


def grid_moves(momenta, side):
    half = side // 2

    def number(momentum, row_half, row_low, col_half, col_low):
        return (momentum * side + row_half * half + row_low) * side + col_half * half + col_low

    column_first, row_first, near = ([], []), ([], []), []
    for momentum in range(momenta):
        for a in range(2):
            for row in range(half):
                for col in range(half):
                    b = 1 - a
                    here = number(momentum, a, row, b, col)
                    mirror = number(momentum, b, col, a, row)
                    over_columns = number(momentum, a, col, a, row)
                    over_rows = number(momentum, b, row, b, col)
                    column_first[0].append((here, over_columns))
                    column_first[1].append((over_columns, mirror))
                    row_first[0].append((here, over_rows))
                    row_first[1].append((over_rows, mirror))
                    if row != col:
                        near.append((number(momentum, a, row, a, col), number(momentum, a, col, a, row)))
    return column_first, row_first, near


def on_device(parts, green_lesser, screened, slot_table):
    momenta = lax.axis_size("ka")
    side = lax.axis_size("br")
    row, col = lax.axis_index("br"), lax.axis_index("bc")
    half = side // 2
    tile = green_lesser.shape[3:]
    column_first, row_first, near_pairs = grid_moves(momenta, side)
    far = (row // half) != (col // half)
    flags = jnp.where(far, 1, jnp.where(row == col, 2, 0)).astype(jnp.int32).reshape(1)

    groups = {}
    for stop, hop in enumerate(HOPS):
        groups.setdefault(hop % momenta, []).append(stop)
    slots = {}
    for shift, stops in groups.items():
        table = slot_table
        if shift:
            table = lax.ppermute(table, "ka", [((k + shift) % momenta, k) for k in range(momenta)])
        slots[shift] = jnp.stack([table[stop, 0, 0] for stop in stops])
    spans = spans_of(NE, parts)

    own = correlate(green_lesser, screened, slots[0], spans, 4)
    arrived = [[] for _ in spans]
    for shift in groups:
        if not shift:
            continue
        pairs = [(k, (k + shift) % momenta) for k in range(momenta)]
        sent = correlate(green_lesser, screened, slots[shift], spans[:1], 4)
        sent += correlate(green_lesser, screened, slots[shift], spans[1:], 4)
        for place, part in enumerate(sent):
            arrived[place].append(lax.ppermute(part, "ka", pairs))

    raws, nears, far_parts = [], [], []
    held_real = held_imag = jnp.zeros((1,) + tile, jnp.float32)
    for place in range(len(spans)):
        raw, send_real, send_imag = mix(flags, own[place], arrived[place], held_real, held_imag)
        legs = 2 if place else 1
        held_real = lax.ppermute(send_real, AXES, sum(column_first[:legs], []))
        held_imag = lax.ppermute(send_imag, AXES, sum(row_first[:legs], []))
        nears.append(lax.ppermute(raw, AXES, near_pairs))
        raws.append(raw)
        far_parts.append((held_real, held_imag))
    held_real = lax.ppermute(held_real, AXES, column_first[1])
    held_imag = lax.ppermute(held_imag, AXES, row_first[1])
    far_parts.append((held_real, held_imag))
    out = None
    for place, (first, _) in enumerate(spans):
        out = skew(flags, raws[place], nears[place], *far_parts[place + 1], first, NE, out)
    return out


def solution(mesh):
    in_specs = (
        P("ka", None, None, "br", "bc"),
        P(None, None, None, "br", "bc"),
        P(None, "ka", None),
    )
    out_specs = P("ka", None, None, "br", "bc")
    return jax.shard_map(
        functools.partial(on_device, 4), mesh=mesh, in_specs=in_specs, out_specs=out_specs, check_vma=False
    )
```

time: 165 us -> 75.4 us (0.46)
  waiting for transfers between devices: 87.6 us -> 12.7 us
  blocking collectives: 30.1 us -> 0 us
  starting transfers between devices: 11.1 us -> 36.2 us
  Pallas kernels: 0 us -> 11.3 us
  between operations: 9.92 us -> 0.2 us
  other arithmetic: 11.9 us -> 3.22 us
  local copies, waits for them, and re-layouts: 12.8 us -> 10.8 us
    ppermute x2 -> x19, waiting for transfers between devices: 61.3 us -> 12.7 us  [the longest x4 7.48 us: on_device(): held_real = lax.ppermute(send_real, AXES, sum(column_first[:legs], []))]
    ppermute x2 -> x19, starting transfers between devices: 3.19 us -> 36.2 us  [the longest x4 12.7 us: on_device(): held_imag = lax.ppermute(send_imag, AXES, sum(row_first[:legs], []))]
    all_to_all x1 -> x0, blocking collectives: 30.1 us -> none  [on_device(): lax.all_to_all(symmetric, ('br', 'bc'), split_axis=1, concat_axis=0, tile...]
    all_to_all x1 -> x0, waiting for transfers between devices: 26.2 us -> none  [on_device(): lax.all_to_all(flattened, ('br', 'bc'), split_axis=0, concat_axis=1, tile...]
    pallas_call x0 -> x11, Pallas kernels: none -> 11.3 us  [the longest x3 7.46 us: correlate(): pl.pallas_call(functools.partial(correlate_kernel, first, counts, freqs,...]
    all_to_all x1 -> x0, starting transfers between devices: 7.93 us -> none  [on_device(): lax.all_to_all(flattened, ('br', 'bc'), split_axis=0, concat_axis=1, tile...]
    another operation x10 -> x2, other arithmetic: 10.4 us -> 3.22 us  [on_device(): slots[shift] = jnp.stack([table[stop, 0, 0] for stop in stops])]
    squeeze x4 -> x0, local copies, waits for them, and re-layouts: 5.97 us -> none  [the longest x3 3.12 us: stop_terms(): window = remote[0, lag_start:lag_start + energies]]
  transfers between devices with their start and end apart: 3 -> 19, of which waited for: 3 -> 7; matrix products, arithmetic and copies ran while one was open for 7% -> 3% of each run, Pallas kernels for 0% -> 12%
where the time goes in v1:
time: 75.4 us; the launch traced here: 74.4 us
  starting transfers between devices  36.2 us (48%)
  waiting for transfers between devices  12.7 us (17%)
  Pallas kernels  11.3 us (15%)
  local copies, waits for them, and re-layouts  10.8 us (14%)
  other arithmetic  3.22 us (4%)
    ppermute x4, starting transfers between devices, on_device(): held_imag = lax.ppermute(send_imag, AXES, sum(row_first[:legs], []))  12.7 us
    unnamed x18, local copies, waits for them, and re-layouts  9.56 us
    ppermute x4, starting transfers between devices, on_device(): nears.append(lax.ppermute(raw, AXES, near_pairs))  9.37 us
    ppermute x4, waiting for transfers between devices, on_device(): held_real = lax.ppermute(send_real, AXES, sum(column_first[:legs], []))  7.48 us
    pallas_call x3, Pallas kernels, correlate(): pl.pallas_call(functools.partial(correlate_kernel, first, counts, freqs,...  7.46 us
    ppermute x1, starting transfers between devices, on_device(): held_imag = lax.ppermute(held_imag, AXES, row_first[1])  5.1 us
    ppermute x4, starting transfers between devices, on_device(): arrived[place].append(lax.ppermute(part, 'ka', pairs))  4.27 us
    ppermute x4, waiting for transfers between devices, on_device(): held_imag = lax.ppermute(send_imag, AXES, sum(row_first[:legs], []))  3.89 us
  transfers between devices with their start and end apart: 19, of which 7 were waited for; matrix products, arithmetic and copies ran while one was open for 3% of the time, Pallas kernels for 12%

profile of v1, /device:TPU:1, one launch (start us, length us, event | category | flops | bytes accessed | tf_op | source)
XLA Modules:
  0.0 74.4 jit_solution(7994392750667990811)
XLA Ops:
  0.0 2.0 %collective-permute-start = (s32[5,1,1]{0,2,1:T(1,128)}, s32[5,1,1]{0,2,1:T(1,128)S(1)}, u32[]{:S(2)}, u32[]{:S(2)}) collective-permute-start(s32[5,1,1]{0,2,1:T(1,128)} %param.5), channel_id=1, source_target_pairs={{16,0},{0,16},{17,1},{1,17},{18,2},{2,18},{19,3},{3,19},{20,4},{4,... | collective-permute-start | bytes 68 | tf_op jit(solution)/shard_map/ppermute | solution.py:235
  2.0 1.1 %collective-permute-done = s32[5,1,1]{0,2,1:T(1,128)S(1)} collective-permute-done((s32[5,1,1]{0,2,1:T(1,128)}, s32[5,1,1]{0,2,1:T(1,128)S(1)}, u32[]{:S(2)}, u32[]{:S(2)}) %collective-permute-start) | collective-permute-done | bytes 52 | tf_op jit(solution)/shard_map/ppermute | solution.py:235
  3.7 1.3 %pad_add_fusion.1.slots_ref = s32[2]{0:T(128)S(1)} fusion(s32[1]{0:T(128)} %bitcast.5, s32[1]{0:T(128)} %bitcast.4), kind=kLoop, calls=%fused_computation.1 | loop fusion | flops 2 | bytes 16 | tf_op jit(solution)/shard_map/stack | solution.py:236
  5.0 2.5 %copy-done = f32[5,8,2,128,128]{4,3,2,1,0:T(8,128)S(1)} copy-done((f32[5,8,2,128,128]{4,3,2,1,0:T(8,128)S(1)}, f32[5,8,2,128,128]{4,3,2,1,0:T(8,128)}, u32[]{:S(2)}) %copy-start) | copy-done | bytes 5242904
  7.5 1.5 %copy-done.2 = f32[1,15,2,128,128]{4,3,2,1,0:T(8,128)S(1)} copy-done((f32[1,15,2,128,128]{4,3,2,1,0:T(8,128)S(1)}, f32[1,15,2,128,128]{4,3,2,1,0:T(8,128)}, u32[]{:S(2)}) %copy-start.2) | copy-done | bytes 1966104
  9.0 1.7 %correlate.5 = f32[2,2,128,128]{3,2,1,0:T(8,128)S(1)} custom-call(s32[2]{0:T(128)S(1)} %pad_add_fusion.1.slots_ref, f32[1,15,2,128,128]{4,3,2,1,0:T(8,128)S(1)} %copy-done.2, f32[5,8,2,128,128]{4,3,2,1,0:T(8,128)S(1)} %copy-done, f32[5,8,2,128,128]{4,3,2,1,0:T(8,128)S(1)} %copy-done), custom_call_target="tpu_custom_call" | custom-call | tf_op jit(solution)/shard_map/correlate/pallas_call | solution.py:80
  10.7 1.5 %collective-permute-start.4 = (f32[2,2,128,128]{3,2,1,0:T(8,128)S(1)}, f32[2,2,128,128]{3,2,1,0:T(8,128)S(1)}, u32[]{:S(2)}, u32[]{:S(2)}) collective-permute-start(f32[2,2,128,128]{3,2,1,0:T(8,128)S(1)} %correlate.5), channel_id=1, source_target_pairs={{0,16},{16,0},{1,17},{17,1},{2,18},{18,2},{3,19},{19,3},{4,20},{20... | collective-permute-start | bytes 786440 | tf_op jit(solution)/shard_map/ppermute | solution.py:248
  12.2 3.0 %correlate.4 = (f32[2,2,128,128]{3,2,1,0:T(8,128)}, f32[2,2,128,128]{3,2,1,0:T(8,128)S(1)}, f32[2,2,128,128]{3,2,1,0:T(8,128)S(1)}) custom-call(s32[2]{0:T(128)S(1)} %pad_add_fusion.1.slots_ref, f32[1,15,2,128,128]{4,3,2,1,0:T(8,128)S(1)} %copy-done.2, f32[5,8,2,128,128]{4,3,2,1,0:T(8,128)S(1)} %copy-done, f32[5,8,2,128,128]{4,3,2,1,0:T(8,128)S(1)} %copy-done), custom_call_target="tpu_custom_call" | custom-call | tf_op jit(solution)/shard_map/correlate/pallas_call | solution.py:80
  17.3 1.9 %pad_add_fusion.slots_ref = s32[3]{0:T(128)S(1)} fusion(s32[1]{0:T(128)} %bitcast.3, s32[1]{0:T(128)} %bitcast.2, s32[1]{0:T(128)} %bitcast.1), kind=kLoop, calls=%fused_computation | loop fusion | flops 6 | bytes 24 | tf_op jit(solution)/shard_map/stack | solution.py:236
  19.2 2.5 %copy-done.1 = f32[5,8,2,128,128]{4,3,2,1,0:T(8,128)S(1)} copy-done((f32[5,8,2,128,128]{4,3,2,1,0:T(8,128)S(1)}, f32[5,8,2,128,128]{4,3,2,1,0:T(8,128)}, u32[]{:S(2)}) %copy-start.1) | copy-done | bytes 5242904
  21.7 2.8 %correlate.3 = (f32[2,2,128,128]{3,2,1,0:T(8,128)S(1)}, f32[2,2,128,128]{3,2,1,0:T(8,128)S(1)}, f32[2,2,128,128]{3,2,1,0:T(8,128)S(1)}, f32[2,2,128,128]{3,2,1,0:T(8,128)S(1)}) custom-call(s32[3]{0:T(128)S(1)} %pad_add_fusion.slots_ref, f32[1,15,2,128,128]{4,3,2,1,0:T(8,128)S(1)} %copy-done.3, f32[5,8,2,128,128]{4,3,2,1,0:T(8,128)S(1)} %copy-done.1, ...), custom_call_target="tpu_custom_call" | custom-call | tf_op jit(solution)/shard_map/correlate/pallas_call | solution.py:80
  25.3 1.3 %collective-permute-start.5 = (f32[2,128,128]{2,1,0:T(8,128)S(1)}, f32[2,128,128]{2,1,0:T(8,128)S(1)}, u32[]{:S(2)}, u32[]{:S(2)}) collective-permute-start(f32[2,128,128]{2,1,0:T(8,128)S(1)} %get-tuple-element.31), channel_id=1, source_target_pairs={{2,0},{3,4},{6,1},{7,5},{8,10},{9,14},{12,11},{13,15},{18,16},{19,... | collective-permute-start | bytes 393224 | tf_op jit(solution)/shard_map/ppermute | solution.py:255
  26.6 1.3 %collective-permute-start.6 = (f32[2,128,128]{2,1,0:T(8,128)S(1)}, f32[2,128,128]{2,1,0:T(8,128)S(1)}, u32[]{:S(2)}, u32[]{:S(2)}) collective-permute-start(f32[2,128,128]{2,1,0:T(8,128)S(1)} %get-tuple-element.32), channel_id=1, source_target_pairs={{2,10},{3,11},{6,14},{7,15},{8,0},{9,1},{12,4},{13,5},{18,26},{19,... | collective-permute-start | bytes 393224 | tf_op jit(solution)/shard_map/ppermute | solution.py:256
  27.9 1.5 %collective-permute-start.2 = (f32[2,2,128,128]{3,2,1,0:T(8,128)}, f32[2,2,128,128]{3,2,1,0:T(8,128)S(1)}, u32[]{:S(2)}, u32[]{:S(2)}) collective-permute-start(f32[2,2,128,128]{3,2,1,0:T(8,128)} %copy-done.7), channel_id=1, source_target_pairs={{0,16},{16,0},{1,17},{17,1},{2,18},{18,2},{3,19},{19,3},{4,20},{20... | collective-permute-start | bytes 786440 | tf_op jit(solution)/shard_map/ppermute | solution.py:248
  29.4 5.7 %collective-permute-done.5.refs_1_ = f32[2,128,128]{2,1,0:T(8,128)S(1)} collective-permute-done((f32[2,128,128]{2,1,0:T(8,128)S(1)}, f32[2,128,128]{2,1,0:T(8,128)S(1)}, u32[]{:S(2)}, u32[]{:S(2)}) %collective-permute-start.5) | collective-permute-done | bytes 131104 | tf_op jit(solution)/shard_map/ppermute | solution.py:255
  35.1 3.7 %collective-permute-done.6.refs_2_ = f32[2,128,128]{2,1,0:T(8,128)S(1)} collective-permute-done((f32[2,128,128]{2,1,0:T(8,128)S(1)}, f32[2,128,128]{2,1,0:T(8,128)S(1)}, u32[]{:S(2)}, u32[]{:S(2)}) %collective-permute-start.6) | collective-permute-done | bytes 131104 | tf_op jit(solution)/shard_map/ppermute | solution.py:256
  38.9 0.9 %copy-done.5 = f32[2,2,128,128]{3,2,1,0:T(8,128)S(1)} copy-done((f32[2,2,128,128]{3,2,1,0:T(8,128)S(1)}, f32[2,2,128,128]{3,2,1,0:T(8,128)}, u32[]{:S(2)}) %copy-start.5) | copy-done | bytes 262168
  39.9 3.5 %collective-permute-start.8 = (f32[2,128,128]{2,1,0:T(8,128)S(1)}, f32[2,128,128]{2,1,0:T(8,128)S(1)}, u32[]{:S(2)}, u32[]{:S(2)}) collective-permute-start(f32[2,128,128]{2,1,0:T(8,128)S(1)} %get-tuple-element.34), channel_id=1, source_target_pairs={{2,10},{3,11},{6,14},{7,15},{8,0},{9,1},{12,4},{13,5},{18,26},{19,... | collective-permute-start | bytes 393224 | tf_op jit(solution)/shard_map/ppermute | solution.py:256
  43.5 1.2 %collective-permute-start.1 = (f32[2,2,128,128]{3,2,1,0:T(8,128)}, f32[2,2,128,128]{3,2,1,0:T(8,128)S(1)}, u32[]{:S(2)}, u32[]{:S(2)}) collective-permute-start(f32[2,2,128,128]{3,2,1,0:T(8,128)} %copy-done.6), channel_id=1, source_target_pairs={{0,16},{16,0},{1,17},{17,1},{2,18},{18,2},{3,19},{19,3},{4,20},{20... | collective-permute-start | bytes 786440 | tf_op jit(solution)/shard_map/ppermute | solution.py:248
  44.7 1.9 %collective-permute-start.18 = (f32[2,2,128,128]{3,2,1,0:T(8,128)S(1)}, f32[2,2,128,128]{3,2,1,0:T(8,128)S(1)}, u32[]{:S(2)}, u32[]{:S(2)}) collective-permute-start(f32[2,2,128,128]{3,2,1,0:T(8,128)S(1)} %get-tuple-element.42.raw_ref), channel_id=1, source_target_pairs={{1,4},{4,1},{11,14},{14,11},{17,20},{20,17},{27,30},{30,27}} | collective-permute-start | bytes 786440 | tf_op jit(solution)/shard_map/ppermute | solution.py:257
  46.8 4.3 %collective-permute-start.10 = (f32[2,128,128]{2,1,0:T(8,128)S(1)}, f32[2,128,128]{2,1,0:T(8,128)S(1)}, u32[]{:S(2)}, u32[]{:S(2)}) collective-permute-start(f32[2,128,128]{2,1,0:T(8,128)S(1)} %get-tuple-element.36), channel_id=1, source_target_pairs={{2,10},{3,11},{6,14},{7,15},{8,0},{9,1},{12,4},{13,5},{18,26},{19,... | collective-permute-start | bytes 393224 | tf_op jit(solution)/shard_map/ppermute | solution.py:256
  51.2 1.9 %collective-permute-start.17 = (f32[2,2,128,128]{3,2,1,0:T(8,128)S(1)}, f32[2,2,128,128]{3,2,1,0:T(8,128)S(1)}, u32[]{:S(2)}, u32[]{:S(2)}) collective-permute-start(f32[2,2,128,128]{3,2,1,0:T(8,128)S(1)} %get-tuple-element.41.raw_ref), channel_id=1, source_target_pairs={{1,4},{4,1},{11,14},{14,11},{17,20},{20,17},{27,30},{30,27}} | collective-permute-start | bytes 786440 | tf_op jit(solution)/shard_map/ppermute | solution.py:257
  53.1 3.6 %collective-permute-start.16 = (f32[2,2,128,128]{3,2,1,0:T(8,128)S(1)}, f32[2,2,128,128]{3,2,1,0:T(8,128)S(1)}, u32[]{:S(2)}, u32[]{:S(2)}) collective-permute-start(f32[2,2,128,128]{3,2,1,0:T(8,128)S(1)} %get-tuple-element.40.raw_ref), channel_id=1, source_target_pairs={{1,4},{4,1},{11,14},{14,11},{17,20},{20,17},{27,30},{30,27}} | collective-permute-start | bytes 786440 | tf_op jit(solution)/shard_map/ppermute | solution.py:257
  57.7 3.5 %collective-permute-start.14 = (f32[2,128,128]{2,1,0:T(8,128)S(1)}, f32[2,128,128]{2,1,0:T(8,128)S(1)}, u32[]{:S(2)}, u32[]{:S(2)}) collective-permute-start(f32[2,128,128]{2,1,0:T(8,128)S(1)} %get-tuple-element.39), channel_id=1, source_target_pairs={{2,10},{3,11},{6,14},{7,15},{8,0},{9,1},{12,4},{13,5},{18,26},{19,... | collective-permute-start | bytes 393224 | tf_op jit(solution)/shard_map/ppermute | solution.py:256
  61.2 1.9 %collective-permute-start.11 = (f32[2,2,128,128]{3,2,1,0:T(8,128)S(1)}, f32[2,2,128,128]{3,2,1,0:T(8,128)S(1)}, u32[]{:S(2)}, u32[]{:S(2)}) collective-permute-start(f32[2,2,128,128]{3,2,1,0:T(8,128)S(1)} %get-tuple-element.37.raw_ref), channel_id=1, source_target_pairs={{1,4},{4,1},{11,14},{14,11},{17,20},{20,17},{27,30},{30,27}} | collective-permute-start | bytes 786440 | tf_op jit(solution)/shard_map/ppermute | solution.py:257
  63.1 0.9 %collective-permute-done.12.far_real_ref = f32[2,128,128]{2,1,0:T(8,128)S(1)} collective-permute-done((f32[2,128,128]{2,1,0:T(8,128)S(1)}, f32[2,128,128]{2,1,0:T(8,128)S(1)}, u32[]{:S(2)}, u32[]{:S(2)}) %collective-permute-start.12) | collective-permute-done | bytes 131104 | tf_op jit(solution)/shard_map/ppermute | solution.py:255
  64.1 1.3 %collective-permute-start.13 = (f32[2,128,128]{2,1,0:T(8,128)S(1)}, f32[2,128,128]{2,1,0:T(8,128)S(1)}, u32[]{:S(2)}, u32[]{:S(2)}) collective-permute-start(f32[2,128,128]{2,1,0:T(8,128)S(1)} %collective-permute-done.12.far_real_ref), channel_id=1, source_target_pairs={{0,8},{4,12},{1,9},{5,13},{10,2},{14,6},{11,3},{15,7},{16,24},{20,... | collective-permute-start | bytes 393224 | tf_op jit(solution)/shard_map/ppermute | solution.py:260
  65.4 5.1 %collective-permute-start.15 = (f32[2,128,128]{2,1,0:T(8,128)S(1)}, f32[2,128,128]{2,1,0:T(8,128)S(1)}, u32[]{:S(2)}, u32[]{:S(2)}) collective-permute-start(f32[2,128,128]{2,1,0:T(8,128)S(1)} %collective-permute-done.14.far_imag_ref), channel_id=1, source_target_pairs={{10,8},{11,12},{14,9},{15,13},{0,2},{1,6},{4,3},{5,7},{26,24},{27,... | collective-permute-start | bytes 393224 | tf_op jit(solution)/shard_map/ppermute | solution.py:261
  70.5 0.9 %skew.4.refs_0_ = f32[1,8,2,128,128]{4,3,2,1,0:T(8,128)} custom-call(s32[1]{0:T(128)} %bitcast.flags_ref, f32[2,2,128,128]{3,2,1,0:T(8,128)S(1)} %get-tuple-element.42.raw_ref, f32[2,2,128,128]{3,2,1,0:T(8,128)S(1)} %collective-permute-done.18.near_ref, f32[2,128,128]{2,1,0:T(8,128)S(1)} %collective-permute-done.7.refs_1_.far_real_ref, ...), custom_call_target="tpu_custom_call" | custom-call | tf_op jit(solution)/shard_map/skew/pallas_call | solution.py:178
  71.4 0.9 %skew.5.refs_0_ = f32[1,8,2,128,128]{4,3,2,1,0:T(8,128)} custom-call(s32[1]{0:T(128)} %bitcast.flags_ref, f32[2,2,128,128]{3,2,1,0:T(8,128)S(1)} %get-tuple-element.41.raw_ref, f32[2,2,128,128]{3,2,1,0:T(8,128)S(1)} %collective-permute-done.17.near_ref, ...), custom_call_target="tpu_custom_call", output_to_operand_aliasing={{}: (5, {})} | custom-call | tf_op jit(solution)/shard_map/skew/pallas_call | solution.py:178
  72.3 0.9 %skew.6.refs_0_ = f32[1,8,2,128,128]{4,3,2,1,0:T(8,128)} custom-call(s32[1]{0:T(128)} %bitcast.flags_ref, f32[2,2,128,128]{3,2,1,0:T(8,128)S(1)} %get-tuple-element.40.raw_ref, f32[2,2,128,128]{3,2,1,0:T(8,128)S(1)} %collective-permute-done.16.near_ref, f32[2,128,128]{2,1,0:T(8,128)S(1)} %collective-permute-done.12.far_real_ref, ...), custom_call_target="tpu_custom_call", output_to_operand_aliasing={{}: (5, {})} | custom-call | tf_op jit(solution)/shard_map/skew/pallas_call | solution.py:178
  73.5 0.9 %skew.7 = f32[1,8,2,128,128]{4,3,2,1,0:T(8,128)} custom-call(s32[1]{0:T(128)} %bitcast.flags_ref, f32[2,2,128,128]{3,2,1,0:T(8,128)S(1)} %get-tuple-element.37.raw_ref, f32[2,2,128,128]{3,2,1,0:T(8,128)S(1)} %collective-permute-done.11.near_ref, f32[2,128,128]{2,1,0:T(8,128)S(1)} %collective-permute-done.13.far_real_ref, ...), custom_call_target="tpu_custom_call", output_to_operand_aliasing={{}: (5, {})} | custom-call | tf_op jit(solution)/shard_map/skew/pallas_call | solution.py:178
  (40 shorter events, 4.9 us)
Async XLA Ops:
  0.0 3.1 %collective-permute-start = (s32[5,1,1]{0,2,1:T(1,128)}, s32[5,1,1]{0,2,1:T(1,128)S(1)}, u32[]{:S(2)}, u32[]{:S(2)}) collective-permute-start(s32[5,1,1]{0,2,1:T(1,128)} %param.5), channel_id=1, source_target_pairs={{16,0},{0,16},{17,1},{1,17},{18,2},{2,18},{19,3},{3,19},{20,4},{4,... | collective-permute-start | bytes 68 | tf_op jit(solution)/shard_map/ppermute | solution.py:235
  5.0 2.5 %copy-start = (f32[5,8,2,128,128]{4,3,2,1,0:T(8,128)S(1)}, f32[5,8,2,128,128]{4,3,2,1,0:T(8,128)}, u32[]{:S(2)}) copy-start(f32[5,8,2,128,128]{4,3,2,1,0:T(8,128)} %refs_1_.5) | copy-start | bytes 15728644
  7.5 1.5 %copy-start.2 = (f32[1,15,2,128,128]{4,3,2,1,0:T(8,128)S(1)}, f32[1,15,2,128,128]{4,3,2,1,0:T(8,128)}, u32[]{:S(2)}) copy-start(f32[1,15,2,128,128]{4,3,2,1,0:T(8,128)} %green_ref.5) | copy-start | bytes 5898244
  10.7 6.0 %copy-start.8 = (s32[5,1,1]{0,2,1:T(1,128)S(1)}, s32[5,1,1]{0,2,1:T(1,128)}, u32[]{:S(2)}) copy-start(s32[5,1,1]{0,2,1:T(1,128)} %param.5) | copy-start | bytes 64
  10.7 8.6 %copy-start.3 = (f32[1,15,2,128,128]{4,3,2,1,0:T(8,128)S(1)}, f32[1,15,2,128,128]{4,3,2,1,0:T(8,128)}, u32[]{:S(2)}) copy-start(f32[1,15,2,128,128]{4,3,2,1,0:T(8,128)} %green_ref.5) | copy-start | bytes 5898244
  10.7 14.5 %collective-permute-start.4 = (f32[2,2,128,128]{3,2,1,0:T(8,128)S(1)}, f32[2,2,128,128]{3,2,1,0:T(8,128)S(1)}, u32[]{:S(2)}, u32[]{:S(2)}) collective-permute-start(f32[2,2,128,128]{3,2,1,0:T(8,128)S(1)} %correlate.5), channel_id=1, source_target_pairs={{0,16},{16,0},{1,17},{17,1},{2,18},{18,2},{3,19},{19,3},{4,20},{20... | collective-permute-start | bytes 786440 | tf_op jit(solution)/shard_map/ppermute | solution.py:248
  15.2 0.7 copy-start.6
  15.9 0.7 copy-start.7
  16.6 12.8 %collective-permute-start.3 = (f32[2,2,128,128]{3,2,1,0:T(8,128)}, f32[2,2,128,128]{3,2,1,0:T(8,128)S(1)}, u32[]{:S(2)}, u32[]{:S(2)}) collective-permute-start(f32[2,2,128,128]{3,2,1,0:T(8,128)} %get-tuple-element.29), channel_id=1, source_target_pairs={{0,16},{16,0},{1,17},{17,1},{2,18},{18,2},{3,19},{19,3},{4,20},{20... | collective-permute-start | bytes 786440 | tf_op jit(solution)/shard_map/ppermute | solution.py:248
  19.2 2.5 %copy-start.1 = (f32[5,8,2,128,128]{4,3,2,1,0:T(8,128)S(1)}, f32[5,8,2,128,128]{4,3,2,1,0:T(8,128)}, u32[]{:S(2)}) copy-start(f32[5,8,2,128,128]{4,3,2,1,0:T(8,128)} %refs_1_.5) | copy-start | bytes 15728644
  24.5 0.7 copy-start.4
  25.3 9.9 %collective-permute-start.5 = (f32[2,128,128]{2,1,0:T(8,128)S(1)}, f32[2,128,128]{2,1,0:T(8,128)S(1)}, u32[]{:S(2)}, u32[]{:S(2)}) collective-permute-start(f32[2,128,128]{2,1,0:T(8,128)S(1)} %get-tuple-element.31), channel_id=1, source_target_pairs={{2,0},{3,4},{6,1},{7,5},{8,10},{9,14},{12,11},{13,15},{18,16},{19,... | collective-permute-start | bytes 393224 | tf_op jit(solution)/shard_map/ppermute | solution.py:255
  26.6 12.3 %collective-permute-start.6 = (f32[2,128,128]{2,1,0:T(8,128)S(1)}, f32[2,128,128]{2,1,0:T(8,128)S(1)}, u32[]{:S(2)}, u32[]{:S(2)}) collective-permute-start(f32[2,128,128]{2,1,0:T(8,128)S(1)} %get-tuple-element.32), channel_id=1, source_target_pairs={{2,10},{3,11},{6,14},{7,15},{8,0},{9,1},{12,4},{13,5},{18,26},{19,... | collective-permute-start | bytes 393224 | tf_op jit(solution)/shard_map/ppermute | solution.py:256
  27.9 18.7 %collective-permute-start.2 = (f32[2,2,128,128]{3,2,1,0:T(8,128)}, f32[2,2,128,128]{3,2,1,0:T(8,128)S(1)}, u32[]{:S(2)}, u32[]{:S(2)}) collective-permute-start(f32[2,2,128,128]{3,2,1,0:T(8,128)} %copy-done.7), channel_id=1, source_target_pairs={{0,16},{16,0},{1,17},{17,1},{2,18},{18,2},{3,19},{19,3},{4,20},{20... | collective-permute-start | bytes 786440 | tf_op jit(solution)/shard_map/ppermute | solution.py:248
  38.9 1.0 %copy-start.5 = (f32[2,2,128,128]{3,2,1,0:T(8,128)S(1)}, f32[2,2,128,128]{3,2,1,0:T(8,128)}, u32[]{:S(2)}) copy-start(f32[2,2,128,128]{3,2,1,0:T(8,128)} %copy-done.4) | copy-start | bytes 786436
  39.9 6.7 %collective-permute-start.7 = (f32[2,128,128]{2,1,0:T(8,128)S(1)}, f32[2,128,128]{2,1,0:T(8,128)S(1)}, u32[]{:S(2)}, u32[]{:S(2)}) collective-permute-start(f32[2,128,128]{2,1,0:T(8,128)S(1)} %get-tuple-element.33), channel_id=1, source_target_pairs={{2,0},{3,4},{6,1},{7,5},{8,10},{9,14},{12,11},{13,15},{18,16},{19,... | collective-permute-start | bytes 393224 | tf_op jit(solution)/shard_map/ppermute | solution.py:255
  39.9 6.8 %collective-permute-start.8 = (f32[2,128,128]{2,1,0:T(8,128)S(1)}, f32[2,128,128]{2,1,0:T(8,128)S(1)}, u32[]{:S(2)}, u32[]{:S(2)}) collective-permute-start(f32[2,128,128]{2,1,0:T(8,128)S(1)} %get-tuple-element.34), channel_id=1, source_target_pairs={{2,10},{3,11},{6,14},{7,15},{8,0},{9,1},{12,4},{13,5},{18,26},{19,... | collective-permute-start | bytes 393224 | tf_op jit(solution)/shard_map/ppermute | solution.py:256
  43.5 9.6 %collective-permute-start.1 = (f32[2,2,128,128]{3,2,1,0:T(8,128)}, f32[2,2,128,128]{3,2,1,0:T(8,128)S(1)}, u32[]{:S(2)}, u32[]{:S(2)}) collective-permute-start(f32[2,2,128,128]{3,2,1,0:T(8,128)} %copy-done.6), channel_id=1, source_target_pairs={{0,16},{16,0},{1,17},{17,1},{2,18},{18,2},{3,19},{19,3},{4,20},{20... | collective-permute-start | bytes 786440 | tf_op jit(solution)/shard_map/ppermute | solution.py:248
  44.7 16.5 %collective-permute-start.18 = (f32[2,2,128,128]{3,2,1,0:T(8,128)S(1)}, f32[2,2,128,128]{3,2,1,0:T(8,128)S(1)}, u32[]{:S(2)}, u32[]{:S(2)}) collective-permute-start(f32[2,2,128,128]{3,2,1,0:T(8,128)S(1)} %get-tuple-element.42.raw_ref), channel_id=1, source_target_pairs={{1,4},{4,1},{11,14},{14,11},{17,20},{20,17},{27,30},{30,27}} | collective-permute-start | bytes 786440 | tf_op jit(solution)/shard_map/ppermute | solution.py:257
  46.8 9.9 %collective-permute-start.10 = (f32[2,128,128]{2,1,0:T(8,128)S(1)}, f32[2,128,128]{2,1,0:T(8,128)S(1)}, u32[]{:S(2)}, u32[]{:S(2)}) collective-permute-start(f32[2,128,128]{2,1,0:T(8,128)S(1)} %get-tuple-element.36), channel_id=1, source_target_pairs={{2,10},{3,11},{6,14},{7,15},{8,0},{9,1},{12,4},{13,5},{18,26},{19,... | collective-permute-start | bytes 393224 | tf_op jit(solution)/shard_map/ppermute | solution.py:256
  51.2 6.4 %collective-permute-start.9 = (f32[2,128,128]{2,1,0:T(8,128)S(1)}, f32[2,128,128]{2,1,0:T(8,128)S(1)}, u32[]{:S(2)}, u32[]{:S(2)}) collective-permute-start(f32[2,128,128]{2,1,0:T(8,128)S(1)} %get-tuple-element.35), channel_id=1, source_target_pairs={{2,0},{3,4},{6,1},{7,5},{8,10},{9,14},{12,11},{13,15},{18,16},{19,... | collective-permute-start | bytes 393224 | tf_op jit(solution)/shard_map/ppermute | solution.py:255
  51.2 20.3 %collective-permute-start.17 = (f32[2,2,128,128]{3,2,1,0:T(8,128)S(1)}, f32[2,2,128,128]{3,2,1,0:T(8,128)S(1)}, u32[]{:S(2)}, u32[]{:S(2)}) collective-permute-start(f32[2,2,128,128]{3,2,1,0:T(8,128)S(1)} %get-tuple-element.41.raw_ref), channel_id=1, source_target_pairs={{1,4},{4,1},{11,14},{14,11},{17,20},{20,17},{27,30},{30,27}} | collective-permute-start | bytes 786440 | tf_op jit(solution)/shard_map/ppermute | solution.py:257
  53.1 19.2 %collective-permute-start.16 = (f32[2,2,128,128]{3,2,1,0:T(8,128)S(1)}, f32[2,2,128,128]{3,2,1,0:T(8,128)S(1)}, u32[]{:S(2)}, u32[]{:S(2)}) collective-permute-start(f32[2,2,128,128]{3,2,1,0:T(8,128)S(1)} %get-tuple-element.40.raw_ref), channel_id=1, source_target_pairs={{1,4},{4,1},{11,14},{14,11},{17,20},{20,17},{27,30},{30,27}} | collective-permute-start | bytes 786440 | tf_op jit(solution)/shard_map/ppermute | solution.py:257
  57.6 6.5 %collective-permute-start.12 = (f32[2,128,128]{2,1,0:T(8,128)S(1)}, f32[2,128,128]{2,1,0:T(8,128)S(1)}, u32[]{:S(2)}, u32[]{:S(2)}) collective-permute-start(f32[2,128,128]{2,1,0:T(8,128)S(1)} %get-tuple-element.38), channel_id=1, source_target_pairs={{2,0},{3,4},{6,1},{7,5},{8,10},{9,14},{12,11},{13,15},{18,16},{19,... | collective-permute-start | bytes 393224 | tf_op jit(solution)/shard_map/ppermute | solution.py:255
  57.7 7.7 %collective-permute-start.14 = (f32[2,128,128]{2,1,0:T(8,128)S(1)}, f32[2,128,128]{2,1,0:T(8,128)S(1)}, u32[]{:S(2)}, u32[]{:S(2)}) collective-permute-start(f32[2,128,128]{2,1,0:T(8,128)S(1)} %get-tuple-element.39), channel_id=1, source_target_pairs={{2,10},{3,11},{6,14},{7,15},{8,0},{9,1},{12,4},{13,5},{18,26},{19,... | collective-permute-start | bytes 393224 | tf_op jit(solution)/shard_map/ppermute | solution.py:256
  61.2 12.3 %collective-permute-start.11 = (f32[2,2,128,128]{3,2,1,0:T(8,128)S(1)}, f32[2,2,128,128]{3,2,1,0:T(8,128)S(1)}, u32[]{:S(2)}, u32[]{:S(2)}) collective-permute-start(f32[2,2,128,128]{3,2,1,0:T(8,128)S(1)} %get-tuple-element.37.raw_ref), channel_id=1, source_target_pairs={{1,4},{4,1},{11,14},{14,11},{17,20},{20,17},{27,30},{30,27}} | collective-permute-start | bytes 786440 | tf_op jit(solution)/shard_map/ppermute | solution.py:257
  64.1 9.2 %collective-permute-start.13 = (f32[2,128,128]{2,1,0:T(8,128)S(1)}, f32[2,128,128]{2,1,0:T(8,128)S(1)}, u32[]{:S(2)}, u32[]{:S(2)}) collective-permute-start(f32[2,128,128]{2,1,0:T(8,128)S(1)} %collective-permute-done.12.far_real_ref), channel_id=1, source_target_pairs={{0,8},{4,12},{1,9},{5,13},{10,2},{14,6},{11,3},{15,7},{16,24},{20,... | collective-permute-start | bytes 393224 | tf_op jit(solution)/shard_map/ppermute | solution.py:260
  65.4 8.1 %collective-permute-start.15 = (f32[2,128,128]{2,1,0:T(8,128)S(1)}, f32[2,128,128]{2,1,0:T(8,128)S(1)}, u32[]{:S(2)}, u32[]{:S(2)}) collective-permute-start(f32[2,128,128]{2,1,0:T(8,128)S(1)} %collective-permute-done.14.far_imag_ref), channel_id=1, source_target_pairs={{10,8},{11,12},{14,9},{15,13},{0,2},{1,6},{4,3},{5,7},{26,24},{27,... | collective-permute-start | bytes 393224 | tf_op jit(solution)/shard_map/ppermute | solution.py:261

commit v2 on v0

v2 whole, which is shorter than its diff:
```python
import functools

import jax
import jax.numpy as jnp
from jax import lax
from jax.experimental import pallas as pl
from jax.experimental.pallas import tpu as pltpu
from jax.sharding import PartitionSpec as P

NE = 8
TIE = True
COUNTS = (2, 2, 2, 2)
NEAR_CUTS = (1, 2, 3)
HOPS = (0, 1, -1, 2, -2)
SUBLANES = 8
AXES = ("ka", "br", "bc")
VMEM_LIMIT = 32 * 1024 * 1024


def correlate_rows(green_ref, screened_ref, table_ref, stops, first, counts, out_refs, low, high):
    freqs = screened_ref.shape[1]
    energies = sum(counts)

    def rows_step(step, carry):
        at = pl.ds(pl.multiple_of(step * SUBLANES, SUBLANES), SUBLANES)

        def inter(freq, part):
            value = screened_ref[table_ref[stops[0]], freq, part, at, :]
            for stop in stops[1:]:
                value = value + screened_ref[table_ref[stop], freq, part, at, :]
            return value

        real = [None] * energies
        imag = [None] * energies
        weights = [(inter(freq, 0), inter(freq, 1)) for freq in range(freqs)]
        for lag in range(energies + freqs - 1):
            green_real = green_ref[0, first + lag, 0, at, :]
            green_imag = green_ref[0, first + lag, 1, at, :]
            for energy in range(energies):
                freq = energy + freqs - 1 - lag
                if 0 <= freq < freqs:
                    inter_real, inter_imag = weights[freq]
                    real_term = green_real * inter_imag + green_imag * inter_real
                    imag_term = green_real * inter_real - green_imag * inter_imag
                    if real[energy] is None:
                        real[energy], imag[energy] = -real_term, imag_term
                    else:
                        real[energy] = real[energy] - real_term
                        imag[energy] = imag[energy] + imag_term
        energy = 0
        for out_ref, count in zip(out_refs, counts):
            for place in range(count):
                out_ref[place, 0, at, :] = real[energy]
                out_ref[place, 1, at, :] = imag[energy]
                energy += 1
        return carry

    lax.fori_loop(low // SUBLANES, high // SUBLANES, rows_step, 0)


def fetch_kernel(stops, first, counts, blocks, table_hbm, green_hbm, screened_hbm, green_ref, screened_ref, *refs):
    out_refs, (table_ref, table_sem, sem) = refs[:-3], refs[-3:]
    rows = green_ref.shape[3] // blocks
    table_copy = pltpu.make_async_copy(table_hbm, table_ref, table_sem)
    table_copy.start()
    copies = []
    for block in range(blocks):
        at = pl.ds(block * rows, rows)
        pair = [
            pltpu.make_async_copy(source.at[:, :, :, at], target.at[:, :, :, at], sem.at[block, which])
            for which, (source, target) in enumerate(((green_hbm, green_ref), (screened_hbm, screened_ref)))
        ]
        for copy in pair:
            copy.start()
        copies.append(pair)
    table_copy.wait()
    for block, pair in enumerate(copies):
        for copy in pair:
            copy.wait()
        correlate_rows(
            green_ref, screened_ref, table_ref, stops, first, counts, out_refs, block * rows, (block + 1) * rows
        )


def on_hbm(*arrays):
    return [pltpu.with_memory_space_constraint(array, pltpu.HBM) for array in arrays]


def run_shapes(green, spans):
    return [jax.ShapeDtypeStruct((count,) + green.shape[2:], jnp.float32) for _, count in spans]


def fetch(green, screened, table, stops, spans, blocks):
    vmem = pl.BlockSpec(memory_space=pltpu.VMEM)
    whole = pl.BlockSpec(memory_space=pltpu.HBM)
    counts = [count for _, count in spans]
    results = pl.pallas_call(
        functools.partial(fetch_kernel, stops, spans[0][0], counts, blocks),
        in_specs=[whole] * 3,
        out_specs=[vmem] * (2 + len(spans)),
        out_shape=[jax.ShapeDtypeStruct(array.shape, array.dtype) for array in (green, screened)]
        + run_shapes(green, spans),
        scratch_shapes=[
            pltpu.SMEM(table.shape, table.dtype),
            pltpu.SemaphoreType.DMA,
            pltpu.SemaphoreType.DMA((blocks, 2)),
        ],
        compiler_params=pltpu.CompilerParams(vmem_limit_bytes=VMEM_LIMIT),
        name="fetch",
    )(table, green, screened)
    return results[0], results[1], results[2:]


def correlate_kernel(stops, first, counts, table_ref, green_ref, screened_ref, *out_refs):
    correlate_rows(
        green_ref, screened_ref, table_ref, stops, first, counts, out_refs, 0, green_ref.shape[3]
    )


def correlate(green, screened, table, stops, spans):
    if not spans:
        return []
    vmem = pl.BlockSpec(memory_space=pltpu.VMEM)
    counts = [count for _, count in spans]
    return pl.pallas_call(
        functools.partial(correlate_kernel, stops, spans[0][0], counts),
        in_specs=[pl.BlockSpec(memory_space=pltpu.SMEM), vmem, vmem],
        out_specs=[vmem] * len(spans),
        out_shape=run_shapes(green, spans),
        compiler_params=pltpu.CompilerParams(vmem_limit_bytes=VMEM_LIMIT),
        name="correlate",
    )(table, green, screened)


def place_of_device():
    row, col = lax.axis_index("br"), lax.axis_index("bc")
    half = lax.axis_size("br") // 2
    return (row // half) != (col // half), row == col


def mix_kernel(received, held, own_ref, *refs):
    recv_refs = refs[:received]
    held_refs = refs[received : received + sum(held)]
    raw_ref, col_ref, row_ref = refs[received + sum(held) :]
    far, _ = place_of_device()
    queue = list(held_refs)
    holds = [queue.pop(0) if has else None for has in held]
    count = own_ref.shape[0]
    for part, hold_ref, send_ref in zip((0, 1), holds, (col_ref, row_ref)):
        for place in range(send_ref.shape[0]):
            value = None
            if place < count:
                value = own_ref[place, part]
                for ref in recv_refs:
                    value = value + ref[place, part]
                raw_ref[place, part] = value
            if hold_ref is not None and place < hold_ref.shape[0]:
                kept = hold_ref[place]
                value = kept if value is None else jnp.where(far, value, kept)
            if value is not None:
                send_ref[place] = value


def mix(own, received, held_columns, held_rows):
    vmem = pl.BlockSpec(memory_space=pltpu.VMEM)
    held = [array is not None for array in (held_columns, held_rows)]
    holds = [array for array in (held_columns, held_rows) if array is not None]
    lengths = [max(own.shape[0], array.shape[0] if array is not None else 0) for array in (held_columns, held_rows)]
    shapes = [own.shape] + [(length,) + own.shape[2:] for length in lengths]
    return pl.pallas_call(
        functools.partial(mix_kernel, len(received), held),
        in_specs=[vmem] * (1 + len(received) + len(holds)),
        out_specs=[vmem] * 3,
        out_shape=[jax.ShapeDtypeStruct(shape, jnp.float32) for shape in shapes],
        compiler_params=pltpu.CompilerParams(vmem_limit_bytes=VMEM_LIMIT),
        name="mix",
    )(own, *received, *holds)


def pack_kernel(*refs):
    out_ref = refs[-1]
    far, _ = place_of_device()

    @pl.when(jnp.logical_not(far))
    def _():
        at = 0
        for ref in refs[:-1]:
            out_ref[pl.ds(at, ref.shape[0])] = ref[...]
            at += ref.shape[0]


def pack(raws):
    if len(raws) == 1:
        return raws[0]
    vmem = pl.BlockSpec(memory_space=pltpu.VMEM)
    return pl.pallas_call(
        pack_kernel,
        in_specs=[vmem] * len(raws),
        out_specs=vmem,
        out_shape=jax.ShapeDtypeStruct((sum(raw.shape[0] for raw in raws),) + raws[0].shape[1:], jnp.float32),
        compiler_params=pltpu.CompilerParams(vmem_limit_bytes=VMEM_LIMIT),
        name="pack",
    )(*raws)


def skew_kernel(which, places, *refs):
    width = 2 + len(which)
    parts = [refs[width * at : width * (at + 1)] for at in range(len(places))]
    out_ref, done_ref, sem = refs[-3:]
    far, own = place_of_device()
    start = places[0][0]

    def write(partner):
        for (raw_ref, near_ref, *far_refs), (first, near_first, far_firsts) in zip(parts, places):
            for at in range(raw_ref.shape[0]):
                for slot, (kind, far_ref, far_first) in enumerate(zip(which, far_refs, far_firsts)):
                    raw = raw_ref[at, kind]
                    mirror = partner(raw, near_ref, near_first + at, kind, far_ref, far_first + at).T
                    done_ref[first - start + at, slot] = (raw + mirror if kind else raw - mirror) * 0.5

    @pl.when(far)
    def _():
        write(lambda raw, near_ref, near_at, kind, far_ref, far_at: far_ref[far_at])

    @pl.when(jnp.logical_and(jnp.logical_not(far), jnp.logical_not(own)))
    def _():
        write(lambda raw, near_ref, near_at, kind, far_ref, far_at: near_ref[near_at, kind])

    @pl.when(own)
    def _():
        write(lambda raw, near_ref, near_at, kind, far_ref, far_at: raw)

    target = out_ref.at[0, pl.ds(start, done_ref.shape[0]), pl.ds(which[0], len(which))]
    copy = pltpu.make_async_copy(done_ref, target, sem)
    copy.start()
    copy.wait()


def skew(parts, which, energies, out):
    vmem = pl.BlockSpec(memory_space=pltpu.VMEM)
    whole = pl.BlockSpec(memory_space=pl.ANY)
    operands = [array for _, raw, near, _, fars, _ in parts for array in (raw, near, *fars)]
    in_specs = [vmem] * len(operands)
    aliases = {}
    if out is not None:
        aliases = {len(operands): 0}
        operands.append(out)
        in_specs.append(whole)
    shape = parts[0][1].shape
    count = sum(raw.shape[0] for _, raw, *_ in parts)
    return pl.pallas_call(
        functools.partial(skew_kernel, which, [(part[0], part[3], part[5]) for part in parts]),
        in_specs=in_specs,
        out_specs=whole,
        out_shape=jax.ShapeDtypeStruct((1, energies) + shape[1:], jnp.float32),
        scratch_shapes=[pltpu.VMEM((count, len(which)) + shape[2:], jnp.float32), pltpu.SemaphoreType.DMA],
        input_output_aliases=aliases,
        compiler_params=pltpu.CompilerParams(vmem_limit_bytes=VMEM_LIMIT),
        name="skew",
    )(*operands)


def grid_moves(momenta, side):
    half = side // 2

    def number(momentum, row_half, row_low, col_half, col_low):
        return (momentum * side + row_half * half + row_low) * side + col_half * half + col_low

    over_columns, over_rows, near = ([], []), ([], []), []
    for momentum in range(momenta):
        for a in range(2):
            for row in range(half):
                for col in range(half):
                    b = 1 - a
                    here = number(momentum, a, row, b, col)
                    mirror = number(momentum, b, col, a, row)
                    by_columns = number(momentum, a, col, a, row)
                    by_rows = number(momentum, b, row, b, col)
                    over_columns[0].append((here, by_columns))
                    over_columns[1].append((by_rows, mirror))
                    over_rows[0].append((here, by_rows))
                    over_rows[1].append((by_columns, mirror))
                    if row != col:
                        near.append((number(momentum, a, row, a, col), number(momentum, a, col, a, row)))
    return over_columns, over_rows, near


def send(array, axes, pairs, what):
    with jax.named_scope(what):
        return lax.ppermute(array, axes, pairs)


def on_device(counts, near_cuts, green_lesser, screened, slot_table):
    momenta = lax.axis_size("ka")
    over_columns, over_rows, near_pairs = grid_moves(momenta, lax.axis_size("br"))
    groups = {}
    for stop, hop in enumerate(HOPS):
        groups.setdefault(hop % momenta, []).append(stop)
    spans = [(sum(counts[:run]), count) for run, count in enumerate(counts)]
    runs = len(spans)
    groups_near = list(zip((0, *near_cuts), (*near_cuts, runs)))

    tables = {}
    for shift in groups:
        table = slot_table
        if shift:
            table = lax.ppermute(table, "ka", [((k + shift) % momenta, k) for k in range(momenta)])
        tables[shift] = table.reshape(len(HOPS))
    green, inter, own = fetch(*on_hbm(green_lesser, screened, tables.pop(0)), groups.pop(0), spans, 4)

    terms = [{} for _ in spans]
    for some in (range(1), range(1, runs)):
        for shift, stops in groups.items():
            found = correlate(green, inter, tables[shift], stops, [spans[run] for run in some])
            for run, term in zip(some, found):
                terms[run][shift] = term

    def exchange(run):
        return [
            send(term, "ka", [(k, (k + shift) % momenta) for k in range(momenta)], f"momentum_{run}")
            for shift, term in terms[run].items()
        ]

    arrived = [exchange(run) for run in range(runs)]
    raws, by_columns, by_rows = [], [], []
    for run in range(runs):
        raw, over_first, over_second = mix(
            own[run],
            arrived[run],
            by_rows[run - 1] if run >= 1 else None,
            by_columns[run - 2] if run >= 2 else None,
        )
        raws.append(raw)
        by_columns.append(send(over_first, AXES, sum(over_columns, []), f"columns_{run}"))
        by_rows.append(send(over_second, AXES, sum(over_rows, []), f"rows_{run}"))
    nears, near_places = [], []
    for low, high in groups_near:
        near = send(pack(raws[low:high]), AXES, near_pairs, f"near_{low}")
        for run in range(low, high):
            nears.append(near)
            near_places.append(spans[run][0] - spans[low][0])
    by_columns.append(send(by_rows[-1], AXES, over_columns[1], f"columns_{runs}"))

    def part(run, fars, far_firsts):
        return spans[run][0], raws[run], nears[run], near_places[run], fars, far_firsts

    out = None
    for run in range(runs - 2):
        out = skew([part(run, [by_rows[run + 2], by_columns[run + 1]], [0, 0])], (0, 1), NE, out)
    last = by_columns[runs - 1]
    if out is not None and TIE:
        last, out = lax.optimization_barrier((last, out))
    by_rows.append(send(by_columns[runs - 2], AXES, over_rows[1], f"rows_{runs}"))
    by_rows.append(send(last, AXES, over_rows[1], f"rows_{runs + 1}"))
    ends = (runs - 2, runs - 1)
    out = skew([part(run, [by_columns[run + 1]], [0]) for run in ends], (1,), NE, out)
    return skew([part(run, [by_rows[run + 2]], [0]) for run in ends], (0,), NE, out)


def solution(mesh):
    in_specs = (
        P("ka", None, None, "br", "bc"),
        P(None, None, None, "br", "bc"),
        P(None, "ka", None),
    )
    out_specs = P("ka", None, None, "br", "bc")
    return jax.shard_map(
        functools.partial(on_device, COUNTS, NEAR_CUTS), mesh=mesh, in_specs=in_specs, out_specs=out_specs, check_vma=False
    )
```

time: 165 us -> 57.9 us (0.35)
  waiting for transfers between devices: 87.6 us -> 5.11 us
  starting transfers between devices: 11.1 us -> 41.3 us
  blocking collectives: 30.1 us -> 0 us
  local copies, waits for them, and re-layouts: 12.8 us -> 0 us
  other arithmetic: 11.9 us -> 0 us
  Pallas kernels: 0 us -> 10.2 us
  between operations: 9.92 us -> 0.23 us
    ppermute x2 -> x20, waiting for transfers between devices: 61.3 us -> 5.11 us  [the longest x19 5.11 us: send(): return lax.ppermute(array, axes, pairs)]
    ppermute x2 -> x20, starting transfers between devices: 3.19 us -> 41.3 us  [the longest x19 39.2 us: send(): return lax.ppermute(array, axes, pairs)]
    all_to_all x1 -> x0, blocking collectives: 30.1 us -> none  [on_device(): lax.all_to_all(symmetric, ('br', 'bc'), split_axis=1, concat_axis=0, tile...]
    all_to_all x1 -> x0, waiting for transfers between devices: 26.2 us -> none  [on_device(): lax.all_to_all(flattened, ('br', 'bc'), split_axis=0, concat_axis=1, tile...]
    another operation x10 -> x0, other arithmetic: 10.4 us -> none  [stop_terms(): blocks_out = [jnp.stack((real_sum, imag_sum), 1)]]
    pallas_call x0 -> x11, Pallas kernels: none -> 10.2 us  [the longest x1 3.59 us: fetch(): pl.pallas_call(functools.partial(fetch_kernel, stops, spans[0][0], counts...]
    all_to_all x1 -> x0, starting transfers between devices: 7.93 us -> none  [on_device(): lax.all_to_all(flattened, ('br', 'bc'), split_axis=0, concat_axis=1, tile...]
    squeeze x4 -> x0, local copies, waits for them, and re-layouts: 5.97 us -> none  [the longest x3 3.12 us: stop_terms(): window = remote[0, lag_start:lag_start + energies]]
  transfers between devices with their start and end apart: 3 -> 20, of which waited for: 3 -> 4; matrix products, arithmetic and copies ran while one was open for 7% -> 0% of each run, Pallas kernels for 0% -> 14%
where the time goes in v2:
time: 57.9 us; the launch traced here: 56.8 us
  starting transfers between devices  41.3 us (71%)
  Pallas kernels  10.2 us (18%)
  waiting for transfers between devices  5.11 us (9%)
    ppermute x19, starting transfers between devices, send(): return lax.ppermute(array, axes, pairs)  39.2 us
    ppermute x19, waiting for transfers between devices, send(): return lax.ppermute(array, axes, pairs)  5.11 us
    pallas_call x1, Pallas kernels, fetch(): pl.pallas_call(functools.partial(fetch_kernel, stops, spans[0][0], counts...  3.59 us
    pallas_call x4, Pallas kernels, skew(): pl.pallas_call(functools.partial(skew_kernel, which, [(part[0], part[3],...  3.44 us
    pallas_call x2, Pallas kernels, correlate(): pl.pallas_call(functools.partial(correlate_kernel, stops, spans[0][0], co...  3.01 us
    ppermute x1, starting transfers between devices, on_device(): lax.ppermute(table, 'ka', [((k + shift) % momenta, k) for k in range(mome...  2.04 us
  transfers between devices with their start and end apart: 20, of which 4 were waited for; matrix products, arithmetic and copies ran while one was open for 0% of the time, Pallas kernels for 14%

profile of v2, /device:TPU:1, one launch (start us, length us, event | category | flops | bytes accessed | tf_op | source)
XLA Modules:
  0.0 56.8 jit_solution(14015129997236518513)
XLA Ops:
  0.0 2.0 %collective-permute-start = (s32[5,1,1]{0,2,1:T(1,128)}, s32[5,1,1]{0,2,1:T(1,128)S(1)}, u32[]{:S(2)}, u32[]{:S(2)}) collective-permute-start(s32[5,1,1]{0,2,1:T(1,128)} %param.5), channel_id=1, source_target_pairs={{16,0},{0,16},{17,1},{1,17},{18,2},{2,18},{19,3},{3,19},{20,4},{4,... | collective-permute-start | bytes 68 | tf_op jit(solution)/shard_map/ppermute | solution.py:307
  2.0 3.6 %fetch.1 = (f32[1,15,2,128,128]{4,3,2,1,0:T(8,128)S(1)}, f32[5,8,2,128,128]{4,3,2,1,0:T(8,128)S(1)}, f32[2,2,128,128]{3,2,1,0:T(8,128)S(1)}, f32[2,2,128,128]{3,...) custom-call(s32[5]{0:T(128)} %bitcast.4, f32[1,15,2,128,128]{4,3,2,1,0:T(8,128)} %green_hbm.1, ...), custom_call_target="tpu_custom_call" | custom-call | tf_op jit(solution)/shard_map/fetch/pallas_call | solution.py:97
  5.7 1.2 %correlate.3 = f32[2,2,128,128]{3,2,1,0:T(8,128)S(1)} custom-call(s32[5]{0:T(128)S(1)} %bitcast.2, f32[1,15,2,128,128]{4,3,2,1,0:T(8,128)S(1)} %get-tuple-element.29.green_ref, f32[5,8,2,128,128]{4,3,2,1,0:T(8,128)S(1)} %get-tuple-element.30.screened_ref), custom_call_target="tpu_custom_call" | custom-call | tf_op jit(solution)/shard_map/correlate/pallas_call | solution.py:125
  6.9 0.1 collective-permute-start.3
  7.0 1.8 %correlate.2 = (f32[2,2,128,128]{3,2,1,0:T(8,128)S(1)}, f32[2,2,128,128]{3,2,1,0:T(8,128)S(1)}, f32[2,2,128,128]{3,2,1,0:T(8,128)S(1)}) custom-call(s32[5]{0:T(128)S(1)} %bitcast.3, f32[1,15,2,128,128]{4,3,2,1,0:T(8,128)S(1)} %get-tuple-element.29.green_ref, f32[5,8,2,128,128]{4,3,2,1,0:T(8,128)S(1)} %get-tuple-element.30.screened_ref), custom_call_target="tpu_custom_call" | custom-call | tf_op jit(solution)/shard_map/correlate/pallas_call | solution.py:125
  8.8 1.5 %collective-permute-start.2 = (f32[2,2,128,128]{3,2,1,0:T(8,128)S(1)}, f32[2,2,128,128]{3,2,1,0:T(8,128)S(1)}, u32[]{:S(2)}, u32[]{:S(2)}) collective-permute-start(f32[2,2,128,128]{3,2,1,0:T(8,128)S(1)} %get-tuple-element.33), channel_id=1, source_target_pairs={{0,16},{16,0},{1,17},{17,1},{2,18},{18,2},{3,19},{19,3},{4,20},{20... | collective-permute-start | bytes 786440 | tf_op jit(solution)/shard_map/momentum_1/ppermute | solution.py:290
  10.3 0.1 collective-permute-start.1
  10.4 3.5 %collective-permute-done.3.refs_0_ = f32[2,2,128,128]{3,2,1,0:T(8,128)S(1)} collective-permute-done((f32[2,2,128,128]{3,2,1,0:T(8,128)S(1)}, f32[2,2,128,128]{3,2,1,0:T(8,128)S(1)}, u32[]{:S(2)}, u32[]{:S(2)}) %collective-permute-start.3) | collective-permute-done | bytes 262176 | tf_op jit(solution)/shard_map/momentum_0/ppermute | solution.py:290
  13.9 1.3 %collective-permute-start.4 = (f32[2,128,128]{2,1,0:T(8,128)S(1)}, f32[2,128,128]{2,1,0:T(8,128)S(1)}, u32[]{:S(2)}, u32[]{:S(2)}) collective-permute-start(f32[2,128,128]{2,1,0:T(8,128)S(1)} %get-tuple-element.35), channel_id=1, source_target_pairs={{2,10},{3,11},{6,14},{7,15},{8,0},{9,1},{12,4},{13,5},{18,26},{19,... | collective-permute-start | bytes 393224 | tf_op jit(solution)/shard_map/rows_0/ppermute | solution.py:290
  15.2 0.3 collective-permute-start.10
  15.4 7.1 %collective-permute-start.6 = (f32[2,128,128]{2,1,0:T(8,128)S(1)}, f32[2,128,128]{2,1,0:T(8,128)S(1)}, u32[]{:S(2)}, u32[]{:S(2)}) collective-permute-start(f32[2,128,128]{2,1,0:T(8,128)S(1)} %get-tuple-element.37), channel_id=1, source_target_pairs={{2,0},{3,4},{6,1},{7,5},{8,10},{9,14},{12,11},{13,15},{18,16},{19,... | collective-permute-start | bytes 393224 | tf_op jit(solution)/shard_map/columns_0/ppermute | solution.py:290
  22.6 0.3 collective-permute-start.5
  22.9 4.6 %collective-permute-start.17 = (f32[2,2,128,128]{3,2,1,0:T(8,128)S(1)}, f32[2,2,128,128]{3,2,1,0:T(8,128)S(1)}, u32[]{:S(2)}, u32[]{:S(2)}) collective-permute-start(f32[2,2,128,128]{3,2,1,0:T(8,128)S(1)} %get-tuple-element.48.refs_0_), channel_id=1, source_target_pairs={{1,4},{4,1},{11,14},{14,11},{17,20},{20,17},{27,30},{30,27}} | collective-permute-start | bytes 786440 | tf_op jit(solution)/shard_map/near_0/ppermute | solution.py:290
  27.5 4.1 %collective-permute-start.12 = (f32[2,128,128]{2,1,0:T(8,128)S(1)}, f32[2,128,128]{2,1,0:T(8,128)S(1)}, u32[]{:S(2)}, u32[]{:S(2)}) collective-permute-start(f32[2,128,128]{2,1,0:T(8,128)S(1)} %get-tuple-element.43), channel_id=1, source_target_pairs={{2,0},{3,4},{6,1},{7,5},{8,10},{9,14},{12,11},{13,15},{18,16},{19,... | collective-permute-start | bytes 393224 | tf_op jit(solution)/shard_map/columns_1/ppermute | solution.py:290
  31.6 1.3 %collective-permute-start.11 = (f32[2,128,128]{2,1,0:T(8,128)S(1)}, f32[2,128,128]{2,1,0:T(8,128)S(1)}, u32[]{:S(2)}, u32[]{:S(2)}) collective-permute-start(f32[2,128,128]{2,1,0:T(8,128)S(1)} %get-tuple-element.42), channel_id=1, source_target_pairs={{2,10},{3,11},{6,14},{7,15},{8,0},{9,1},{12,4},{13,5},{18,26},{19,... | collective-permute-start | bytes 393224 | tf_op jit(solution)/shard_map/rows_2/ppermute | solution.py:290
  33.0 1.9 %collective-permute-start.15 = (f32[2,2,128,128]{3,2,1,0:T(8,128)S(1)}, f32[2,2,128,128]{3,2,1,0:T(8,128)S(1)}, u32[]{:S(2)}, u32[]{:S(2)}) collective-permute-start(f32[2,2,128,128]{3,2,1,0:T(8,128)S(1)} %get-tuple-element.46.refs_0_), channel_id=1, source_target_pairs={{1,4},{4,1},{11,14},{14,11},{17,20},{20,17},{27,30},{30,27}} | collective-permute-start | bytes 786440 | tf_op jit(solution)/shard_map/near_1/ppermute | solution.py:290
  34.9 0.9 %collective-permute-start.8 = (f32[2,128,128]{2,1,0:T(8,128)S(1)}, f32[2,128,128]{2,1,0:T(8,128)S(1)}, u32[]{:S(2)}, u32[]{:S(2)}) collective-permute-start(f32[2,128,128]{2,1,0:T(8,128)S(1)} %get-tuple-element.39), channel_id=1, source_target_pairs={{2,0},{3,4},{6,1},{7,5},{8,10},{9,14},{12,11},{13,15},{18,16},{19,... | collective-permute-start | bytes 393224 | tf_op jit(solution)/shard_map/columns_2/ppermute | solution.py:290
  35.7 3.9 %collective-permute-start.7 = (f32[2,2,128,128]{3,2,1,0:T(8,128)S(1)}, f32[2,2,128,128]{3,2,1,0:T(8,128)S(1)}, u32[]{:S(2)}, u32[]{:S(2)}) collective-permute-start(f32[2,2,128,128]{3,2,1,0:T(8,128)S(1)} %get-tuple-element.38.refs_0_), channel_id=1, source_target_pairs={{1,4},{4,1},{11,14},{14,11},{17,20},{20,17},{27,30},{30,27}} | collective-permute-start | bytes 786440 | tf_op jit(solution)/shard_map/near_2/ppermute | solution.py:290
  39.7 0.1 mix.7
  39.8 0.1 collective-permute-start.14
  39.8 2.3 %collective-permute-start.16 = (f32[2,128,128]{2,1,0:T(8,128)S(1)}, f32[2,128,128]{2,1,0:T(8,128)S(1)}, u32[]{:S(2)}, u32[]{:S(2)}) collective-permute-start(f32[2,128,128]{2,1,0:T(8,128)S(1)} %get-tuple-element.47), channel_id=1, source_target_pairs={{2,10},{3,11},{6,14},{7,15},{8,0},{9,1},{12,4},{13,5},{18,26},{19,... | collective-permute-start | bytes 393224 | tf_op jit(solution)/shard_map/rows_3/ppermute | solution.py:290
  42.2 0.3 collective-permute-done.8.refs_3_
  42.4 3.9 %collective-permute-start.13 = (f32[2,2,128,128]{3,2,1,0:T(8,128)S(1)}, f32[2,2,128,128]{3,2,1,0:T(8,128)S(1)}, u32[]{:S(2)}, u32[]{:S(2)}) collective-permute-start(f32[2,2,128,128]{3,2,1,0:T(8,128)S(1)} %get-tuple-element.44.refs_3_), channel_id=1, source_target_pairs={{1,4},{4,1},{11,14},{14,11},{17,20},{20,17},{27,30},{30,27}} | collective-permute-start | bytes 786440 | tf_op jit(solution)/shard_map/near_3/ppermute | solution.py:290
  46.3 0.9 %skew.4.refs_4_ = f32[1,8,2,128,128]{4,3,2,1,0:T(8,128)} custom-call(f32[2,2,128,128]{3,2,1,0:T(8,128)S(1)} %get-tuple-element.48.refs_0_, f32[2,2,128,128]{3,2,1,0:T(8,128)S(1)} %collective-permute-done.17.refs_1_, f32[2,128,128]{2,1,0:T(8,128)S(1)} %collective-permute-done.11.refs_1_.refs_2_, f32[2,128,128]{2,1,0:T(8,128)S(1)} %collective-permute-done.12.refs_2_.refs_3_), custom_call_target="tpu_custom_call" | custom-call | tf_op jit(solution)/shard_map/skew/pallas_call | solution.py:251
  47.2 1.3 %collective-permute-start.9 = (f32[2,128,128]{2,1,0:T(8,128)S(1)}, f32[2,128,128]{2,1,0:T(8,128)S(1)}, u32[]{:S(2)}, u32[]{:S(2)}) collective-permute-start(f32[2,128,128]{2,1,0:T(8,128)S(1)} %collective-permute-done.8.refs_3_), channel_id=1, source_target_pairs={{0,8},{4,12},{1,9},{5,13},{10,2},{14,6},{11,3},{15,7},{16,24},{20,... | collective-permute-start | bytes 393224 | tf_op jit(solution)/shard_map/rows_4/ppermute | solution.py:290
  48.5 3.0 %collective-permute-start.19 = (f32[2,128,128]{2,1,0:T(8,128)S(1)}, f32[2,128,128]{2,1,0:T(8,128)S(1)}, u32[]{:S(2)}, u32[]{:S(2)}) collective-permute-start(f32[2,128,128]{2,1,0:T(8,128)S(1)} %collective-permute-done.16.refs_2_), channel_id=1, source_target_pairs={{10,8},{11,12},{14,9},{15,13},{0,2},{1,6},{4,3},{5,7},{26,24},{27,... | collective-permute-start | bytes 393224 | tf_op jit(solution)/shard_map/columns_4/ppermute | solution.py:290
  51.6 0.9 %skew.5.refs_6_ = f32[1,8,2,128,128]{4,3,2,1,0:T(8,128)} custom-call(f32[2,2,128,128]{3,2,1,0:T(8,128)S(1)} %get-tuple-element.46.refs_0_, f32[2,2,128,128]{3,2,1,0:T(8,128)S(1)} %collective-permute-done.15.refs_1_, f32[2,128,128]{2,1,0:T(8,128)S(1)} %collective-permute-done.16.refs_2_, ...), custom_call_target="tpu_custom_call", output_to_operand_aliasing={{}: (4, {})} | custom-call | tf_op jit(solution)/shard_map/skew/pallas_call | solution.py:251
  52.4 1.3 %collective-permute-start.18 = (f32[2,128,128]{2,1,0:T(8,128)S(1)}, f32[2,128,128]{2,1,0:T(8,128)S(1)}, u32[]{:S(2)}, u32[]{:S(2)}) collective-permute-start(f32[2,128,128]{2,1,0:T(8,128)S(1)} %collective-permute-done.14.refs_2_), channel_id=1, source_target_pairs={{0,8},{4,12},{1,9},{5,13},{10,2},{14,6},{11,3},{15,7},{16,24},{20,... | collective-permute-start | bytes 393224 | tf_op jit(solution)/shard_map/rows_5/ppermute | solution.py:290
  53.8 0.1 collective-permute-done.19.refs_5_
  53.8 0.8 %skew.6.refs_6_ = f32[1,8,2,128,128]{4,3,2,1,0:T(8,128)} custom-call(f32[2,2,128,128]{3,2,1,0:T(8,128)S(1)} %get-tuple-element.38.refs_0_, f32[2,2,128,128]{3,2,1,0:T(8,128)S(1)} %collective-permute-done.7.refs_1_, f32[2,128,128]{2,1,0:T(8,128)S(1)} %collective-permute-done.14.refs_2_, ...), custom_call_target="tpu_custom_call", output_to_operand_aliasing={{}: (6, {})} | custom-call | tf_op jit(solution)/shard_map/skew/pallas_call | solution.py:251
  54.7 1.3 %collective-permute-done.18.refs_5_ = f32[2,128,128]{2,1,0:T(8,128)S(1)} collective-permute-done((f32[2,128,128]{2,1,0:T(8,128)S(1)}, f32[2,128,128]{2,1,0:T(8,128)S(1)}, u32[]{:S(2)}, u32[]{:S(2)}) %collective-permute-start.18) | collective-permute-done | bytes 131104 | tf_op jit(solution)/shard_map/rows_5/ppermute | solution.py:290
  56.0 0.8 %skew.7 = f32[1,8,2,128,128]{4,3,2,1,0:T(8,128)} custom-call(f32[2,2,128,128]{3,2,1,0:T(8,128)S(1)} %get-tuple-element.38.refs_0_, f32[2,2,128,128]{3,2,1,0:T(8,128)S(1)} %collective-permute-done.7.refs_1_, f32[2,128,128]{2,1,0:T(8,128)S(1)} %collective-permute-done.9.refs_2_, ...), custom_call_target="tpu_custom_call", output_to_operand_aliasing={{}: (6, {})} | custom-call | tf_op jit(solution)/shard_map/skew/pallas_call | solution.py:251
  (19 shorter events, 0.2 us)
Async XLA Ops:
  0.0 5.6 %collective-permute-start = (s32[5,1,1]{0,2,1:T(1,128)}, s32[5,1,1]{0,2,1:T(1,128)S(1)}, u32[]{:S(2)}, u32[]{:S(2)}) collective-permute-start(s32[5,1,1]{0,2,1:T(1,128)} %param.5), channel_id=1, source_target_pairs={{16,0},{0,16},{17,1},{1,17},{18,2},{2,18},{19,3},{3,19},{20,4},{4,... | collective-permute-start | bytes 68 | tf_op jit(solution)/shard_map/ppermute | solution.py:307
  6.9 6.9 %collective-permute-start.3 = (f32[2,2,128,128]{3,2,1,0:T(8,128)S(1)}, f32[2,2,128,128]{3,2,1,0:T(8,128)S(1)}, u32[]{:S(2)}, u32[]{:S(2)}) collective-permute-start(f32[2,2,128,128]{3,2,1,0:T(8,128)S(1)} %correlate.3), channel_id=1, source_target_pairs={{0,16},{16,0},{1,17},{17,1},{2,18},{18,2},{3,19},{19,3},{4,20},{20... | collective-permute-start | bytes 786440 | tf_op jit(solution)/shard_map/momentum_0/ppermute | solution.py:290
  8.8 13.8 %collective-permute-start.2 = (f32[2,2,128,128]{3,2,1,0:T(8,128)S(1)}, f32[2,2,128,128]{3,2,1,0:T(8,128)S(1)}, u32[]{:S(2)}, u32[]{:S(2)}) collective-permute-start(f32[2,2,128,128]{3,2,1,0:T(8,128)S(1)} %get-tuple-element.33), channel_id=1, source_target_pairs={{0,16},{16,0},{1,17},{17,1},{2,18},{18,2},{3,19},{19,3},{4,20},{20... | collective-permute-start | bytes 786440 | tf_op jit(solution)/shard_map/momentum_1/ppermute | solution.py:290
  10.3 17.2 %collective-permute-start.1 = (f32[2,2,128,128]{3,2,1,0:T(8,128)S(1)}, f32[2,2,128,128]{3,2,1,0:T(8,128)S(1)}, u32[]{:S(2)}, u32[]{:S(2)}) collective-permute-start(f32[2,2,128,128]{3,2,1,0:T(8,128)S(1)} %get-tuple-element.31), channel_id=1, source_target_pairs={{0,16},{16,0},{1,17},{17,1},{2,18},{18,2},{3,19},{19,3},{4,20},{20... | collective-permute-start | bytes 786440 | tf_op jit(solution)/shard_map/momentum_2/ppermute | solution.py:290
  13.9 8.7 %collective-permute-start.4 = (f32[2,128,128]{2,1,0:T(8,128)S(1)}, f32[2,128,128]{2,1,0:T(8,128)S(1)}, u32[]{:S(2)}, u32[]{:S(2)}) collective-permute-start(f32[2,128,128]{2,1,0:T(8,128)S(1)} %get-tuple-element.35), channel_id=1, source_target_pairs={{2,10},{3,11},{6,14},{7,15},{8,0},{9,1},{12,4},{13,5},{18,26},{19,... | collective-permute-start | bytes 393224 | tf_op jit(solution)/shard_map/rows_0/ppermute | solution.py:290
  15.2 19.7 %collective-permute-start.10 = (f32[2,2,128,128]{3,2,1,0:T(8,128)S(1)}, f32[2,2,128,128]{3,2,1,0:T(8,128)S(1)}, u32[]{:S(2)}, u32[]{:S(2)}) collective-permute-start(f32[2,2,128,128]{3,2,1,0:T(8,128)S(1)} %get-tuple-element.41), channel_id=1, source_target_pairs={{0,16},{16,0},{1,17},{17,1},{2,18},{18,2},{3,19},{19,3},{4,20},{20... | collective-permute-start | bytes 786440 | tf_op jit(solution)/shard_map/momentum_3/ppermute | solution.py:290
  15.4 16.2 %collective-permute-start.6 = (f32[2,128,128]{2,1,0:T(8,128)S(1)}, f32[2,128,128]{2,1,0:T(8,128)S(1)}, u32[]{:S(2)}, u32[]{:S(2)}) collective-permute-start(f32[2,128,128]{2,1,0:T(8,128)S(1)} %get-tuple-element.37), channel_id=1, source_target_pairs={{2,0},{3,4},{6,1},{7,5},{8,10},{9,14},{12,11},{13,15},{18,16},{19,... | collective-permute-start | bytes 393224 | tf_op jit(solution)/shard_map/columns_0/ppermute | solution.py:290
  22.6 9.0 %collective-permute-start.5 = (f32[2,128,128]{2,1,0:T(8,128)S(1)}, f32[2,128,128]{2,1,0:T(8,128)S(1)}, u32[]{:S(2)}, u32[]{:S(2)}) collective-permute-start(f32[2,128,128]{2,1,0:T(8,128)S(1)} %get-tuple-element.36), channel_id=1, source_target_pairs={{2,10},{3,11},{6,14},{7,15},{8,0},{9,1},{12,4},{13,5},{18,26},{19,... | collective-permute-start | bytes 393224 | tf_op jit(solution)/shard_map/rows_1/ppermute | solution.py:290
  22.9 17.0 %collective-permute-start.17 = (f32[2,2,128,128]{3,2,1,0:T(8,128)S(1)}, f32[2,2,128,128]{3,2,1,0:T(8,128)S(1)}, u32[]{:S(2)}, u32[]{:S(2)}) collective-permute-start(f32[2,2,128,128]{3,2,1,0:T(8,128)S(1)} %get-tuple-element.48.refs_0_), channel_id=1, source_target_pairs={{1,4},{4,1},{11,14},{14,11},{17,20},{20,17},{27,30},{30,27}} | collective-permute-start | bytes 786440 | tf_op jit(solution)/shard_map/near_0/ppermute | solution.py:290
  27.5 8.2 %collective-permute-start.12 = (f32[2,128,128]{2,1,0:T(8,128)S(1)}, f32[2,128,128]{2,1,0:T(8,128)S(1)}, u32[]{:S(2)}, u32[]{:S(2)}) collective-permute-start(f32[2,128,128]{2,1,0:T(8,128)S(1)} %get-tuple-element.43), channel_id=1, source_target_pairs={{2,0},{3,4},{6,1},{7,5},{8,10},{9,14},{12,11},{13,15},{18,16},{19,... | collective-permute-start | bytes 393224 | tf_op jit(solution)/shard_map/columns_1/ppermute | solution.py:290
  31.6 8.0 %collective-permute-start.11 = (f32[2,128,128]{2,1,0:T(8,128)S(1)}, f32[2,128,128]{2,1,0:T(8,128)S(1)}, u32[]{:S(2)}, u32[]{:S(2)}) collective-permute-start(f32[2,128,128]{2,1,0:T(8,128)S(1)} %get-tuple-element.42), channel_id=1, source_target_pairs={{2,10},{3,11},{6,14},{7,15},{8,0},{9,1},{12,4},{13,5},{18,26},{19,... | collective-permute-start | bytes 393224 | tf_op jit(solution)/shard_map/rows_2/ppermute | solution.py:290
  33.0 14.2 %collective-permute-start.15 = (f32[2,2,128,128]{3,2,1,0:T(8,128)S(1)}, f32[2,2,128,128]{3,2,1,0:T(8,128)S(1)}, u32[]{:S(2)}, u32[]{:S(2)}) collective-permute-start(f32[2,2,128,128]{3,2,1,0:T(8,128)S(1)} %get-tuple-element.46.refs_0_), channel_id=1, source_target_pairs={{1,4},{4,1},{11,14},{14,11},{17,20},{20,17},{27,30},{30,27}} | collective-permute-start | bytes 786440 | tf_op jit(solution)/shard_map/near_1/ppermute | solution.py:290
  34.9 7.5 %collective-permute-start.8 = (f32[2,128,128]{2,1,0:T(8,128)S(1)}, f32[2,128,128]{2,1,0:T(8,128)S(1)}, u32[]{:S(2)}, u32[]{:S(2)}) collective-permute-start(f32[2,128,128]{2,1,0:T(8,128)S(1)} %get-tuple-element.39), channel_id=1, source_target_pairs={{2,0},{3,4},{6,1},{7,5},{8,10},{9,14},{12,11},{13,15},{18,16},{19,... | collective-permute-start | bytes 393224 | tf_op jit(solution)/shard_map/columns_2/ppermute | solution.py:290
  35.7 18.0 %collective-permute-start.7 = (f32[2,2,128,128]{3,2,1,0:T(8,128)S(1)}, f32[2,2,128,128]{3,2,1,0:T(8,128)S(1)}, u32[]{:S(2)}, u32[]{:S(2)}) collective-permute-start(f32[2,2,128,128]{3,2,1,0:T(8,128)S(1)} %get-tuple-element.38.refs_0_), channel_id=1, source_target_pairs={{1,4},{4,1},{11,14},{14,11},{17,20},{20,17},{27,30},{30,27}} | collective-permute-start | bytes 786440 | tf_op jit(solution)/shard_map/near_2/ppermute | solution.py:290
  39.8 12.7 %collective-permute-start.14 = (f32[2,128,128]{2,1,0:T(8,128)S(1)}, f32[2,128,128]{2,1,0:T(8,128)S(1)}, u32[]{:S(2)}, u32[]{:S(2)}) collective-permute-start(f32[2,128,128]{2,1,0:T(8,128)S(1)} %get-tuple-element.45), channel_id=1, source_target_pairs={{2,0},{3,4},{6,1},{7,5},{8,10},{9,14},{12,11},{13,15},{18,16},{19,... | collective-permute-start | bytes 393224 | tf_op jit(solution)/shard_map/columns_3/ppermute | solution.py:290
  39.8 8.6 %collective-permute-start.16 = (f32[2,128,128]{2,1,0:T(8,128)S(1)}, f32[2,128,128]{2,1,0:T(8,128)S(1)}, u32[]{:S(2)}, u32[]{:S(2)}) collective-permute-start(f32[2,128,128]{2,1,0:T(8,128)S(1)} %get-tuple-element.47), channel_id=1, source_target_pairs={{2,10},{3,11},{6,14},{7,15},{8,0},{9,1},{12,4},{13,5},{18,26},{19,... | collective-permute-start | bytes 393224 | tf_op jit(solution)/shard_map/rows_3/ppermute | solution.py:290
  42.4 11.4 %collective-permute-start.13 = (f32[2,2,128,128]{3,2,1,0:T(8,128)S(1)}, f32[2,2,128,128]{3,2,1,0:T(8,128)S(1)}, u32[]{:S(2)}, u32[]{:S(2)}) collective-permute-start(f32[2,2,128,128]{3,2,1,0:T(8,128)S(1)} %get-tuple-element.44.refs_3_), channel_id=1, source_target_pairs={{1,4},{4,1},{11,14},{14,11},{17,20},{20,17},{27,30},{30,27}} | collective-permute-start | bytes 786440 | tf_op jit(solution)/shard_map/near_3/ppermute | solution.py:290
  47.2 7.5 %collective-permute-start.9 = (f32[2,128,128]{2,1,0:T(8,128)S(1)}, f32[2,128,128]{2,1,0:T(8,128)S(1)}, u32[]{:S(2)}, u32[]{:S(2)}) collective-permute-start(f32[2,128,128]{2,1,0:T(8,128)S(1)} %collective-permute-done.8.refs_3_), channel_id=1, source_target_pairs={{0,8},{4,12},{1,9},{5,13},{10,2},{14,6},{11,3},{15,7},{16,24},{20,... | collective-permute-start | bytes 393224 | tf_op jit(solution)/shard_map/rows_4/ppermute | solution.py:290
  48.5 5.3 %collective-permute-start.19 = (f32[2,128,128]{2,1,0:T(8,128)S(1)}, f32[2,128,128]{2,1,0:T(8,128)S(1)}, u32[]{:S(2)}, u32[]{:S(2)}) collective-permute-start(f32[2,128,128]{2,1,0:T(8,128)S(1)} %collective-permute-done.16.refs_2_), channel_id=1, source_target_pairs={{10,8},{11,12},{14,9},{15,13},{0,2},{1,6},{4,3},{5,7},{26,24},{27,... | collective-permute-start | bytes 393224 | tf_op jit(solution)/shard_map/columns_4/ppermute | solution.py:290
  52.4 3.5 %collective-permute-start.18 = (f32[2,128,128]{2,1,0:T(8,128)S(1)}, f32[2,128,128]{2,1,0:T(8,128)S(1)}, u32[]{:S(2)}, u32[]{:S(2)}) collective-permute-start(f32[2,128,128]{2,1,0:T(8,128)S(1)} %collective-permute-done.14.refs_2_), channel_id=1, source_target_pairs={{0,8},{4,12},{1,9},{5,13},{10,2},{14,6},{11,3},{15,7},{16,24},{20,... | collective-permute-start | bytes 393224 | tf_op jit(solution)/shard_map/rows_5/ppermute | solution.py:290

commit v3 on v2

--- a/solution.py
+++ b/solution.py
@@ -9,8 +9,11 @@
 
 NE = 8
 TIE = True
-COUNTS = (2, 2, 2, 2)
-NEAR_CUTS = (1, 2, 3)
+BLOCKS = 2
+OWN_TIE = True
+FLOPS = 20_000_000_000
+COUNTS = (2,2,2,2)
+NEAR_CUTS = (1,3)
 HOPS = (0, 1, -1, 2, -2)
 SUBLANES = 8
 AXES = ("ka", "br", "bc")
@@ -58,57 +61,40 @@
     lax.fori_loop(low // SUBLANES, high // SUBLANES, rows_step, 0)
 
 
-def fetch_kernel(stops, first, counts, blocks, table_hbm, green_hbm, screened_hbm, green_ref, screened_ref, *refs):
-    out_refs, (table_ref, table_sem, sem) = refs[:-3], refs[-3:]
-    rows = green_ref.shape[3] // blocks
-    table_copy = pltpu.make_async_copy(table_hbm, table_ref, table_sem)
-    table_copy.start()
+def fetch_kernel(blocks, green_hbm, screened_hbm, green_ref, screened_ref, sem):
     copies = []
-    for block in range(blocks):
-        at = pl.ds(block * rows, rows)
-        pair = [
-            pltpu.make_async_copy(source.at[:, :, :, at], target.at[:, :, :, at], sem.at[block, which])
-            for which, (source, target) in enumerate(((green_hbm, green_ref), (screened_hbm, screened_ref)))
-        ]
-        for copy in pair:
-            copy.start()
-        copies.append(pair)
-    table_copy.wait()
-    for block, pair in enumerate(copies):
-        for copy in pair:
-            copy.wait()
-        correlate_rows(
-            green_ref, screened_ref, table_ref, stops, first, counts, out_refs, block * rows, (block + 1) * rows
-        )
+    for which, (source, target) in enumerate(((screened_hbm, screened_ref), (green_hbm, green_ref))):
+        rows = source.shape[3] // blocks
+        for block in range(blocks):
+            at = pl.ds(block * rows, rows)
+            copies.append(
+                pltpu.make_async_copy(source.at[:, :, :, at], target.at[:, :, :, at], sem.at[which, block])
+            )
+    for copy in copies:
+        copy.start()
+    for copy in copies:
+        copy.wait()
 
 
 def on_hbm(*arrays):
     return [pltpu.with_memory_space_constraint(array, pltpu.HBM) for array in arrays]
 
 
+def fetch(green, screened, blocks):
+    vmem = pl.BlockSpec(memory_space=pltpu.VMEM)
+    return pl.pallas_call(
+        functools.partial(fetch_kernel, blocks),
+        in_specs=[pl.BlockSpec(memory_space=pltpu.HBM)] * 2,
+        out_specs=[vmem] * 2,
+        out_shape=[jax.ShapeDtypeStruct(array.shape, array.dtype) for array in (green, screened)],
+        scratch_shapes=[pltpu.SemaphoreType.DMA((2, blocks))],
+        compiler_params=pltpu.CompilerParams(vmem_limit_bytes=VMEM_LIMIT),
+        name="fetch",
+    )(*on_hbm(green, screened))
+
+
 def run_shapes(green, spans):
     return [jax.ShapeDtypeStruct((count,) + green.shape[2:], jnp.float32) for _, count in spans]
-
-
-def fetch(green, screened, table, stops, spans, blocks):
-    vmem = pl.BlockSpec(memory_space=pltpu.VMEM)
-    whole = pl.BlockSpec(memory_space=pltpu.HBM)
-    counts = [count for _, count in spans]
-    results = pl.pallas_call(
-        functools.partial(fetch_kernel, stops, spans[0][0], counts, blocks),
-        in_specs=[whole] * 3,
-        out_specs=[vmem] * (2 + len(spans)),
-        out_shape=[jax.ShapeDtypeStruct(array.shape, array.dtype) for array in (green, screened)]
-        + run_shapes(green, spans),
-        scratch_shapes=[
-            pltpu.SMEM(table.shape, table.dtype),
-            pltpu.SemaphoreType.DMA,
-            pltpu.SemaphoreType.DMA((blocks, 2)),
-        ],
-        compiler_params=pltpu.CompilerParams(vmem_limit_bytes=VMEM_LIMIT),
-        name="fetch",
-    )(table, green, screened)
-    return results[0], results[1], results[2:]
 
 
 def correlate_kernel(stops, first, counts, table_ref, green_ref, screened_ref, *out_refs):
@@ -173,7 +159,7 @@
         out_specs=[vmem] * 3,
         out_shape=[jax.ShapeDtypeStruct(shape, jnp.float32) for shape in shapes],
         compiler_params=pltpu.CompilerParams(vmem_limit_bytes=VMEM_LIMIT),
-        name="mix",
+        name="mix", cost_estimate=pl.CostEstimate(flops=FLOPS, bytes_accessed=1000000, transcendentals=0),
     )(own, *received, *holds)
 
 
@@ -306,7 +292,8 @@
         if shift:
             table = lax.ppermute(table, "ka", [((k + shift) % momenta, k) for k in range(momenta)])
         tables[shift] = table.reshape(len(HOPS))
-    green, inter, own = fetch(*on_hbm(green_lesser, screened, tables.pop(0)), groups.pop(0), spans, 4)
+    green, inter = fetch(green_lesser, screened, BLOCKS)
+    own_table, own_stops = tables.pop(0), groups.pop(0)
 
     terms = [{} for _ in spans]
     for some in (range(1), range(1, runs)):
@@ -321,6 +308,9 @@
             for shift, term in terms[run].items()
         ]
 
+    if runs > 1 and OWN_TIE:
+        own_table, terms[0] = lax.optimization_barrier((own_table, terms[0]))
+    own = correlate(green, inter, own_table, own_stops, spans)
     arrived = [exchange(run) for run in range(runs)]
     raws, by_columns, by_rows = [], [], []
     for run in range(runs):

time: 57.9 us -> 55.9 us (0.965)
  the two profiles are of different devices: /device:TPU:1 before, /device:TPU:24 now
where the time goes in v3:
time: 55.9 us; the launch traced here: 55.7 us
  waiting for transfers between devices  23.5 us (42%)
  starting transfers between devices  20.1 us (36%)
  Pallas kernels  11.9 us (21%)
    ppermute x18, waiting for transfers between devices, send(): return lax.ppermute(array, axes, pairs)  23.5 us
    ppermute x18, starting transfers between devices, send(): return lax.ppermute(array, axes, pairs)  18.6 us
    pallas_call x3, Pallas kernels, correlate(): pl.pallas_call(functools.partial(correlate_kernel, stops, spans[0][0], co...  5.18 us
    pallas_call x4, Pallas kernels, skew(): pl.pallas_call(functools.partial(skew_kernel, which, [(part[0], part[3],...  3.45 us
    pallas_call x1, Pallas kernels, fetch(): pl.pallas_call(functools.partial(fetch_kernel, blocks), in_specs=[pl.Bloc...  3.08 us
    ppermute x1, starting transfers between devices, on_device(): lax.ppermute(table, 'ka', [((k + shift) % momenta, k) for k in range(mome...  1.49 us
  transfers between devices with their start and end apart: 19, of which 7 were waited for; matrix products, arithmetic and copies ran while one was open for 0% of the time, Pallas kernels for 18%

profile of v3, /device:TPU:24, one launch (start us, length us, event | category | flops | bytes accessed | tf_op | source)
XLA Modules:
  0.0 55.7 jit_solution(3934121969729187286)
XLA Ops:
  0.0 1.5 %collective-permute-start = (s32[5,1,1]{0,2,1:T(1,128)}, s32[5,1,1]{0,2,1:T(1,128)S(1)}, u32[]{:S(2)}, u32[]{:S(2)}) collective-permute-start(s32[5,1,1]{0,2,1:T(1,128)} %param.5), channel_id=1, source_target_pairs={{16,0},{0,16},{17,1},{1,17},{18,2},{2,18},{19,3},{3,19},{20,4},{4,... | collective-permute-start | bytes 68 | tf_op jit(solution)/shard_map/ppermute | solution.py:293
  1.5 3.1 %fetch.1 = (f32[1,15,2,128,128]{4,3,2,1,0:T(8,128)S(1)}, f32[5,8,2,128,128]{4,3,2,1,0:T(8,128)S(1)}) custom-call(f32[1,15,2,128,128]{4,3,2,1,0:T(8,128)} %green_hbm.1, f32[5,8,2,128,128]{4,3,2,1,0:T(8,128)} %screened_hbm.1), custom_call_target="tpu_custom_call" | custom-call | tf_op jit(solution)/shard_map/fetch/pallas_call | solution.py:85
  4.6 1.2 %correlate.3 = f32[2,2,128,128]{3,2,1,0:T(8,128)S(1)} custom-call(s32[5]{0:T(128)S(1)} %bitcast.2, f32[1,15,2,128,128]{4,3,2,1,0:T(8,128)S(1)} %get-tuple-element.30.green_ref, f32[5,8,2,128,128]{4,3,2,1,0:T(8,128)S(1)} %get-tuple-element.31.screened_ref), custom_call_target="tpu_custom_call" | custom-call | tf_op jit(solution)/shard_map/correlate/pallas_call | solution.py:111
  5.8 0.6 %collective-permute-start.3 = (f32[2,2,128,128]{3,2,1,0:T(8,128)S(1)}, f32[2,2,128,128]{3,2,1,0:T(8,128)S(1)}, u32[]{:S(2)}, u32[]{:S(2)}) collective-permute-start(f32[2,2,128,128]{3,2,1,0:T(8,128)S(1)} %correlate.3), channel_id=1, source_target_pairs={{0,16},{16,0},{1,17},{17,1},{2,18},{18,2},{3,19},{19,3},{4,20},{20... | collective-permute-start | bytes 786440 | tf_op jit(solution)/shard_map/momentum_0/ppermute | solution.py:276
  6.5 1.8 %correlate.5 = (f32[2,2,128,128]{3,2,1,0:T(8,128)S(1)}, f32[2,2,128,128]{3,2,1,0:T(8,128)S(1)}, f32[2,2,128,128]{3,2,1,0:T(8,128)S(1)}) custom-call(s32[5]{0:T(128)S(1)} %bitcast.3, f32[1,15,2,128,128]{4,3,2,1,0:T(8,128)S(1)} %get-tuple-element.30.green_ref, f32[5,8,2,128,128]{4,3,2,1,0:T(8,128)S(1)} %get-tuple-element.31.screened_ref), custom_call_target="tpu_custom_call" | custom-call | tf_op jit(solution)/shard_map/correlate/pallas_call | solution.py:111
  8.3 2.2 %correlate.4 = (f32[2,2,128,128]{3,2,1,0:T(8,128)S(1)}, f32[2,2,128,128]{3,2,1,0:T(8,128)S(1)}, f32[2,2,128,128]{3,2,1,0:T(8,128)S(1)}, f32[2,2,128,128]{3,2,1,0:T(8,128)S(1)}) custom-call(s32[5]{0:T(128)S(1)} %bitcast.4, f32[1,15,2,128,128]{4,3,2,1,0:T(8,128)S(1)} %get-tuple-element.30.green_ref, f32[5,8,2,128,128]{4,3,2,1,0:T(8,128)S(1)} %get-tuple-element.31.screened_ref), custom_call_target="tpu_custom_call" | custom-call | tf_op jit(solution)/shard_map/correlate/pallas_call | solution.py:111
  10.5 1.5 %collective-permute-start.2 = (f32[2,2,128,128]{3,2,1,0:T(8,128)S(1)}, f32[2,2,128,128]{3,2,1,0:T(8,128)S(1)}, u32[]{:S(2)}, u32[]{:S(2)}) collective-permute-start(f32[2,2,128,128]{3,2,1,0:T(8,128)S(1)} %get-tuple-element.36), channel_id=1, source_target_pairs={{0,16},{16,0},{1,17},{17,1},{2,18},{18,2},{3,19},{19,3},{4,20},{20... | collective-permute-start | bytes 786440 | tf_op jit(solution)/shard_map/momentum_1/ppermute | solution.py:276
  12.0 3.0 %collective-permute-done.3.refs_0_ = f32[2,2,128,128]{3,2,1,0:T(8,128)S(1)} collective-permute-done((f32[2,2,128,128]{3,2,1,0:T(8,128)S(1)}, f32[2,2,128,128]{3,2,1,0:T(8,128)S(1)}, u32[]{:S(2)}, u32[]{:S(2)}) %collective-permute-start.3) | collective-permute-done | bytes 262176 | tf_op jit(solution)/shard_map/momentum_0/ppermute | solution.py:276
  15.0 1.6 %collective-permute-start.4 = (f32[2,128,128]{2,1,0:T(8,128)S(1)}, f32[2,128,128]{2,1,0:T(8,128)S(1)}, u32[]{:S(2)}, u32[]{:S(2)}) collective-permute-start(f32[2,128,128]{2,1,0:T(8,128)S(1)} %get-tuple-element.39), channel_id=1, source_target_pairs={{2,10},{3,11},{6,14},{7,15},{8,0},{9,1},{12,4},{13,5},{18,26},{19,... | collective-permute-start | bytes 393224 | tf_op jit(solution)/shard_map/rows_0/ppermute | solution.py:276
  16.6 4.0 %collective-permute-done.2.refs_0_ = f32[2,2,128,128]{3,2,1,0:T(8,128)S(1)} collective-permute-done((f32[2,2,128,128]{3,2,1,0:T(8,128)S(1)}, f32[2,2,128,128]{3,2,1,0:T(8,128)S(1)}, u32[]{:S(2)}, u32[]{:S(2)}) %collective-permute-start.2) | collective-permute-done | bytes 262176 | tf_op jit(solution)/shard_map/momentum_1/ppermute | solution.py:276
  20.6 1.6 %collective-permute-start.5 = (f32[2,128,128]{2,1,0:T(8,128)S(1)}, f32[2,128,128]{2,1,0:T(8,128)S(1)}, u32[]{:S(2)}, u32[]{:S(2)}) collective-permute-start(f32[2,128,128]{2,1,0:T(8,128)S(1)} %get-tuple-element.40), channel_id=1, source_target_pairs={{2,10},{3,11},{6,14},{7,15},{8,0},{9,1},{12,4},{13,5},{18,26},{19,... | collective-permute-start | bytes 393224 | tf_op jit(solution)/shard_map/rows_1/ppermute | solution.py:276
  22.2 0.7 %collective-permute-start.10 = (f32[2,2,128,128]{3,2,1,0:T(8,128)S(1)}, f32[2,2,128,128]{3,2,1,0:T(8,128)S(1)}, u32[]{:S(2)}, u32[]{:S(2)}) collective-permute-start(f32[2,2,128,128]{3,2,1,0:T(8,128)S(1)} %get-tuple-element.46), channel_id=1, source_target_pairs={{0,16},{16,0},{1,17},{17,1},{2,18},{18,2},{3,19},{19,3},{4,20},{20... | collective-permute-start | bytes 786440 | tf_op jit(solution)/shard_map/momentum_3/ppermute | solution.py:276
  22.9 3.3 %collective-permute-done.1.refs_0_ = f32[2,2,128,128]{3,2,1,0:T(8,128)S(1)} collective-permute-done((f32[2,2,128,128]{3,2,1,0:T(8,128)S(1)}, f32[2,2,128,128]{3,2,1,0:T(8,128)S(1)}, u32[]{:S(2)}, u32[]{:S(2)}) %collective-permute-start.1) | collective-permute-done | bytes 262176 | tf_op jit(solution)/shard_map/momentum_2/ppermute | solution.py:276
  26.2 1.6 %collective-permute-start.11 = (f32[2,128,128]{2,1,0:T(8,128)S(1)}, f32[2,128,128]{2,1,0:T(8,128)S(1)}, u32[]{:S(2)}, u32[]{:S(2)}) collective-permute-start(f32[2,128,128]{2,1,0:T(8,128)S(1)} %get-tuple-element.47), channel_id=1, source_target_pairs={{2,10},{3,11},{6,14},{7,15},{8,0},{9,1},{12,4},{13,5},{18,26},{19,... | collective-permute-start | bytes 393224 | tf_op jit(solution)/shard_map/rows_2/ppermute | solution.py:276
  27.8 0.7 %collective-permute-start.16 = (f32[2,2,128,128]{3,2,1,0:T(8,128)S(1)}, f32[2,2,128,128]{3,2,1,0:T(8,128)S(1)}, u32[]{:S(2)}, u32[]{:S(2)}) collective-permute-start(f32[2,2,128,128]{3,2,1,0:T(8,128)S(1)} %get-tuple-element.52.refs_0_), channel_id=1, source_target_pairs={{1,4},{4,1},{11,14},{14,11},{17,20},{20,17},{27,30},{30,27}} | collective-permute-start | bytes 786440 | tf_op jit(solution)/shard_map/near_0/ppermute | solution.py:276
  28.5 2.8 %collective-permute-start.8 = (f32[2,128,128]{2,1,0:T(8,128)S(1)}, f32[2,128,128]{2,1,0:T(8,128)S(1)}, u32[]{:S(2)}, u32[]{:S(2)}) collective-permute-start(f32[2,128,128]{2,1,0:T(8,128)S(1)} %get-tuple-element.44), channel_id=1, source_target_pairs={{2,0},{3,4},{6,1},{7,5},{8,10},{9,14},{12,11},{13,15},{18,16},{19,... | collective-permute-start | bytes 393224 | tf_op jit(solution)/shard_map/columns_2/ppermute | solution.py:276
  31.3 0.7 %collective-permute-start.7 = (f32[4,2,128,128]{3,2,1,0:T(8,128)S(1)}, f32[4,2,128,128]{3,2,1,0:T(8,128)S(1)}, u32[]{:S(2)}, u32[]{:S(2)}) collective-permute-start(f32[4,2,128,128]{3,2,1,0:T(8,128)S(1)} %pack.1), channel_id=1, source_target_pairs={{1,4},{4,1},{11,14},{14,11},{17,20},{20,17},{27,30},{30,27}} | collective-permute-start | bytes 1572872 | tf_op jit(solution)/shard_map/near_1/ppermute | solution.py:276
  32.0 0.1 mix.7
  32.1 2.1 %collective-permute-start.15 = (f32[2,128,128]{2,1,0:T(8,128)S(1)}, f32[2,128,128]{2,1,0:T(8,128)S(1)}, u32[]{:S(2)}, u32[]{:S(2)}) collective-permute-start(f32[2,128,128]{2,1,0:T(8,128)S(1)} %get-tuple-element.51), channel_id=1, source_target_pairs={{2,10},{3,11},{6,14},{7,15},{8,0},{9,1},{12,4},{13,5},{18,26},{19,... | collective-permute-start | bytes 393224 | tf_op jit(solution)/shard_map/rows_3/ppermute | solution.py:276
  34.2 0.2 collective-permute-start.14
  34.4 0.7 %collective-permute-start.13 = (f32[2,2,128,128]{3,2,1,0:T(8,128)S(1)}, f32[2,2,128,128]{3,2,1,0:T(8,128)S(1)}, u32[]{:S(2)}, u32[]{:S(2)}) collective-permute-start(f32[2,2,128,128]{3,2,1,0:T(8,128)S(1)} %get-tuple-element.49.refs_3_), channel_id=1, source_target_pairs={{1,4},{4,1},{11,14},{14,11},{17,20},{20,17},{27,30},{30,27}} | collective-permute-start | bytes 786440 | tf_op jit(solution)/shard_map/near_3/ppermute | solution.py:276
  35.1 3.8 %collective-permute-done.8.refs_3_ = f32[2,128,128]{2,1,0:T(8,128)S(1)} collective-permute-done((f32[2,128,128]{2,1,0:T(8,128)S(1)}, f32[2,128,128]{2,1,0:T(8,128)S(1)}, u32[]{:S(2)}, u32[]{:S(2)}) %collective-permute-start.8) | collective-permute-done | bytes 131104 | tf_op jit(solution)/shard_map/columns_2/ppermute | solution.py:276
  38.9 1.3 %collective-permute-start.9 = (f32[2,128,128]{2,1,0:T(8,128)S(1)}, f32[2,128,128]{2,1,0:T(8,128)S(1)}, u32[]{:S(2)}, u32[]{:S(2)}) collective-permute-start(f32[2,128,128]{2,1,0:T(8,128)S(1)} %collective-permute-done.8.refs_3_), channel_id=1, source_target_pairs={{0,8},{4,12},{1,9},{5,13},{10,2},{14,6},{11,3},{15,7},{16,24},{20,... | collective-permute-start | bytes 393224 | tf_op jit(solution)/shard_map/rows_4/ppermute | solution.py:276
  40.2 0.9 %skew.4.refs_4_ = f32[1,8,2,128,128]{4,3,2,1,0:T(8,128)} custom-call(f32[2,2,128,128]{3,2,1,0:T(8,128)S(1)} %get-tuple-element.52.refs_0_, f32[2,2,128,128]{3,2,1,0:T(8,128)S(1)} %collective-permute-done.16.refs_1_, f32[2,128,128]{2,1,0:T(8,128)S(1)} %collective-permute-done.11.refs_1_.refs_2_, f32[2,128,128]{2,1,0:T(8,128)S(1)} %collective-permute-done.12.refs_2_.refs_3_), custom_call_target="tpu_custom_call" | custom-call | tf_op jit(solution)/shard_map/skew/pallas_call | solution.py:237
  41.1 1.3 %collective-permute-start.18 = (f32[2,128,128]{2,1,0:T(8,128)S(1)}, f32[2,128,128]{2,1,0:T(8,128)S(1)}, u32[]{:S(2)}, u32[]{:S(2)}) collective-permute-start(f32[2,128,128]{2,1,0:T(8,128)S(1)} %collective-permute-done.15.refs_2_), channel_id=1, source_target_pairs={{10,8},{11,12},{14,9},{15,13},{0,2},{1,6},{4,3},{5,7},{26,24},{27,... | collective-permute-start | bytes 393224 | tf_op jit(solution)/shard_map/columns_4/ppermute | solution.py:276
  42.4 0.9 %skew.5.refs_6_ = f32[1,8,2,128,128]{4,3,2,1,0:T(8,128)} custom-call(f32[2,2,128,128]{3,2,1,0:T(8,128)S(1)} %get-tuple-element.43.refs_0_, f32[4,2,128,128]{3,2,1,0:T(8,128)S(1)} %collective-permute-done.7.refs_1_, f32[2,128,128]{2,1,0:T(8,128)S(1)} %collective-permute-done.15.refs_2_, ...), custom_call_target="tpu_custom_call", output_to_operand_aliasing={{}: (4, {})} | custom-call | tf_op jit(solution)/shard_map/skew/pallas_call | solution.py:237
  43.3 4.7 %collective-permute-done.14.refs_2_ = f32[2,128,128]{2,1,0:T(8,128)S(1)} collective-permute-done((f32[2,128,128]{2,1,0:T(8,128)S(1)}, f32[2,128,128]{2,1,0:T(8,128)S(1)}, u32[]{:S(2)}, u32[]{:S(2)}) %collective-permute-start.14) | collective-permute-done | bytes 131104 | tf_op jit(solution)/shard_map/columns_3/ppermute | solution.py:276
  48.0 1.3 %collective-permute-start.17 = (f32[2,128,128]{2,1,0:T(8,128)S(1)}, f32[2,128,128]{2,1,0:T(8,128)S(1)}, u32[]{:S(2)}, u32[]{:S(2)}) collective-permute-start(f32[2,128,128]{2,1,0:T(8,128)S(1)} %collective-permute-done.14.refs_2_), channel_id=1, source_target_pairs={{0,8},{4,12},{1,9},{5,13},{10,2},{14,6},{11,3},{15,7},{16,24},{20,... | collective-permute-start | bytes 393224 | tf_op jit(solution)/shard_map/rows_5/ppermute | solution.py:276
  49.3 2.8 %collective-permute-done.18.refs_5_ = f32[2,128,128]{2,1,0:T(8,128)S(1)} collective-permute-done((f32[2,128,128]{2,1,0:T(8,128)S(1)}, f32[2,128,128]{2,1,0:T(8,128)S(1)}, u32[]{:S(2)}, u32[]{:S(2)}) %collective-permute-start.18) | collective-permute-done | bytes 131104 | tf_op jit(solution)/shard_map/columns_4/ppermute | solution.py:276
  52.1 0.9 %skew.6.refs_6_ = f32[1,8,2,128,128]{4,3,2,1,0:T(8,128)} custom-call(f32[2,2,128,128]{3,2,1,0:T(8,128)S(1)} %get-tuple-element.42.refs_1_.refs_0_, f32[4,2,128,128]{3,2,1,0:T(8,128)S(1)} %collective-permute-done.7.refs_1_, f32[2,128,128]{2,1,0:T(8,128)S(1)} %collective-permute-done.14.refs_2_, ...), custom_call_target="tpu_custom_call", output_to_operand_aliasing={{}: (6, {})} | custom-call | tf_op jit(solution)/shard_map/skew/pallas_call | solution.py:237
  53.0 1.8 %collective-permute-done.17.refs_5_ = f32[2,128,128]{2,1,0:T(8,128)S(1)} collective-permute-done((f32[2,128,128]{2,1,0:T(8,128)S(1)}, f32[2,128,128]{2,1,0:T(8,128)S(1)}, u32[]{:S(2)}, u32[]{:S(2)}) %collective-permute-start.17) | collective-permute-done | bytes 131104 | tf_op jit(solution)/shard_map/rows_5/ppermute | solution.py:276
  54.8 0.9 %skew.7 = f32[1,8,2,128,128]{4,3,2,1,0:T(8,128)} custom-call(f32[2,2,128,128]{3,2,1,0:T(8,128)S(1)} %get-tuple-element.42.refs_1_.refs_0_, f32[4,2,128,128]{3,2,1,0:T(8,128)S(1)} %collective-permute-done.7.refs_1_, f32[2,128,128]{2,1,0:T(8,128)S(1)} %collective-permute-done.9.refs_2_, ...), custom_call_target="tpu_custom_call", output_to_operand_aliasing={{}: (6, {})} | custom-call | tf_op jit(solution)/shard_map/skew/pallas_call | solution.py:237
  (21 shorter events, 0.2 us)
Async XLA Ops:
  0.0 4.6 %collective-permute-start = (s32[5,1,1]{0,2,1:T(1,128)}, s32[5,1,1]{0,2,1:T(1,128)S(1)}, u32[]{:S(2)}, u32[]{:S(2)}) collective-permute-start(s32[5,1,1]{0,2,1:T(1,128)} %param.5), channel_id=1, source_target_pairs={{16,0},{0,16},{17,1},{1,17},{18,2},{2,18},{19,3},{3,19},{20,4},{4,... | collective-permute-start | bytes 68 | tf_op jit(solution)/shard_map/ppermute | solution.py:293
  5.8 2.4 %copy-start = (s32[5,1,1]{0,2,1:T(1,128)S(1)}, s32[5,1,1]{0,2,1:T(1,128)}, u32[]{:S(2)}) copy-start(s32[5,1,1]{0,2,1:T(1,128)} %param.5) | copy-start | bytes 64
  5.8 9.1 %collective-permute-start.3 = (f32[2,2,128,128]{3,2,1,0:T(8,128)S(1)}, f32[2,2,128,128]{3,2,1,0:T(8,128)S(1)}, u32[]{:S(2)}, u32[]{:S(2)}) collective-permute-start(f32[2,2,128,128]{3,2,1,0:T(8,128)S(1)} %correlate.3), channel_id=1, source_target_pairs={{0,16},{16,0},{1,17},{17,1},{2,18},{18,2},{3,19},{19,3},{4,20},{20... | collective-permute-start | bytes 786440 | tf_op jit(solution)/shard_map/momentum_0/ppermute | solution.py:276
  10.5 10.1 %collective-permute-start.2 = (f32[2,2,128,128]{3,2,1,0:T(8,128)S(1)}, f32[2,2,128,128]{3,2,1,0:T(8,128)S(1)}, u32[]{:S(2)}, u32[]{:S(2)}) collective-permute-start(f32[2,2,128,128]{3,2,1,0:T(8,128)S(1)} %get-tuple-element.36), channel_id=1, source_target_pairs={{0,16},{16,0},{1,17},{17,1},{2,18},{18,2},{3,19},{19,3},{4,20},{20... | collective-permute-start | bytes 786440 | tf_op jit(solution)/shard_map/momentum_1/ppermute | solution.py:276
  15.0 5.6 %collective-permute-start.4 = (f32[2,128,128]{2,1,0:T(8,128)S(1)}, f32[2,128,128]{2,1,0:T(8,128)S(1)}, u32[]{:S(2)}, u32[]{:S(2)}) collective-permute-start(f32[2,128,128]{2,1,0:T(8,128)S(1)} %get-tuple-element.39), channel_id=1, source_target_pairs={{2,10},{3,11},{6,14},{7,15},{8,0},{9,1},{12,4},{13,5},{18,26},{19,... | collective-permute-start | bytes 393224 | tf_op jit(solution)/shard_map/rows_0/ppermute | solution.py:276
  16.6 9.6 %collective-permute-start.1 = (f32[2,2,128,128]{3,2,1,0:T(8,128)S(1)}, f32[2,2,128,128]{3,2,1,0:T(8,128)S(1)}, u32[]{:S(2)}, u32[]{:S(2)}) collective-permute-start(f32[2,2,128,128]{3,2,1,0:T(8,128)S(1)} %get-tuple-element.34), channel_id=1, source_target_pairs={{0,16},{16,0},{1,17},{17,1},{2,18},{18,2},{3,19},{19,3},{4,20},{20... | collective-permute-start | bytes 786440 | tf_op jit(solution)/shard_map/momentum_2/ppermute | solution.py:276
  16.6 9.6 %collective-permute-start.6 = (f32[2,128,128]{2,1,0:T(8,128)S(1)}, f32[2,128,128]{2,1,0:T(8,128)S(1)}, u32[]{:S(2)}, u32[]{:S(2)}) collective-permute-start(f32[2,128,128]{2,1,0:T(8,128)S(1)} %get-tuple-element.41), channel_id=1, source_target_pairs={{2,0},{3,4},{6,1},{7,5},{8,10},{9,14},{12,11},{13,15},{18,16},{19,... | collective-permute-start | bytes 393224 | tf_op jit(solution)/shard_map/columns_0/ppermute | solution.py:276
  20.6 5.6 %collective-permute-start.5 = (f32[2,128,128]{2,1,0:T(8,128)S(1)}, f32[2,128,128]{2,1,0:T(8,128)S(1)}, u32[]{:S(2)}, u32[]{:S(2)}) collective-permute-start(f32[2,128,128]{2,1,0:T(8,128)S(1)} %get-tuple-element.40), channel_id=1, source_target_pairs={{2,10},{3,11},{6,14},{7,15},{8,0},{9,1},{12,4},{13,5},{18,26},{19,... | collective-permute-start | bytes 393224 | tf_op jit(solution)/shard_map/rows_1/ppermute | solution.py:276
  22.2 9.1 %collective-permute-start.10 = (f32[2,2,128,128]{3,2,1,0:T(8,128)S(1)}, f32[2,2,128,128]{3,2,1,0:T(8,128)S(1)}, u32[]{:S(2)}, u32[]{:S(2)}) collective-permute-start(f32[2,2,128,128]{3,2,1,0:T(8,128)S(1)} %get-tuple-element.46), channel_id=1, source_target_pairs={{0,16},{16,0},{1,17},{17,1},{2,18},{18,2},{3,19},{19,3},{4,20},{20... | collective-permute-start | bytes 786440 | tf_op jit(solution)/shard_map/momentum_3/ppermute | solution.py:276
  22.9 9.1 %collective-permute-start.12 = (f32[2,128,128]{2,1,0:T(8,128)S(1)}, f32[2,128,128]{2,1,0:T(8,128)S(1)}, u32[]{:S(2)}, u32[]{:S(2)}) collective-permute-start(f32[2,128,128]{2,1,0:T(8,128)S(1)} %get-tuple-element.48), channel_id=1, source_target_pairs={{2,0},{3,4},{6,1},{7,5},{8,10},{9,14},{12,11},{13,15},{18,16},{19,... | collective-permute-start | bytes 393224 | tf_op jit(solution)/shard_map/columns_1/ppermute | solution.py:276
  26.2 5.8 %collective-permute-start.11 = (f32[2,128,128]{2,1,0:T(8,128)S(1)}, f32[2,128,128]{2,1,0:T(8,128)S(1)}, u32[]{:S(2)}, u32[]{:S(2)}) collective-permute-start(f32[2,128,128]{2,1,0:T(8,128)S(1)} %get-tuple-element.47), channel_id=1, source_target_pairs={{2,10},{3,11},{6,14},{7,15},{8,0},{9,1},{12,4},{13,5},{18,26},{19,... | collective-permute-start | bytes 393224 | tf_op jit(solution)/shard_map/rows_2/ppermute | solution.py:276
  27.8 6.6 %collective-permute-start.16 = (f32[2,2,128,128]{3,2,1,0:T(8,128)S(1)}, f32[2,2,128,128]{3,2,1,0:T(8,128)S(1)}, u32[]{:S(2)}, u32[]{:S(2)}) collective-permute-start(f32[2,2,128,128]{3,2,1,0:T(8,128)S(1)} %get-tuple-element.52.refs_0_), channel_id=1, source_target_pairs={{1,4},{4,1},{11,14},{14,11},{17,20},{20,17},{27,30},{30,27}} | collective-permute-start | bytes 786440 | tf_op jit(solution)/shard_map/near_0/ppermute | solution.py:276
  28.5 10.4 %collective-permute-start.8 = (f32[2,128,128]{2,1,0:T(8,128)S(1)}, f32[2,128,128]{2,1,0:T(8,128)S(1)}, u32[]{:S(2)}, u32[]{:S(2)}) collective-permute-start(f32[2,128,128]{2,1,0:T(8,128)S(1)} %get-tuple-element.44), channel_id=1, source_target_pairs={{2,0},{3,4},{6,1},{7,5},{8,10},{9,14},{12,11},{13,15},{18,16},{19,... | collective-permute-start | bytes 393224 | tf_op jit(solution)/shard_map/columns_2/ppermute | solution.py:276
  31.3 11.1 %collective-permute-start.7 = (f32[4,2,128,128]{3,2,1,0:T(8,128)S(1)}, f32[4,2,128,128]{3,2,1,0:T(8,128)S(1)}, u32[]{:S(2)}, u32[]{:S(2)}) collective-permute-start(f32[4,2,128,128]{3,2,1,0:T(8,128)S(1)} %pack.1), channel_id=1, source_target_pairs={{1,4},{4,1},{11,14},{14,11},{17,20},{20,17},{27,30},{30,27}} | collective-permute-start | bytes 1572872 | tf_op jit(solution)/shard_map/near_1/ppermute | solution.py:276
  32.1 9.0 %collective-permute-start.15 = (f32[2,128,128]{2,1,0:T(8,128)S(1)}, f32[2,128,128]{2,1,0:T(8,128)S(1)}, u32[]{:S(2)}, u32[]{:S(2)}) collective-permute-start(f32[2,128,128]{2,1,0:T(8,128)S(1)} %get-tuple-element.51), channel_id=1, source_target_pairs={{2,10},{3,11},{6,14},{7,15},{8,0},{9,1},{12,4},{13,5},{18,26},{19,... | collective-permute-start | bytes 393224 | tf_op jit(solution)/shard_map/rows_3/ppermute | solution.py:276
  34.2 13.8 %collective-permute-start.14 = (f32[2,128,128]{2,1,0:T(8,128)S(1)}, f32[2,128,128]{2,1,0:T(8,128)S(1)}, u32[]{:S(2)}, u32[]{:S(2)}) collective-permute-start(f32[2,128,128]{2,1,0:T(8,128)S(1)} %get-tuple-element.50), channel_id=1, source_target_pairs={{2,0},{3,4},{6,1},{7,5},{8,10},{9,14},{12,11},{13,15},{18,16},{19,... | collective-permute-start | bytes 393224 | tf_op jit(solution)/shard_map/columns_3/ppermute | solution.py:276
  34.4 17.7 %collective-permute-start.13 = (f32[2,2,128,128]{3,2,1,0:T(8,128)S(1)}, f32[2,2,128,128]{3,2,1,0:T(8,128)S(1)}, u32[]{:S(2)}, u32[]{:S(2)}) collective-permute-start(f32[2,2,128,128]{3,2,1,0:T(8,128)S(1)} %get-tuple-element.49.refs_3_), channel_id=1, source_target_pairs={{1,4},{4,1},{11,14},{14,11},{17,20},{20,17},{27,30},{30,27}} | collective-permute-start | bytes 786440 | tf_op jit(solution)/shard_map/near_3/ppermute | solution.py:276
  38.9 14.1 %collective-permute-start.9 = (f32[2,128,128]{2,1,0:T(8,128)S(1)}, f32[2,128,128]{2,1,0:T(8,128)S(1)}, u32[]{:S(2)}, u32[]{:S(2)}) collective-permute-start(f32[2,128,128]{2,1,0:T(8,128)S(1)} %collective-permute-done.8.refs_3_), channel_id=1, source_target_pairs={{0,8},{4,12},{1,9},{5,13},{10,2},{14,6},{11,3},{15,7},{16,24},{20,... | collective-permute-start | bytes 393224 | tf_op jit(solution)/shard_map/rows_4/ppermute | solution.py:276
  41.1 11.1 %collective-permute-start.18 = (f32[2,128,128]{2,1,0:T(8,128)S(1)}, f32[2,128,128]{2,1,0:T(8,128)S(1)}, u32[]{:S(2)}, u32[]{:S(2)}) collective-permute-start(f32[2,128,128]{2,1,0:T(8,128)S(1)} %collective-permute-done.15.refs_2_), channel_id=1, source_target_pairs={{10,8},{11,12},{14,9},{15,13},{0,2},{1,6},{4,3},{5,7},{26,24},{27,... | collective-permute-start | bytes 393224 | tf_op jit(solution)/shard_map/columns_4/ppermute | solution.py:276
  48.0 6.8 %collective-permute-start.17 = (f32[2,128,128]{2,1,0:T(8,128)S(1)}, f32[2,128,128]{2,1,0:T(8,128)S(1)}, u32[]{:S(2)}, u32[]{:S(2)}) collective-permute-start(f32[2,128,128]{2,1,0:T(8,128)S(1)} %collective-permute-done.14.refs_2_), channel_id=1, source_target_pairs={{0,8},{4,12},{1,9},{5,13},{10,2},{14,6},{11,3},{15,7},{16,24},{20,... | collective-permute-start | bytes 393224 | tf_op jit(solution)/shard_map/rows_5/ppermute | solution.py:276

commit v4 on v3

--- a/solution.py
+++ b/solution.py
@@ -10,10 +10,13 @@
 NE = 8
 TIE = True
 BLOCKS = 2
+NEAR_LAST = False
+ROWS_LAST = False
+SKEW_TIE = True
 OWN_TIE = True
 FLOPS = 20_000_000_000
 COUNTS = (2,2,2,2)
-NEAR_CUTS = (1,3)
+NEAR_CUTS = (3,)
 HOPS = (0, 1, -1, 2, -2)
 SUBLANES = 8
 AXES = ("ka", "br", "bc")
@@ -325,7 +328,10 @@
         by_rows.append(send(over_second, AXES, sum(over_rows, []), f"rows_{run}"))
     nears, near_places = [], []
     for low, high in groups_near:
-        near = send(pack(raws[low:high]), AXES, near_pairs, f"near_{low}")
+        some = raws[low:high]
+        if NEAR_LAST and high == runs:
+            some, _ = lax.optimization_barrier((some, by_rows[runs - 1]))
+        near = send(pack(some), AXES, near_pairs, f"near_{low}")
         for run in range(low, high):
             nears.append(near)
             near_places.append(spans[run][0] - spans[low][0])
@@ -336,11 +342,17 @@
 
     out = None
     for run in range(runs - 2):
-        out = skew([part(run, [by_rows[run + 2], by_columns[run + 1]], [0, 0])], (0, 1), NE, out)
+        fars = [by_rows[run + 2], by_columns[run + 1]]
+        if SKEW_TIE and run == 0:
+            fars, _ = lax.optimization_barrier((fars, by_rows[runs - 1]))
+        out = skew([part(run, fars, [0, 0])], (0, 1), NE, out)
     last = by_columns[runs - 1]
     if out is not None and TIE:
         last, out = lax.optimization_barrier((last, out))
-    by_rows.append(send(by_columns[runs - 2], AXES, over_rows[1], f"rows_{runs}"))
+    before = by_columns[runs - 2]
+    if ROWS_LAST:
+        before, _ = lax.optimization_barrier((before, by_rows[runs - 1]))
+    by_rows.append(send(before, AXES, over_rows[1], f"rows_{runs}"))
     by_rows.append(send(last, AXES, over_rows[1], f"rows_{runs + 1}"))
     ends = (runs - 2, runs - 1)
     out = skew([part(run, [by_columns[run + 1]], [0]) for run in ends], (1,), NE, out)

time: 55.9 us -> 55.6 us (level)
  the two profiles are of different devices: /device:TPU:24 before, /device:TPU:1 now
where the time goes in v4:
time: 55.6 us; the launch traced here: 55.4 us
  starting transfers between devices  34.2 us (62%)
  Pallas kernels  11.9 us (21%)
  waiting for transfers between devices  8.95 us (16%)
    ppermute x17, starting transfers between devices, send(): return lax.ppermute(array, axes, pairs)  32.2 us
    ppermute x17, waiting for transfers between devices, send(): return lax.ppermute(array, axes, pairs)  8.95 us
    pallas_call x3, Pallas kernels, correlate(): pl.pallas_call(functools.partial(correlate_kernel, stops, spans[0][0], co...  5.18 us
    pallas_call x4, Pallas kernels, skew(): pl.pallas_call(functools.partial(skew_kernel, which, [(part[0], part[3],...  3.45 us
    pallas_call x1, Pallas kernels, fetch(): pl.pallas_call(functools.partial(fetch_kernel, blocks), in_specs=[pl.Bloc...  3.08 us
    ppermute x1, starting transfers between devices, on_device(): lax.ppermute(table, 'ka', [((k + shift) % momenta, k) for k in range(mome...  2.04 us
  transfers between devices with their start and end apart: 18, of which 3 were waited for; matrix products, arithmetic and copies ran while one was open for 0% of the time, Pallas kernels for 18%

profile of v4, /device:TPU:1, one launch (start us, length us, event | category | flops | bytes accessed | tf_op | source)
XLA Modules:
  0.0 55.4 jit_solution(13412069022614157792)
XLA Ops:
  0.0 2.0 %collective-permute-start = (s32[5,1,1]{0,2,1:T(1,128)}, s32[5,1,1]{0,2,1:T(1,128)S(1)}, u32[]{:S(2)}, u32[]{:S(2)}) collective-permute-start(s32[5,1,1]{0,2,1:T(1,128)} %param.5), channel_id=1, source_target_pairs={{16,0},{0,16},{17,1},{1,17},{18,2},{2,18},{19,3},{3,19},{20,4},{4,... | collective-permute-start | bytes 68 | tf_op jit(solution)/shard_map/ppermute | solution.py:296
  2.0 3.1 %fetch.1 = (f32[1,15,2,128,128]{4,3,2,1,0:T(8,128)S(1)}, f32[5,8,2,128,128]{4,3,2,1,0:T(8,128)S(1)}) custom-call(f32[1,15,2,128,128]{4,3,2,1,0:T(8,128)} %green_hbm.1, f32[5,8,2,128,128]{4,3,2,1,0:T(8,128)} %screened_hbm.1), custom_call_target="tpu_custom_call" | custom-call | tf_op jit(solution)/shard_map/fetch/pallas_call | solution.py:88
  5.1 1.2 %correlate.3 = f32[2,2,128,128]{3,2,1,0:T(8,128)S(1)} custom-call(s32[5]{0:T(128)S(1)} %bitcast.2, f32[1,15,2,128,128]{4,3,2,1,0:T(8,128)S(1)} %get-tuple-element.32.green_ref, f32[5,8,2,128,128]{4,3,2,1,0:T(8,128)S(1)} %get-tuple-element.33.screened_ref), custom_call_target="tpu_custom_call" | custom-call | tf_op jit(solution)/shard_map/correlate/pallas_call | solution.py:114
  6.4 0.1 collective-permute-start.3
  6.5 1.8 %correlate.5 = (f32[2,2,128,128]{3,2,1,0:T(8,128)S(1)}, f32[2,2,128,128]{3,2,1,0:T(8,128)S(1)}, f32[2,2,128,128]{3,2,1,0:T(8,128)S(1)}) custom-call(s32[5]{0:T(128)S(1)} %bitcast.3, f32[1,15,2,128,128]{4,3,2,1,0:T(8,128)S(1)} %get-tuple-element.32.green_ref, f32[5,8,2,128,128]{4,3,2,1,0:T(8,128)S(1)} %get-tuple-element.33.screened_ref), custom_call_target="tpu_custom_call" | custom-call | tf_op jit(solution)/shard_map/correlate/pallas_call | solution.py:114
  8.3 2.2 %correlate.4 = (f32[2,2,128,128]{3,2,1,0:T(8,128)S(1)}, f32[2,2,128,128]{3,2,1,0:T(8,128)S(1)}, f32[2,2,128,128]{3,2,1,0:T(8,128)S(1)}, f32[2,2,128,128]{3,2,1,0:T(8,128)S(1)}) custom-call(s32[5]{0:T(128)S(1)} %bitcast.4, f32[1,15,2,128,128]{4,3,2,1,0:T(8,128)S(1)} %get-tuple-element.32.green_ref, f32[5,8,2,128,128]{4,3,2,1,0:T(8,128)S(1)} %get-tuple-element.33.screened_ref), custom_call_target="tpu_custom_call" | custom-call | tf_op jit(solution)/shard_map/correlate/pallas_call | solution.py:114
  10.5 1.5 %collective-permute-start.2 = (f32[2,2,128,128]{3,2,1,0:T(8,128)S(1)}, f32[2,2,128,128]{3,2,1,0:T(8,128)S(1)}, u32[]{:S(2)}, u32[]{:S(2)}) collective-permute-start(f32[2,2,128,128]{3,2,1,0:T(8,128)S(1)} %get-tuple-element.38), channel_id=1, source_target_pairs={{0,16},{16,0},{1,17},{17,1},{2,18},{18,2},{3,19},{19,3},{4,20},{20... | collective-permute-start | bytes 786440 | tf_op jit(solution)/shard_map/momentum_1/ppermute | solution.py:279
  12.0 1.4 %collective-permute-done.3.refs_0_ = f32[2,2,128,128]{3,2,1,0:T(8,128)S(1)} collective-permute-done((f32[2,2,128,128]{3,2,1,0:T(8,128)S(1)}, f32[2,2,128,128]{3,2,1,0:T(8,128)S(1)}, u32[]{:S(2)}, u32[]{:S(2)}) %collective-permute-start.3) | collective-permute-done | bytes 262176 | tf_op jit(solution)/shard_map/momentum_0/ppermute | solution.py:279
  13.4 1.3 %collective-permute-start.4 = (f32[2,128,128]{2,1,0:T(8,128)S(1)}, f32[2,128,128]{2,1,0:T(8,128)S(1)}, u32[]{:S(2)}, u32[]{:S(2)}) collective-permute-start(f32[2,128,128]{2,1,0:T(8,128)S(1)} %get-tuple-element.41), channel_id=1, source_target_pairs={{2,10},{3,11},{6,14},{7,15},{8,0},{9,1},{12,4},{13,5},{18,26},{19,... | collective-permute-start | bytes 393224 | tf_op jit(solution)/shard_map/rows_0/ppermute | solution.py:279
  14.7 0.2 collective-permute-start.1
  14.9 6.4 %collective-permute-start.6 = (f32[2,128,128]{2,1,0:T(8,128)S(1)}, f32[2,128,128]{2,1,0:T(8,128)S(1)}, u32[]{:S(2)}, u32[]{:S(2)}) collective-permute-start(f32[2,128,128]{2,1,0:T(8,128)S(1)} %get-tuple-element.43), channel_id=1, source_target_pairs={{2,0},{3,4},{6,1},{7,5},{8,10},{9,14},{12,11},{13,15},{18,16},{19,... | collective-permute-start | bytes 393224 | tf_op jit(solution)/shard_map/columns_0/ppermute | solution.py:279
  21.3 0.3 collective-permute-start.5
  21.6 1.7 %collective-permute-start.10 = (f32[2,2,128,128]{3,2,1,0:T(8,128)S(1)}, f32[2,2,128,128]{3,2,1,0:T(8,128)S(1)}, u32[]{:S(2)}, u32[]{:S(2)}) collective-permute-start(f32[2,2,128,128]{3,2,1,0:T(8,128)S(1)} %get-tuple-element.49), channel_id=1, source_target_pairs={{0,16},{16,0},{1,17},{17,1},{2,18},{18,2},{3,19},{19,3},{4,20},{20... | collective-permute-start | bytes 786440 | tf_op jit(solution)/shard_map/momentum_3/ppermute | solution.py:279
  23.4 4.2 %collective-permute-start.12 = (f32[2,128,128]{2,1,0:T(8,128)S(1)}, f32[2,128,128]{2,1,0:T(8,128)S(1)}, u32[]{:S(2)}, u32[]{:S(2)}) collective-permute-start(f32[2,128,128]{2,1,0:T(8,128)S(1)} %get-tuple-element.51), channel_id=1, source_target_pairs={{2,0},{3,4},{6,1},{7,5},{8,10},{9,14},{12,11},{13,15},{18,16},{19,... | collective-permute-start | bytes 393224 | tf_op jit(solution)/shard_map/columns_1/ppermute | solution.py:279
  27.6 0.1 mix.6
  27.6 0.3 collective-permute-start.11
  27.9 4.6 %collective-permute-start.8 = (f32[2,128,128]{2,1,0:T(8,128)S(1)}, f32[2,128,128]{2,1,0:T(8,128)S(1)}, u32[]{:S(2)}, u32[]{:S(2)}) collective-permute-start(f32[2,128,128]{2,1,0:T(8,128)S(1)} %get-tuple-element.47), channel_id=1, source_target_pairs={{2,0},{3,4},{6,1},{7,5},{8,10},{9,14},{12,11},{13,15},{18,16},{19,... | collective-permute-start | bytes 393224 | tf_op jit(solution)/shard_map/columns_2/ppermute | solution.py:279
  32.5 0.1 pack.1
  32.6 1.9 %collective-permute-start.7 = (f32[6,2,128,128]{3,2,1,0:T(8,128)S(1)}, f32[6,2,128,128]{3,2,1,0:T(8,128)S(1)}, u32[]{:S(2)}, u32[]{:S(2)}) collective-permute-start(f32[6,2,128,128]{3,2,1,0:T(8,128)S(1)} %pack.1), channel_id=1, source_target_pairs={{1,4},{4,1},{11,14},{14,11},{17,20},{20,17},{27,30},{30,27}} | collective-permute-start | bytes 2359304 | tf_op jit(solution)/shard_map/near_0/ppermute | solution.py:279
  34.5 0.1 mix.7
  34.6 0.1 collective-permute-start.15
  34.7 2.9 %collective-permute-start.14 = (f32[2,128,128]{2,1,0:T(8,128)S(1)}, f32[2,128,128]{2,1,0:T(8,128)S(1)}, u32[]{:S(2)}, u32[]{:S(2)}) collective-permute-start(f32[2,128,128]{2,1,0:T(8,128)S(1)} %get-tuple-element.53), channel_id=1, source_target_pairs={{2,0},{3,4},{6,1},{7,5},{8,10},{9,14},{12,11},{13,15},{18,16},{19,... | collective-permute-start | bytes 393224 | tf_op jit(solution)/shard_map/columns_3/ppermute | solution.py:279
  37.6 1.9 %collective-permute-start.13 = (f32[2,2,128,128]{3,2,1,0:T(8,128)S(1)}, f32[2,2,128,128]{3,2,1,0:T(8,128)S(1)}, u32[]{:S(2)}, u32[]{:S(2)}) collective-permute-start(f32[2,2,128,128]{3,2,1,0:T(8,128)S(1)} %get-tuple-element.52.refs_3_), channel_id=1, source_target_pairs={{1,4},{4,1},{11,14},{14,11},{17,20},{20,17},{27,30},{30,27}} | collective-permute-start | bytes 786440 | tf_op jit(solution)/shard_map/near_3/ppermute | solution.py:279
  39.5 1.3 %collective-permute-start.9 = (f32[2,128,128]{2,1,0:T(8,128)S(1)}, f32[2,128,128]{2,1,0:T(8,128)S(1)}, u32[]{:S(2)}, u32[]{:S(2)}) collective-permute-start(f32[2,128,128]{2,1,0:T(8,128)S(1)} %collective-permute-done.8.refs_3_), channel_id=1, source_target_pairs={{0,8},{4,12},{1,9},{5,13},{10,2},{14,6},{11,3},{15,7},{16,24},{20,... | collective-permute-start | bytes 393224 | tf_op jit(solution)/shard_map/rows_4/ppermute | solution.py:279
  40.9 2.1 %collective-permute-start.17 = (f32[2,128,128]{2,1,0:T(8,128)S(1)}, f32[2,128,128]{2,1,0:T(8,128)S(1)}, u32[]{:S(2)}, u32[]{:S(2)}) collective-permute-start(f32[2,128,128]{2,1,0:T(8,128)S(1)} %collective-permute-done.15.refs_2_), channel_id=1, source_target_pairs={{10,8},{11,12},{14,9},{15,13},{0,2},{1,6},{4,3},{5,7},{26,24},{27,... | collective-permute-start | bytes 393224 | tf_op jit(solution)/shard_map/columns_4/ppermute | solution.py:279
  43.0 6.6 %collective-permute-done.7.refs_1_ = f32[6,2,128,128]{3,2,1,0:T(8,128)S(1)} collective-permute-done((f32[6,2,128,128]{3,2,1,0:T(8,128)S(1)}, f32[6,2,128,128]{3,2,1,0:T(8,128)S(1)}, u32[]{:S(2)}, u32[]{:S(2)}) %collective-permute-start.7) | collective-permute-done | bytes 786464 | tf_op jit(solution)/shard_map/near_0/ppermute | solution.py:279
  49.6 0.8 %skew.4.refs_4_ = f32[1,8,2,128,128]{4,3,2,1,0:T(8,128)} custom-call(f32[2,2,128,128]{3,2,1,0:T(8,128)S(1)} %get-tuple-element.45.refs_0_, f32[6,2,128,128]{3,2,1,0:T(8,128)S(1)} %collective-permute-done.7.refs_1_, f32[2,128,128]{2,1,0:T(8,128)S(1)} %collective-permute-done.11.refs_1_.refs_2_, f32[2,128,128]{2,1,0:T(8,128)S(1)} %collective-permute-done.12.refs_2_.refs_3_), custom_call_target="tpu_custom_call" | custom-call | tf_op jit(solution)/shard_map/skew/pallas_call | solution.py:240
  50.4 0.9 %skew.5.refs_6_ = f32[1,8,2,128,128]{4,3,2,1,0:T(8,128)} custom-call(f32[2,2,128,128]{3,2,1,0:T(8,128)S(1)} %get-tuple-element.46.refs_1_.refs_0_, f32[6,2,128,128]{3,2,1,0:T(8,128)S(1)} %collective-permute-done.7.refs_1_, f32[2,128,128]{2,1,0:T(8,128)S(1)} %collective-permute-done.15.refs_2_, ...), custom_call_target="tpu_custom_call", output_to_operand_aliasing={{}: (4, {})} | custom-call | tf_op jit(solution)/shard_map/skew/pallas_call | solution.py:240
  51.3 1.3 %collective-permute-start.16 = (f32[2,128,128]{2,1,0:T(8,128)S(1)}, f32[2,128,128]{2,1,0:T(8,128)S(1)}, u32[]{:S(2)}, u32[]{:S(2)}) collective-permute-start(f32[2,128,128]{2,1,0:T(8,128)S(1)} %collective-permute-done.14.refs_2_), channel_id=1, source_target_pairs={{0,8},{4,12},{1,9},{5,13},{10,2},{14,6},{11,3},{15,7},{16,24},{20,... | collective-permute-start | bytes 393224 | tf_op jit(solution)/shard_map/rows_5/ppermute | solution.py:279
  52.6 0.9 %skew.6.refs_6_ = f32[1,8,2,128,128]{4,3,2,1,0:T(8,128)} custom-call(f32[2,2,128,128]{3,2,1,0:T(8,128)S(1)} %get-tuple-element.44.refs_2_.refs_0_, f32[6,2,128,128]{3,2,1,0:T(8,128)S(1)} %collective-permute-done.7.refs_1_, f32[2,128,128]{2,1,0:T(8,128)S(1)} %collective-permute-done.14.refs_2_, ...), custom_call_target="tpu_custom_call", output_to_operand_aliasing={{}: (6, {})} | custom-call | tf_op jit(solution)/shard_map/skew/pallas_call | solution.py:240
  53.5 1.0 %collective-permute-done.16.refs_5_ = f32[2,128,128]{2,1,0:T(8,128)S(1)} collective-permute-done((f32[2,128,128]{2,1,0:T(8,128)S(1)}, f32[2,128,128]{2,1,0:T(8,128)S(1)}, u32[]{:S(2)}, u32[]{:S(2)}) %collective-permute-start.16) | collective-permute-done | bytes 131104 | tf_op jit(solution)/shard_map/rows_5/ppermute | solution.py:279
  54.5 0.8 %skew.7 = f32[1,8,2,128,128]{4,3,2,1,0:T(8,128)} custom-call(f32[2,2,128,128]{3,2,1,0:T(8,128)S(1)} %get-tuple-element.44.refs_2_.refs_0_, f32[6,2,128,128]{3,2,1,0:T(8,128)S(1)} %collective-permute-done.7.refs_1_, f32[2,128,128]{2,1,0:T(8,128)S(1)} %collective-permute-done.9.refs_2_, ...), custom_call_target="tpu_custom_call", output_to_operand_aliasing={{}: (6, {})} | custom-call | tf_op jit(solution)/shard_map/skew/pallas_call | solution.py:240
  (19 shorter events, 0.1 us)
Async XLA Ops:
  0.0 5.1 %collective-permute-start = (s32[5,1,1]{0,2,1:T(1,128)}, s32[5,1,1]{0,2,1:T(1,128)S(1)}, u32[]{:S(2)}, u32[]{:S(2)}) collective-permute-start(s32[5,1,1]{0,2,1:T(1,128)} %param.5), channel_id=1, source_target_pairs={{16,0},{0,16},{17,1},{1,17},{18,2},{2,18},{19,3},{3,19},{20,4},{4,... | collective-permute-start | bytes 68 | tf_op jit(solution)/shard_map/ppermute | solution.py:296
  6.4 1.9 %copy-start = (s32[5,1,1]{0,2,1:T(1,128)S(1)}, s32[5,1,1]{0,2,1:T(1,128)}, u32[]{:S(2)}) copy-start(s32[5,1,1]{0,2,1:T(1,128)} %param.5) | copy-start | bytes 64
  6.4 6.9 %collective-permute-start.3 = (f32[2,2,128,128]{3,2,1,0:T(8,128)S(1)}, f32[2,2,128,128]{3,2,1,0:T(8,128)S(1)}, u32[]{:S(2)}, u32[]{:S(2)}) collective-permute-start(f32[2,2,128,128]{3,2,1,0:T(8,128)S(1)} %correlate.3), channel_id=1, source_target_pairs={{0,16},{16,0},{1,17},{17,1},{2,18},{18,2},{3,19},{19,3},{4,20},{20... | collective-permute-start | bytes 786440 | tf_op jit(solution)/shard_map/momentum_0/ppermute | solution.py:279
  10.5 10.8 %collective-permute-start.2 = (f32[2,2,128,128]{3,2,1,0:T(8,128)S(1)}, f32[2,2,128,128]{3,2,1,0:T(8,128)S(1)}, u32[]{:S(2)}, u32[]{:S(2)}) collective-permute-start(f32[2,2,128,128]{3,2,1,0:T(8,128)S(1)} %get-tuple-element.38), channel_id=1, source_target_pairs={{0,16},{16,0},{1,17},{17,1},{2,18},{18,2},{3,19},{19,3},{4,20},{20... | collective-permute-start | bytes 786440 | tf_op jit(solution)/shard_map/momentum_1/ppermute | solution.py:279
  13.4 7.9 %collective-permute-start.4 = (f32[2,128,128]{2,1,0:T(8,128)S(1)}, f32[2,128,128]{2,1,0:T(8,128)S(1)}, u32[]{:S(2)}, u32[]{:S(2)}) collective-permute-start(f32[2,128,128]{2,1,0:T(8,128)S(1)} %get-tuple-element.41), channel_id=1, source_target_pairs={{2,10},{3,11},{6,14},{7,15},{8,0},{9,1},{12,4},{13,5},{18,26},{19,... | collective-permute-start | bytes 393224 | tf_op jit(solution)/shard_map/rows_0/ppermute | solution.py:279
  14.7 12.9 %collective-permute-start.1 = (f32[2,2,128,128]{3,2,1,0:T(8,128)S(1)}, f32[2,2,128,128]{3,2,1,0:T(8,128)S(1)}, u32[]{:S(2)}, u32[]{:S(2)}) collective-permute-start(f32[2,2,128,128]{3,2,1,0:T(8,128)S(1)} %get-tuple-element.36), channel_id=1, source_target_pairs={{0,16},{16,0},{1,17},{17,1},{2,18},{18,2},{3,19},{19,3},{4,20},{20... | collective-permute-start | bytes 786440 | tf_op jit(solution)/shard_map/momentum_2/ppermute | solution.py:279
  14.9 12.7 %collective-permute-start.6 = (f32[2,128,128]{2,1,0:T(8,128)S(1)}, f32[2,128,128]{2,1,0:T(8,128)S(1)}, u32[]{:S(2)}, u32[]{:S(2)}) collective-permute-start(f32[2,128,128]{2,1,0:T(8,128)S(1)} %get-tuple-element.43), channel_id=1, source_target_pairs={{2,0},{3,4},{6,1},{7,5},{8,10},{9,14},{12,11},{13,15},{18,16},{19,... | collective-permute-start | bytes 393224 | tf_op jit(solution)/shard_map/columns_0/ppermute | solution.py:279
  21.3 6.2 %collective-permute-start.5 = (f32[2,128,128]{2,1,0:T(8,128)S(1)}, f32[2,128,128]{2,1,0:T(8,128)S(1)}, u32[]{:S(2)}, u32[]{:S(2)}) collective-permute-start(f32[2,128,128]{2,1,0:T(8,128)S(1)} %get-tuple-element.42), channel_id=1, source_target_pairs={{2,10},{3,11},{6,14},{7,15},{8,0},{9,1},{12,4},{13,5},{18,26},{19,... | collective-permute-start | bytes 393224 | tf_op jit(solution)/shard_map/rows_1/ppermute | solution.py:279
  21.6 12.9 %collective-permute-start.10 = (f32[2,2,128,128]{3,2,1,0:T(8,128)S(1)}, f32[2,2,128,128]{3,2,1,0:T(8,128)S(1)}, u32[]{:S(2)}, u32[]{:S(2)}) collective-permute-start(f32[2,2,128,128]{3,2,1,0:T(8,128)S(1)} %get-tuple-element.49), channel_id=1, source_target_pairs={{0,16},{16,0},{1,17},{17,1},{2,18},{18,2},{3,19},{19,3},{4,20},{20... | collective-permute-start | bytes 786440 | tf_op jit(solution)/shard_map/momentum_3/ppermute | solution.py:279
  23.4 11.2 %collective-permute-start.12 = (f32[2,128,128]{2,1,0:T(8,128)S(1)}, f32[2,128,128]{2,1,0:T(8,128)S(1)}, u32[]{:S(2)}, u32[]{:S(2)}) collective-permute-start(f32[2,128,128]{2,1,0:T(8,128)S(1)} %get-tuple-element.51), channel_id=1, source_target_pairs={{2,0},{3,4},{6,1},{7,5},{8,10},{9,14},{12,11},{13,15},{18,16},{19,... | collective-permute-start | bytes 393224 | tf_op jit(solution)/shard_map/columns_1/ppermute | solution.py:279
  27.6 6.9 %collective-permute-start.11 = (f32[2,128,128]{2,1,0:T(8,128)S(1)}, f32[2,128,128]{2,1,0:T(8,128)S(1)}, u32[]{:S(2)}, u32[]{:S(2)}) collective-permute-start(f32[2,128,128]{2,1,0:T(8,128)S(1)} %get-tuple-element.50), channel_id=1, source_target_pairs={{2,10},{3,11},{6,14},{7,15},{8,0},{9,1},{12,4},{13,5},{18,26},{19,... | collective-permute-start | bytes 393224 | tf_op jit(solution)/shard_map/rows_2/ppermute | solution.py:279
  27.9 11.6 %collective-permute-start.8 = (f32[2,128,128]{2,1,0:T(8,128)S(1)}, f32[2,128,128]{2,1,0:T(8,128)S(1)}, u32[]{:S(2)}, u32[]{:S(2)}) collective-permute-start(f32[2,128,128]{2,1,0:T(8,128)S(1)} %get-tuple-element.47), channel_id=1, source_target_pairs={{2,0},{3,4},{6,1},{7,5},{8,10},{9,14},{12,11},{13,15},{18,16},{19,... | collective-permute-start | bytes 393224 | tf_op jit(solution)/shard_map/columns_2/ppermute | solution.py:279
  32.6 17.0 %collective-permute-start.7 = (f32[6,2,128,128]{3,2,1,0:T(8,128)S(1)}, f32[6,2,128,128]{3,2,1,0:T(8,128)S(1)}, u32[]{:S(2)}, u32[]{:S(2)}) collective-permute-start(f32[6,2,128,128]{3,2,1,0:T(8,128)S(1)} %pack.1), channel_id=1, source_target_pairs={{1,4},{4,1},{11,14},{14,11},{17,20},{20,17},{27,30},{30,27}} | collective-permute-start | bytes 2359304 | tf_op jit(solution)/shard_map/near_0/ppermute | solution.py:279
  34.6 6.2 %collective-permute-start.15 = (f32[2,128,128]{2,1,0:T(8,128)S(1)}, f32[2,128,128]{2,1,0:T(8,128)S(1)}, u32[]{:S(2)}, u32[]{:S(2)}) collective-permute-start(f32[2,128,128]{2,1,0:T(8,128)S(1)} %get-tuple-element.54), channel_id=1, source_target_pairs={{2,10},{3,11},{6,14},{7,15},{8,0},{9,1},{12,4},{13,5},{18,26},{19,... | collective-permute-start | bytes 393224 | tf_op jit(solution)/shard_map/rows_3/ppermute | solution.py:279
  34.7 16.6 %collective-permute-start.14 = (f32[2,128,128]{2,1,0:T(8,128)S(1)}, f32[2,128,128]{2,1,0:T(8,128)S(1)}, u32[]{:S(2)}, u32[]{:S(2)}) collective-permute-start(f32[2,128,128]{2,1,0:T(8,128)S(1)} %get-tuple-element.53), channel_id=1, source_target_pairs={{2,0},{3,4},{6,1},{7,5},{8,10},{9,14},{12,11},{13,15},{18,16},{19,... | collective-permute-start | bytes 393224 | tf_op jit(solution)/shard_map/columns_3/ppermute | solution.py:279
  37.6 15.0 %collective-permute-start.13 = (f32[2,2,128,128]{3,2,1,0:T(8,128)S(1)}, f32[2,2,128,128]{3,2,1,0:T(8,128)S(1)}, u32[]{:S(2)}, u32[]{:S(2)}) collective-permute-start(f32[2,2,128,128]{3,2,1,0:T(8,128)S(1)} %get-tuple-element.52.refs_3_), channel_id=1, source_target_pairs={{1,4},{4,1},{11,14},{14,11},{17,20},{20,17},{27,30},{30,27}} | collective-permute-start | bytes 786440 | tf_op jit(solution)/shard_map/near_3/ppermute | solution.py:279
  39.5 14.0 %collective-permute-start.9 = (f32[2,128,128]{2,1,0:T(8,128)S(1)}, f32[2,128,128]{2,1,0:T(8,128)S(1)}, u32[]{:S(2)}, u32[]{:S(2)}) collective-permute-start(f32[2,128,128]{2,1,0:T(8,128)S(1)} %collective-permute-done.8.refs_3_), channel_id=1, source_target_pairs={{0,8},{4,12},{1,9},{5,13},{10,2},{14,6},{11,3},{15,7},{16,24},{20,... | collective-permute-start | bytes 393224 | tf_op jit(solution)/shard_map/rows_4/ppermute | solution.py:279
  40.9 11.8 %collective-permute-start.17 = (f32[2,128,128]{2,1,0:T(8,128)S(1)}, f32[2,128,128]{2,1,0:T(8,128)S(1)}, u32[]{:S(2)}, u32[]{:S(2)}) collective-permute-start(f32[2,128,128]{2,1,0:T(8,128)S(1)} %collective-permute-done.15.refs_2_), channel_id=1, source_target_pairs={{10,8},{11,12},{14,9},{15,13},{0,2},{1,6},{4,3},{5,7},{26,24},{27,... | collective-permute-start | bytes 393224 | tf_op jit(solution)/shard_map/columns_4/ppermute | solution.py:279
  51.3 3.2 %collective-permute-start.16 = (f32[2,128,128]{2,1,0:T(8,128)S(1)}, f32[2,128,128]{2,1,0:T(8,128)S(1)}, u32[]{:S(2)}, u32[]{:S(2)}) collective-permute-start(f32[2,128,128]{2,1,0:T(8,128)S(1)} %collective-permute-done.14.refs_2_), channel_id=1, source_target_pairs={{0,8},{4,12},{1,9},{5,13},{10,2},{14,6},{11,3},{15,7},{16,24},{20,... | collective-permute-start | bytes 393224 | tf_op jit(solution)/shard_map/rows_5/ppermute | solution.py:279

commit v5 on v3

--- a/solution.py
+++ b/solution.py
@@ -340,8 +340,8 @@
     last = by_columns[runs - 1]
     if out is not None and TIE:
         last, out = lax.optimization_barrier((last, out))
-    by_rows.append(send(by_columns[runs - 2], AXES, over_rows[1], f"rows_{runs}"))
-    by_rows.append(send(last, AXES, over_rows[1], f"rows_{runs + 1}"))
+    by_rows.append(send(by_columns[runs - 2], AXES, sum(over_rows, []), f"rows_{runs}"))
+    by_rows.append(send(last, AXES, sum(over_rows, []), f"rows_{runs + 1}"))
     ends = (runs - 2, runs - 1)
     out = skew([part(run, [by_columns[run + 1]], [0]) for run in ends], (1,), NE, out)
     return skew([part(run, [by_rows[run + 2]], [0]) for run in ends], (0,), NE, out)

time: 55.9 us -> 54.5 us (0.975)
  the two profiles are of different devices: /device:TPU:24 before, /device:TPU:1 now
where the time goes in v5:
time: 54.5 us; the launch traced here: 54.3 us
  starting transfers between devices  37.8 us (69%)
  Pallas kernels  11.9 us (22%)
  waiting for transfers between devices  4.33 us (8%)
    ppermute x18, starting transfers between devices, send(): return lax.ppermute(array, axes, pairs)  35.8 us
    pallas_call x3, Pallas kernels, correlate(): pl.pallas_call(functools.partial(correlate_kernel, stops, spans[0][0], co...  5.18 us
    ppermute x18, waiting for transfers between devices, send(): return lax.ppermute(array, axes, pairs)  4.33 us
    pallas_call x4, Pallas kernels, skew(): pl.pallas_call(functools.partial(skew_kernel, which, [(part[0], part[3],...  3.42 us
    pallas_call x1, Pallas kernels, fetch(): pl.pallas_call(functools.partial(fetch_kernel, blocks), in_specs=[pl.Bloc...  3.08 us
    ppermute x1, starting transfers between devices, on_device(): lax.ppermute(table, 'ka', [((k + shift) % momenta, k) for k in range(mome...  2.04 us
  transfers between devices with their start and end apart: 19, of which 3 were waited for; matrix products, arithmetic and copies ran while one was open for 0% of the time, Pallas kernels for 18%

profile of v5, /device:TPU:1, one launch (start us, length us, event | category | flops | bytes accessed | tf_op | source)
XLA Modules:
  0.0 54.3 jit_solution(4750598696729703180)
XLA Ops:
  0.0 2.0 %collective-permute-start = (s32[5,1,1]{0,2,1:T(1,128)}, s32[5,1,1]{0,2,1:T(1,128)S(1)}, u32[]{:S(2)}, u32[]{:S(2)}) collective-permute-start(s32[5,1,1]{0,2,1:T(1,128)} %param.5), channel_id=1, source_target_pairs={{16,0},{0,16},{17,1},{1,17},{18,2},{2,18},{19,3},{3,19},{20,4},{4,... | collective-permute-start | bytes 68 | tf_op jit(solution)/shard_map/ppermute | solution.py:293
  2.0 3.1 %fetch.1 = (f32[1,15,2,128,128]{4,3,2,1,0:T(8,128)S(1)}, f32[5,8,2,128,128]{4,3,2,1,0:T(8,128)S(1)}) custom-call(f32[1,15,2,128,128]{4,3,2,1,0:T(8,128)} %green_hbm.1, f32[5,8,2,128,128]{4,3,2,1,0:T(8,128)} %screened_hbm.1), custom_call_target="tpu_custom_call" | custom-call | tf_op jit(solution)/shard_map/fetch/pallas_call | solution.py:85
  5.1 1.2 %correlate.3 = f32[2,2,128,128]{3,2,1,0:T(8,128)S(1)} custom-call(s32[5]{0:T(128)S(1)} %bitcast.2, f32[1,15,2,128,128]{4,3,2,1,0:T(8,128)S(1)} %get-tuple-element.30.green_ref, f32[5,8,2,128,128]{4,3,2,1,0:T(8,128)S(1)} %get-tuple-element.31.screened_ref), custom_call_target="tpu_custom_call" | custom-call | tf_op jit(solution)/shard_map/correlate/pallas_call | solution.py:111
  6.4 0.1 collective-permute-start.3
  6.5 1.8 %correlate.5 = (f32[2,2,128,128]{3,2,1,0:T(8,128)S(1)}, f32[2,2,128,128]{3,2,1,0:T(8,128)S(1)}, f32[2,2,128,128]{3,2,1,0:T(8,128)S(1)}) custom-call(s32[5]{0:T(128)S(1)} %bitcast.3, f32[1,15,2,128,128]{4,3,2,1,0:T(8,128)S(1)} %get-tuple-element.30.green_ref, f32[5,8,2,128,128]{4,3,2,1,0:T(8,128)S(1)} %get-tuple-element.31.screened_ref), custom_call_target="tpu_custom_call" | custom-call | tf_op jit(solution)/shard_map/correlate/pallas_call | solution.py:111
  8.3 2.2 %correlate.4 = (f32[2,2,128,128]{3,2,1,0:T(8,128)S(1)}, f32[2,2,128,128]{3,2,1,0:T(8,128)S(1)}, f32[2,2,128,128]{3,2,1,0:T(8,128)S(1)}, f32[2,2,128,128]{3,2,1,0:T(8,128)S(1)}) custom-call(s32[5]{0:T(128)S(1)} %bitcast.4, f32[1,15,2,128,128]{4,3,2,1,0:T(8,128)S(1)} %get-tuple-element.30.green_ref, f32[5,8,2,128,128]{4,3,2,1,0:T(8,128)S(1)} %get-tuple-element.31.screened_ref), custom_call_target="tpu_custom_call" | custom-call | tf_op jit(solution)/shard_map/correlate/pallas_call | solution.py:111
  10.5 1.5 %collective-permute-start.2 = (f32[2,2,128,128]{3,2,1,0:T(8,128)S(1)}, f32[2,2,128,128]{3,2,1,0:T(8,128)S(1)}, u32[]{:S(2)}, u32[]{:S(2)}) collective-permute-start(f32[2,2,128,128]{3,2,1,0:T(8,128)S(1)} %get-tuple-element.36), channel_id=1, source_target_pairs={{0,16},{16,0},{1,17},{17,1},{2,18},{18,2},{3,19},{19,3},{4,20},{20... | collective-permute-start | bytes 786440 | tf_op jit(solution)/shard_map/momentum_1/ppermute | solution.py:276
  12.0 1.4 %collective-permute-done.3.refs_0_ = f32[2,2,128,128]{3,2,1,0:T(8,128)S(1)} collective-permute-done((f32[2,2,128,128]{3,2,1,0:T(8,128)S(1)}, f32[2,2,128,128]{3,2,1,0:T(8,128)S(1)}, u32[]{:S(2)}, u32[]{:S(2)}) %collective-permute-start.3) | collective-permute-done | bytes 262176 | tf_op jit(solution)/shard_map/momentum_0/ppermute | solution.py:276
  13.4 1.3 %collective-permute-start.4 = (f32[2,128,128]{2,1,0:T(8,128)S(1)}, f32[2,128,128]{2,1,0:T(8,128)S(1)}, u32[]{:S(2)}, u32[]{:S(2)}) collective-permute-start(f32[2,128,128]{2,1,0:T(8,128)S(1)} %get-tuple-element.39), channel_id=1, source_target_pairs={{2,10},{3,11},{6,14},{7,15},{8,0},{9,1},{12,4},{13,5},{18,26},{19,... | collective-permute-start | bytes 393224 | tf_op jit(solution)/shard_map/rows_0/ppermute | solution.py:276
  14.7 0.2 collective-permute-start.1
  14.9 6.4 %collective-permute-start.6 = (f32[2,128,128]{2,1,0:T(8,128)S(1)}, f32[2,128,128]{2,1,0:T(8,128)S(1)}, u32[]{:S(2)}, u32[]{:S(2)}) collective-permute-start(f32[2,128,128]{2,1,0:T(8,128)S(1)} %get-tuple-element.41), channel_id=1, source_target_pairs={{2,0},{3,4},{6,1},{7,5},{8,10},{9,14},{12,11},{13,15},{18,16},{19,... | collective-permute-start | bytes 393224 | tf_op jit(solution)/shard_map/columns_0/ppermute | solution.py:276
  21.3 0.3 collective-permute-start.5
  21.6 1.7 %collective-permute-start.10 = (f32[2,2,128,128]{3,2,1,0:T(8,128)S(1)}, f32[2,2,128,128]{3,2,1,0:T(8,128)S(1)}, u32[]{:S(2)}, u32[]{:S(2)}) collective-permute-start(f32[2,2,128,128]{3,2,1,0:T(8,128)S(1)} %get-tuple-element.46), channel_id=1, source_target_pairs={{0,16},{16,0},{1,17},{17,1},{2,18},{18,2},{3,19},{19,3},{4,20},{20... | collective-permute-start | bytes 786440 | tf_op jit(solution)/shard_map/momentum_3/ppermute | solution.py:276
  23.4 4.2 %collective-permute-start.12 = (f32[2,128,128]{2,1,0:T(8,128)S(1)}, f32[2,128,128]{2,1,0:T(8,128)S(1)}, u32[]{:S(2)}, u32[]{:S(2)}) collective-permute-start(f32[2,128,128]{2,1,0:T(8,128)S(1)} %get-tuple-element.48), channel_id=1, source_target_pairs={{2,0},{3,4},{6,1},{7,5},{8,10},{9,14},{12,11},{13,15},{18,16},{19,... | collective-permute-start | bytes 393224 | tf_op jit(solution)/shard_map/columns_1/ppermute | solution.py:276
  27.6 0.1 mix.6
  27.6 0.3 collective-permute-start.11
  27.9 4.5 %collective-permute-start.16 = (f32[2,2,128,128]{3,2,1,0:T(8,128)S(1)}, f32[2,2,128,128]{3,2,1,0:T(8,128)S(1)}, u32[]{:S(2)}, u32[]{:S(2)}) collective-permute-start(f32[2,2,128,128]{3,2,1,0:T(8,128)S(1)} %get-tuple-element.52.refs_0_), channel_id=1, source_target_pairs={{1,4},{4,1},{11,14},{14,11},{17,20},{20,17},{27,30},{30,27}} | collective-permute-start | bytes 786440 | tf_op jit(solution)/shard_map/near_0/ppermute | solution.py:276
  32.4 0.9 %collective-permute-start.8 = (f32[2,128,128]{2,1,0:T(8,128)S(1)}, f32[2,128,128]{2,1,0:T(8,128)S(1)}, u32[]{:S(2)}, u32[]{:S(2)}) collective-permute-start(f32[2,128,128]{2,1,0:T(8,128)S(1)} %get-tuple-element.44), channel_id=1, source_target_pairs={{2,0},{3,4},{6,1},{7,5},{8,10},{9,14},{12,11},{13,15},{18,16},{19,... | collective-permute-start | bytes 393224 | tf_op jit(solution)/shard_map/columns_2/ppermute | solution.py:276
  33.3 1.9 %collective-permute-start.7 = (f32[4,2,128,128]{3,2,1,0:T(8,128)S(1)}, f32[4,2,128,128]{3,2,1,0:T(8,128)S(1)}, u32[]{:S(2)}, u32[]{:S(2)}) collective-permute-start(f32[4,2,128,128]{3,2,1,0:T(8,128)S(1)} %pack.1), channel_id=1, source_target_pairs={{1,4},{4,1},{11,14},{14,11},{17,20},{20,17},{27,30},{30,27}} | collective-permute-start | bytes 1572872 | tf_op jit(solution)/shard_map/near_1/ppermute | solution.py:276
  35.3 0.1 mix.7
  35.3 0.3 collective-permute-start.15
  35.6 3.3 %collective-permute-start.14 = (f32[2,128,128]{2,1,0:T(8,128)S(1)}, f32[2,128,128]{2,1,0:T(8,128)S(1)}, u32[]{:S(2)}, u32[]{:S(2)}) collective-permute-start(f32[2,128,128]{2,1,0:T(8,128)S(1)} %get-tuple-element.50), channel_id=1, source_target_pairs={{2,0},{3,4},{6,1},{7,5},{8,10},{9,14},{12,11},{13,15},{18,16},{19,... | collective-permute-start | bytes 393224 | tf_op jit(solution)/shard_map/columns_3/ppermute | solution.py:276
  38.9 2.6 %collective-permute-start.13 = (f32[2,2,128,128]{3,2,1,0:T(8,128)S(1)}, f32[2,2,128,128]{3,2,1,0:T(8,128)S(1)}, u32[]{:S(2)}, u32[]{:S(2)}) collective-permute-start(f32[2,2,128,128]{3,2,1,0:T(8,128)S(1)} %get-tuple-element.49.refs_3_), channel_id=1, source_target_pairs={{1,4},{4,1},{11,14},{14,11},{17,20},{20,17},{27,30},{30,27}} | collective-permute-start | bytes 786440 | tf_op jit(solution)/shard_map/near_3/ppermute | solution.py:276
  41.5 0.1 collective-permute-start.9
  41.6 0.8 %skew.4.refs_4_ = f32[1,8,2,128,128]{4,3,2,1,0:T(8,128)} custom-call(f32[2,2,128,128]{3,2,1,0:T(8,128)S(1)} %get-tuple-element.52.refs_0_, f32[2,2,128,128]{3,2,1,0:T(8,128)S(1)} %collective-permute-done.16.refs_1_, f32[2,128,128]{2,1,0:T(8,128)S(1)} %collective-permute-done.11.refs_1_.refs_2_, f32[2,128,128]{2,1,0:T(8,128)S(1)} %collective-permute-done.12.refs_2_.refs_3_), custom_call_target="tpu_custom_call" | custom-call | tf_op jit(solution)/shard_map/skew/pallas_call | solution.py:237
  42.5 5.1 %collective-permute-start.18 = (f32[2,128,128]{2,1,0:T(8,128)S(1)}, f32[2,128,128]{2,1,0:T(8,128)S(1)}, u32[]{:S(2)}, u32[]{:S(2)}) collective-permute-start(f32[2,128,128]{2,1,0:T(8,128)S(1)} %collective-permute-done.15.refs_2_), channel_id=1, source_target_pairs={{10,8},{11,12},{14,9},{15,13},{0,2},{1,6},{4,3},{5,7},{26,24},{27,... | collective-permute-start | bytes 393224 | tf_op jit(solution)/shard_map/columns_4/ppermute | solution.py:276
  47.5 0.4 collective-permute-done.7.refs_1_
  48.0 0.8 %skew.5.refs_6_ = f32[1,8,2,128,128]{4,3,2,1,0:T(8,128)} custom-call(f32[2,2,128,128]{3,2,1,0:T(8,128)S(1)} %get-tuple-element.43.refs_0_, f32[4,2,128,128]{3,2,1,0:T(8,128)S(1)} %collective-permute-done.7.refs_1_, f32[2,128,128]{2,1,0:T(8,128)S(1)} %collective-permute-done.15.refs_2_, ...), custom_call_target="tpu_custom_call", output_to_operand_aliasing={{}: (4, {})} | custom-call | tf_op jit(solution)/shard_map/skew/pallas_call | solution.py:237
  48.8 1.2 %collective-permute-start.17 = (f32[2,128,128]{2,1,0:T(8,128)S(1)}, f32[2,128,128]{2,1,0:T(8,128)S(1)}, u32[]{:S(2)}, u32[]{:S(2)}) collective-permute-start(f32[2,128,128]{2,1,0:T(8,128)S(1)} %collective-permute-done.14.refs_2_), channel_id=1, source_target_pairs={{2,10},{3,11},{6,14},{7,15},{8,0},{9,1},{12,4},{13,5},{18,26},{19,... | collective-permute-start | bytes 393224 | tf_op jit(solution)/shard_map/rows_5/ppermute | solution.py:276
  50.1 2.5 %collective-permute-done.18.refs_5_ = f32[2,128,128]{2,1,0:T(8,128)S(1)} collective-permute-done((f32[2,128,128]{2,1,0:T(8,128)S(1)}, f32[2,128,128]{2,1,0:T(8,128)S(1)}, u32[]{:S(2)}, u32[]{:S(2)}) %collective-permute-start.18) | collective-permute-done | bytes 131104 | tf_op jit(solution)/shard_map/columns_4/ppermute | solution.py:276
  52.6 0.8 %skew.6.refs_6_ = f32[1,8,2,128,128]{4,3,2,1,0:T(8,128)} custom-call(f32[2,2,128,128]{3,2,1,0:T(8,128)S(1)} %get-tuple-element.42.refs_1_.refs_0_, f32[4,2,128,128]{3,2,1,0:T(8,128)S(1)} %collective-permute-done.7.refs_1_, f32[2,128,128]{2,1,0:T(8,128)S(1)} %collective-permute-done.14.refs_2_, ...), custom_call_target="tpu_custom_call", output_to_operand_aliasing={{}: (6, {})} | custom-call | tf_op jit(solution)/shard_map/skew/pallas_call | solution.py:237
  53.4 0.9 %skew.7 = f32[1,8,2,128,128]{4,3,2,1,0:T(8,128)} custom-call(f32[2,2,128,128]{3,2,1,0:T(8,128)S(1)} %get-tuple-element.42.refs_1_.refs_0_, f32[4,2,128,128]{3,2,1,0:T(8,128)S(1)} %collective-permute-done.7.refs_1_, f32[2,128,128]{2,1,0:T(8,128)S(1)} %collective-permute-done.9.refs_2_, ...), custom_call_target="tpu_custom_call", output_to_operand_aliasing={{}: (6, {})} | custom-call | tf_op jit(solution)/shard_map/skew/pallas_call | solution.py:237
  (21 shorter events, 0.2 us)
Async XLA Ops:
  0.0 5.1 %collective-permute-start = (s32[5,1,1]{0,2,1:T(1,128)}, s32[5,1,1]{0,2,1:T(1,128)S(1)}, u32[]{:S(2)}, u32[]{:S(2)}) collective-permute-start(s32[5,1,1]{0,2,1:T(1,128)} %param.5), channel_id=1, source_target_pairs={{16,0},{0,16},{17,1},{1,17},{18,2},{2,18},{19,3},{3,19},{20,4},{4,... | collective-permute-start | bytes 68 | tf_op jit(solution)/shard_map/ppermute | solution.py:293
  6.4 1.9 %copy-start = (s32[5,1,1]{0,2,1:T(1,128)S(1)}, s32[5,1,1]{0,2,1:T(1,128)}, u32[]{:S(2)}) copy-start(s32[5,1,1]{0,2,1:T(1,128)} %param.5) | copy-start | bytes 64
  6.4 6.9 %collective-permute-start.3 = (f32[2,2,128,128]{3,2,1,0:T(8,128)S(1)}, f32[2,2,128,128]{3,2,1,0:T(8,128)S(1)}, u32[]{:S(2)}, u32[]{:S(2)}) collective-permute-start(f32[2,2,128,128]{3,2,1,0:T(8,128)S(1)} %correlate.3), channel_id=1, source_target_pairs={{0,16},{16,0},{1,17},{17,1},{2,18},{18,2},{3,19},{19,3},{4,20},{20... | collective-permute-start | bytes 786440 | tf_op jit(solution)/shard_map/momentum_0/ppermute | solution.py:276
  10.5 10.8 %collective-permute-start.2 = (f32[2,2,128,128]{3,2,1,0:T(8,128)S(1)}, f32[2,2,128,128]{3,2,1,0:T(8,128)S(1)}, u32[]{:S(2)}, u32[]{:S(2)}) collective-permute-start(f32[2,2,128,128]{3,2,1,0:T(8,128)S(1)} %get-tuple-element.36), channel_id=1, source_target_pairs={{0,16},{16,0},{1,17},{17,1},{2,18},{18,2},{3,19},{19,3},{4,20},{20... | collective-permute-start | bytes 786440 | tf_op jit(solution)/shard_map/momentum_1/ppermute | solution.py:276
  13.4 7.9 %collective-permute-start.4 = (f32[2,128,128]{2,1,0:T(8,128)S(1)}, f32[2,128,128]{2,1,0:T(8,128)S(1)}, u32[]{:S(2)}, u32[]{:S(2)}) collective-permute-start(f32[2,128,128]{2,1,0:T(8,128)S(1)} %get-tuple-element.39), channel_id=1, source_target_pairs={{2,10},{3,11},{6,14},{7,15},{8,0},{9,1},{12,4},{13,5},{18,26},{19,... | collective-permute-start | bytes 393224 | tf_op jit(solution)/shard_map/rows_0/ppermute | solution.py:276
  14.7 12.9 %collective-permute-start.1 = (f32[2,2,128,128]{3,2,1,0:T(8,128)S(1)}, f32[2,2,128,128]{3,2,1,0:T(8,128)S(1)}, u32[]{:S(2)}, u32[]{:S(2)}) collective-permute-start(f32[2,2,128,128]{3,2,1,0:T(8,128)S(1)} %get-tuple-element.34), channel_id=1, source_target_pairs={{0,16},{16,0},{1,17},{17,1},{2,18},{18,2},{3,19},{19,3},{4,20},{20... | collective-permute-start | bytes 786440 | tf_op jit(solution)/shard_map/momentum_2/ppermute | solution.py:276
  14.9 12.7 %collective-permute-start.6 = (f32[2,128,128]{2,1,0:T(8,128)S(1)}, f32[2,128,128]{2,1,0:T(8,128)S(1)}, u32[]{:S(2)}, u32[]{:S(2)}) collective-permute-start(f32[2,128,128]{2,1,0:T(8,128)S(1)} %get-tuple-element.41), channel_id=1, source_target_pairs={{2,0},{3,4},{6,1},{7,5},{8,10},{9,14},{12,11},{13,15},{18,16},{19,... | collective-permute-start | bytes 393224 | tf_op jit(solution)/shard_map/columns_0/ppermute | solution.py:276
  21.3 6.2 %collective-permute-start.5 = (f32[2,128,128]{2,1,0:T(8,128)S(1)}, f32[2,128,128]{2,1,0:T(8,128)S(1)}, u32[]{:S(2)}, u32[]{:S(2)}) collective-permute-start(f32[2,128,128]{2,1,0:T(8,128)S(1)} %get-tuple-element.40), channel_id=1, source_target_pairs={{2,10},{3,11},{6,14},{7,15},{8,0},{9,1},{12,4},{13,5},{18,26},{19,... | collective-permute-start | bytes 393224 | tf_op jit(solution)/shard_map/rows_1/ppermute | solution.py:276
  21.6 11.7 %collective-permute-start.10 = (f32[2,2,128,128]{3,2,1,0:T(8,128)S(1)}, f32[2,2,128,128]{3,2,1,0:T(8,128)S(1)}, u32[]{:S(2)}, u32[]{:S(2)}) collective-permute-start(f32[2,2,128,128]{3,2,1,0:T(8,128)S(1)} %get-tuple-element.46), channel_id=1, source_target_pairs={{0,16},{16,0},{1,17},{17,1},{2,18},{18,2},{3,19},{19,3},{4,20},{20... | collective-permute-start | bytes 786440 | tf_op jit(solution)/shard_map/momentum_3/ppermute | solution.py:276
  23.4 11.9 %collective-permute-start.12 = (f32[2,128,128]{2,1,0:T(8,128)S(1)}, f32[2,128,128]{2,1,0:T(8,128)S(1)}, u32[]{:S(2)}, u32[]{:S(2)}) collective-permute-start(f32[2,128,128]{2,1,0:T(8,128)S(1)} %get-tuple-element.48), channel_id=1, source_target_pairs={{2,0},{3,4},{6,1},{7,5},{8,10},{9,14},{12,11},{13,15},{18,16},{19,... | collective-permute-start | bytes 393224 | tf_op jit(solution)/shard_map/columns_1/ppermute | solution.py:276
  27.6 7.6 %collective-permute-start.11 = (f32[2,128,128]{2,1,0:T(8,128)S(1)}, f32[2,128,128]{2,1,0:T(8,128)S(1)}, u32[]{:S(2)}, u32[]{:S(2)}) collective-permute-start(f32[2,128,128]{2,1,0:T(8,128)S(1)} %get-tuple-element.47), channel_id=1, source_target_pairs={{2,10},{3,11},{6,14},{7,15},{8,0},{9,1},{12,4},{13,5},{18,26},{19,... | collective-permute-start | bytes 393224 | tf_op jit(solution)/shard_map/rows_2/ppermute | solution.py:276
  27.9 11.0 %collective-permute-start.16 = (f32[2,2,128,128]{3,2,1,0:T(8,128)S(1)}, f32[2,2,128,128]{3,2,1,0:T(8,128)S(1)}, u32[]{:S(2)}, u32[]{:S(2)}) collective-permute-start(f32[2,2,128,128]{3,2,1,0:T(8,128)S(1)} %get-tuple-element.52.refs_0_), channel_id=1, source_target_pairs={{1,4},{4,1},{11,14},{14,11},{17,20},{20,17},{27,30},{30,27}} | collective-permute-start | bytes 786440 | tf_op jit(solution)/shard_map/near_0/ppermute | solution.py:276
  32.4 9.1 %collective-permute-start.8 = (f32[2,128,128]{2,1,0:T(8,128)S(1)}, f32[2,128,128]{2,1,0:T(8,128)S(1)}, u32[]{:S(2)}, u32[]{:S(2)}) collective-permute-start(f32[2,128,128]{2,1,0:T(8,128)S(1)} %get-tuple-element.44), channel_id=1, source_target_pairs={{2,0},{3,4},{6,1},{7,5},{8,10},{9,14},{12,11},{13,15},{18,16},{19,... | collective-permute-start | bytes 393224 | tf_op jit(solution)/shard_map/columns_2/ppermute | solution.py:276
  33.3 14.7 %collective-permute-start.7 = (f32[4,2,128,128]{3,2,1,0:T(8,128)S(1)}, f32[4,2,128,128]{3,2,1,0:T(8,128)S(1)}, u32[]{:S(2)}, u32[]{:S(2)}) collective-permute-start(f32[4,2,128,128]{3,2,1,0:T(8,128)S(1)} %pack.1), channel_id=1, source_target_pairs={{1,4},{4,1},{11,14},{14,11},{17,20},{20,17},{27,30},{30,27}} | collective-permute-start | bytes 1572872 | tf_op jit(solution)/shard_map/near_1/ppermute | solution.py:276
  35.3 7.1 %collective-permute-start.15 = (f32[2,128,128]{2,1,0:T(8,128)S(1)}, f32[2,128,128]{2,1,0:T(8,128)S(1)}, u32[]{:S(2)}, u32[]{:S(2)}) collective-permute-start(f32[2,128,128]{2,1,0:T(8,128)S(1)} %get-tuple-element.51), channel_id=1, source_target_pairs={{2,10},{3,11},{6,14},{7,15},{8,0},{9,1},{12,4},{13,5},{18,26},{19,... | collective-permute-start | bytes 393224 | tf_op jit(solution)/shard_map/rows_3/ppermute | solution.py:276
  35.6 13.3 %collective-permute-start.14 = (f32[2,128,128]{2,1,0:T(8,128)S(1)}, f32[2,128,128]{2,1,0:T(8,128)S(1)}, u32[]{:S(2)}, u32[]{:S(2)}) collective-permute-start(f32[2,128,128]{2,1,0:T(8,128)S(1)} %get-tuple-element.50), channel_id=1, source_target_pairs={{2,0},{3,4},{6,1},{7,5},{8,10},{9,14},{12,11},{13,15},{18,16},{19,... | collective-permute-start | bytes 393224 | tf_op jit(solution)/shard_map/columns_3/ppermute | solution.py:276
  38.9 13.7 %collective-permute-start.13 = (f32[2,2,128,128]{3,2,1,0:T(8,128)S(1)}, f32[2,2,128,128]{3,2,1,0:T(8,128)S(1)}, u32[]{:S(2)}, u32[]{:S(2)}) collective-permute-start(f32[2,2,128,128]{3,2,1,0:T(8,128)S(1)} %get-tuple-element.49.refs_3_), channel_id=1, source_target_pairs={{1,4},{4,1},{11,14},{14,11},{17,20},{20,17},{27,30},{30,27}} | collective-permute-start | bytes 786440 | tf_op jit(solution)/shard_map/near_3/ppermute | solution.py:276
  41.5 11.9 %collective-permute-start.9 = (f32[2,128,128]{2,1,0:T(8,128)S(1)}, f32[2,128,128]{2,1,0:T(8,128)S(1)}, u32[]{:S(2)}, u32[]{:S(2)}) collective-permute-start(f32[2,128,128]{2,1,0:T(8,128)S(1)} %collective-permute-done.8.refs_3_), channel_id=1, source_target_pairs={{2,10},{3,11},{6,14},{7,15},{8,0},{9,1},{12,4},{13,5},{18,26},{19,... | collective-permute-start | bytes 393224 | tf_op jit(solution)/shard_map/rows_4/ppermute | solution.py:276
  42.5 10.1 %collective-permute-start.18 = (f32[2,128,128]{2,1,0:T(8,128)S(1)}, f32[2,128,128]{2,1,0:T(8,128)S(1)}, u32[]{:S(2)}, u32[]{:S(2)}) collective-permute-start(f32[2,128,128]{2,1,0:T(8,128)S(1)} %collective-permute-done.15.refs_2_), channel_id=1, source_target_pairs={{10,8},{11,12},{14,9},{15,13},{0,2},{1,6},{4,3},{5,7},{26,24},{27,... | collective-permute-start | bytes 393224 | tf_op jit(solution)/shard_map/columns_4/ppermute | solution.py:276
  48.8 4.6 %collective-permute-start.17 = (f32[2,128,128]{2,1,0:T(8,128)S(1)}, f32[2,128,128]{2,1,0:T(8,128)S(1)}, u32[]{:S(2)}, u32[]{:S(2)}) collective-permute-start(f32[2,128,128]{2,1,0:T(8,128)S(1)} %collective-permute-done.14.refs_2_), channel_id=1, source_target_pairs={{2,10},{3,11},{6,14},{7,15},{8,0},{9,1},{12,4},{13,5},{18,26},{19,... | collective-permute-start | bytes 393224 | tf_op jit(solution)/shard_map/rows_5/ppermute | solution.py:276
